TPU v7x, 128 devices: a whole 4x4x4 slice. The times are simulated.
128 devices in a mesh: lat: 8 (over y, z_hi), lon: 16 (over x, z_lo, core).
Axes of the slice: x: 4, y: 4, z: 4 (z_hi: 2, z_lo: 2; z = z_hi * 2 + z_lo), core: 2. Of those that a mesh axis runs over, the one named last changes fastest.
Arguments:
- humidity: bfloat16 [137, 1024, 2048], P(None, 'lat', 'lon'), may hold values from 0.099609375 to 10
- wind_u: bfloat16 [137, 1024, 2048], P(None, 'lat', 'lon'), may hold values from -6 to 6
- wind_v: bfloat16 [137, 1024, 2048], P(None, 'lat', 'lon'), may hold values from -6 to 6
- weights: float32 [137], replicated, may hold values from 0.002 to 0.02
- labels: int32 [1024, 2048], P('lat', 'lon'), may hold values from 0 to 127, as said below
- global_labels: int32 [8, 16, 128], P('lat', 'lon'), may hold values from 0 to 4095, as said below
Outputs:
- anomaly: float32 [1024, 2048], P('lat', 'lon')
Inputs may be any that keep to these rules, and one draw needn't show every extreme that they name: Each tile's labels are constant on aligned patches of 4 rows by 8 columns. `global_labels`: each of the 4096 global objects is named by exactly 4 entries. The tiles form groups of four: tile row i or i plus half of 8, with tile column j or j plus 1 for even j. All entries that name one object lie in one such group.
All inputs are finite; a program needn't handle non-finite values.
Results may differ from a plain program's by a relative error of at most 0.0039.
Values may be sent and summed in bfloat16 or wider, within the bound.
No kernel may reach another device: no remote copies, remote signals or barrier semaphores. Data moves between devices by JAX's collectives and lax.ppermute only.
A program may use at most 128 MiB of HBM per device.

v0:
```python
import jax
import jax.numpy as jnp
from jax import lax
from jax.sharding import PartitionSpec as P


def extended(x, sides, width, wrap):
    for axis, dim in sides:
        count, length = (lax.axis_size(axis), x.shape[dim])
        up = [(i, (i + 1) % count) for i in range(count if wrap else count - 1)]
        down = [(j, i) for i, j in up]
        last = lax.slice_in_dim(x, length - width, length, axis=dim)
        leading = lax.slice_in_dim(x, 0, width, axis=dim)
        before = lax.ppermute(last, axis, up)
        after = lax.ppermute(leading, axis, down)
        x = jnp.concatenate([before, x, after], axis=dim)
    return x


def shards(humidity, wind_u, wind_v, weights, labels, global_labels):
    levels, rows, cols = humidity.shape
    local_count = global_labels.shape[2]
    object_count = lax.axis_size("lat") * lax.axis_size("lon") * local_count // 4
    wind_speed = jnp.sqrt(wind_u.astype(jnp.float32) ** 2 + wind_v.astype(jnp.float32) ** 2 + 1.0)
    transport = (humidity.astype(jnp.float32) * wind_speed).astype(jnp.bfloat16)
    north_south = extended(transport, (("lat", 1),), 1, False)
    east_west = extended(transport, (("lon", 2),), 1, True)
    neighbours = (
        north_south[:, :-2, :].astype(jnp.float32)
        + north_south[:, 2:, :].astype(jnp.float32)
        + east_west[:, :, :-2].astype(jnp.float32)
        + east_west[:, :, 2:].astype(jnp.float32)
    )
    smoothed = (0.5 * transport.astype(jnp.float32) + 0.125 * neighbours).astype(jnp.bfloat16)
    columns_flat = smoothed.reshape(levels, rows * cols)
    label_flat = labels.reshape(rows * cols)
    local_ids = jnp.arange(local_count, dtype=jnp.int32)
    onehot = (label_flat[:, None] == local_ids[None, :]).astype(jnp.bfloat16)
    local_totals = jnp.dot(columns_flat, onehot, preferred_element_type=jnp.float32)
    local_counts = jnp.sum(onehot, axis=0, dtype=jnp.float32)
    own_globals = global_labels.reshape(local_count)
    object_ids = jnp.arange(object_count, dtype=jnp.int32)
    placing = (own_globals[:, None] == object_ids[None, :]).astype(jnp.float32)
    part_totals = jnp.dot(local_totals, placing, precision=lax.Precision.HIGHEST)
    part_counts = jnp.dot(local_counts, placing, precision=lax.Precision.HIGHEST)
    totals, counts = lax.psum((part_totals, part_counts), ("lat", "lon"))
    profile = totals / jnp.maximum(counts, 1.0)[None, :]
    local_profile = jnp.dot(profile, placing.T, precision=lax.Precision.HIGHEST)
    weighted = weights[:, None] * local_profile
    energy = jnp.sum(weighted * local_profile, axis=0)
    values_f32 = columns_flat.astype(jnp.float32)
    own_term = jnp.sum(weights[:, None] * values_f32 * values_f32, axis=0)
    crossed = lax.dot_general(
        values_f32, weighted, (((0,), (0,)), ((), ())), precision=lax.Precision.HIGHEST
    )
    onehot_f32 = onehot.astype(jnp.float32)
    cross_term = jnp.sum(crossed * onehot_f32, axis=1)
    pixel_energy = jnp.dot(onehot_f32, energy, precision=lax.Precision.HIGHEST)
    spread = jnp.maximum(own_term - 2.0 * cross_term + pixel_energy, 0.0)
    return jnp.sqrt(spread / pixel_energy).reshape(rows, cols)


def solution(mesh):
    return jax.shard_map(
        shards,
        mesh=mesh,
        in_specs=(
            P(None, "lat", "lon"),
            P(None, "lat", "lon"),
            P(None, "lat", "lon"),
            P(),
            P("lat", "lon"),
            P("lat", "lon", None),
        ),
        out_specs=P("lat", "lon"),
        check_vma=False,
    )
```

profile of v0, /device:TPU:1, one launch (start us, length us, event | category | flops | bytes accessed | tf_op | source)
XLA Modules:
  0.0 259.6 jit_solution(11619539107477188280)
XLA Ops:
  6.5 0.0 all-reduce.2.cloned.1.call-start
  6.5 14.0 %multiply_convert_fusion = bf16[137,128,128]{2,0,1:T(8,128)(2,1)S(1)} fusion(bf16[137,128,128]{2,1,0:T(8,128)(2,1)} %param.8, bf16[137,128,128]{2,1,0:T(8,128)(2,1)} %param.7, bf16[137,128,128]{2,1,0:T(8,128)(2,1)} %param.6), kind=kLoop, calls=%fused_computation.5 | loop fusion | flops 20201472 | bytes 17956864 | tf_op jit(solution)/shard_map/convert_element_type | solution.py:25
  20.5 0.0 copy-start
  20.6 5.2 %fusion.26 = (bf16[137,128,1]{2,0,1:T(8,128)(2,1)}, bf16[137,128,1]{2,0,1:T(8,128)(2,1)}) fusion(bf16[137,128,128]{2,0,1:T(8,128)(2,1)S(1)} %multiply_convert_fusion), kind=kLoop, calls=%fused_computation.40 | loop fusion | bytes 140288 | tf_op jit(solution)/shard_map/slice | solution.py:12
  25.7 0.0 copy-done
  25.8 5.1 %copy.26 = bf16[137,128,1]{1,0,2:T(8,128)(2,1)S(1)} copy(bf16[137,128,1]{2,0,1:T(8,128)(2,1)} %get-tuple-element.9) | data formatting | bytes 70144 | tf_op jit(solution)/shard_map/slice | solution.py:12
  30.9 3.1 %collective-permute-start.2 = (bf16[137,128,1]{1,0,2:T(8,128)(2,1)S(1)}, bf16[137,128,1]{1,0,2:T(8,128)(2,1)S(1)}, u32[]{:S(2)}, u32[]{:S(2)}) collective-permute-start(bf16[137,128,1]{1,0,2:T(8,128)(2,1)S(1)} %copy.26), channel_id=1, source_target_pairs={{0,1},{1,2},{2,3},{3,4},{4,5},{5,6},{6,7},{7,8},{8,9},{9,10},{10,1... | collective-permute-start | bytes 105224 | tf_op jit(solution)/shard_map/ppermute | solution.py:14
  34.0 5.1 %copy.28 = bf16[137,128,1]{1,0,2:T(8,128)(2,1)S(1)} copy(bf16[137,128,1]{2,0,1:T(8,128)(2,1)} %get-tuple-element.10) | data formatting | bytes 70144 | tf_op jit(solution)/shard_map/slice | solution.py:13
  39.1 0.1 collective-permute-start.3
  39.2 0.8 fusion.25
  40.0 5.2 %collective-permute-start = (bf16[137,1,128]{2,0,1:T(8,128)(2,1)S(1)}, bf16[137,1,128]{2,0,1:T(8,128)(2,1)S(1)}, u32[]{:S(2)}, u32[]{:S(2)}) collective-permute-start(bf16[137,1,128]{2,0,1:T(8,128)(2,1)S(1)} %get-tuple-element.7), channel_id=1, source_target_pairs={{0,16},{16,32},{32,48},{48,64},{64,80},{80,96},{96,112},{1,17},{17... | collective-permute-start | bytes 105224 | tf_op jit(solution)/shard_map/ppermute | solution.py:14
  45.2 0.0 copy-start.3
  45.2 1.5 collective-permute-start.1
  46.7 0.0 collective-permute-done.2
  46.7 4.0 %copy.27 = bf16[137,128,1]{2,0,1:T(8,128)(2,1)} copy(bf16[137,128,1]{1,0,2:T(8,128)(2,1)S(1)} %collective-permute-done.2) | data formatting | bytes 70144 | tf_op jit(solution)/shard_map/ppermute | solution.py:14
  50.7 0.0 collective-permute-done.3
  50.7 3.9 %copy.29 = bf16[137,128,1]{2,0,1:T(8,128)(2,1)} copy(bf16[137,128,1]{1,0,2:T(8,128)(2,1)S(1)} %collective-permute-done.3) | data formatting | bytes 70144 | tf_op jit(solution)/shard_map/ppermute | solution.py:15
  54.6 0.0 collective-permute-done
  54.6 0.0 collective-permute-done.1
  54.6 0.0 copy-done.3
  54.6 16.9 %fusion = (f32[128,128]{1,0:T(8,128)S(1)}, bf16[137,128,128]{2,0,1:T(8,128)(2,1)S(1)}) fusion(f32[137]{0:T(256)S(1)} %copy-done.3, bf16[137,128,1]{2,0,1:T(8,128)(2,1)} %copy.29, bf16[137,128,128]{2,0,1:T(8,128)(2,1)} %copy-done, bf16[137,128,1]{2,0,1:T(8,128)(2,1)} %copy.27, bf16[137,1,128]{2,0,1:T(8,128)(2,1)S(1)} %collective-permute-done.1, ...), kind=kLoop, calls=%fused_computation.3 | loop fusion | flops 62832640 | bytes 9184804 | tf_op jit(solution)/shard_map/reduce_sum | solution.py:52
  71.6 1.2 copy.32
  72.8 0.9 pad.16
  73.7 0.0 copy-start.2
  73.7 4.1 %copy.34 = bf16[18,8,128,128]{3,1,2,0:T(8,128)(2,1)S(1)} copy(bf16[18,8,128,128]{3,2,1,0:T(8,128)(2,1)S(1)} %bitcast.30) | data formatting | bytes 9437184
  77.8 0.0 copy-start.1
  77.8 0.0 copy-start.4
  77.8 2.1 copy-done.1
  80.0 0.0 copy-done.2
  80.0 1.5 fusion.3
  81.5 0.0 copy-done.4
  81.5 2.7 %fusion.10 = f32[137,4096]{1,0:T(8,128)} fusion(f32[137,128]{1,0:T(8,128)S(1)} %fusion.3, s32[128]{0:T(128)S(1)} %bitcast.39), kind=kOutput, calls=%fused_computation.21 | convolution fusion | flops 862453760 | bytes 2315264 | tf_op jit(solution)/shard_map/dot_general | solution.py:44
  84.2 0.0 all-reduce.2.cloned.1.call-update
  84.2 0.9 convert_reduce_fusion
  85.1 0.8 fusion.9
  86.0 67.9 %psum.15 = f32[4096]{0:T(1024)S(1)} all-reduce(f32[4096]{0:T(1024)S(1)} %bitcast.38), channel_id=1, replica_groups=mesh['lat'=8,'lon'=16] {'lat','lon'}, use_global_device_ids=true, to_apply=%region_3.0 | all-reduce | flops 4096 | bytes 32768 | tf_op jit(solution)/shard_map/psum | solution.py:46
  153.9 85.1 %all-reduce.2.cloned.1.call-done = f32[137,4096]{1,0:T(8,128)} async-done(((f32[137,4096]{1,0:T(8,128)}), f32[137,4096]{1,0:T(8,128)}) %all-reduce.2.cloned.1.call-update) | async-done | bytes 2244624 | tf_op jit(solution)/shard_map/psum | solution.py:46
  239.0 3.3 %fusion.16 = (f32[128]{0:T(128)S(1)}, f32[137,128]{1,0:T(8,128)S(1)}) fusion(f32[137]{0:T(256)S(1)} %copy-done.3, s32[128]{0:T(128)S(1)} %bitcast.41, f32[137,4096]{1,0:T(8,128)} %all-reduce.2.cloned.1.call-done, f32[4096]{0:T(1024)S(1)} %broadcast_maximum_fusion), kind=kOutput, calls=%fused_computation.28 | convolution fusion | flops 863067392 | bytes 2332708 | tf_op jit(solution)/shard_map/dot_general | solution.py:48
  242.3 7.1 %fusion.8 = f32[16384]{0:T(1024)S(1)} fusion(s32[16384]{0:T(1024)S(1)} %bitcast.35, bf16[137,16384]{1,0:T(8,128)(2,1)} %bitcast.32, f32[137,128]{1,0:T(8,128)S(1)} %get-tuple-element.12, f32[137]{0:T(256)S(1)} %copy-done.3), kind=kOutput, calls=%fused_computation.18 | convolution fusion | flops 3458204672 | bytes 4690980 | tf_op jit(solution)/shard_map/dot_general | solution.py:53
  249.4 2.7 %fusion.1 = f32[1,16384]{1,0:T(1,128)S(1)} fusion(s32[16384]{0:T(1024)S(1)} %bitcast.36, f32[128]{0:T(128)S(1)} %get-tuple-element.11), kind=kOutput, calls=%fused_computation.7 | convolution fusion | flops 27262976 | bytes 131584 | tf_op jit(solution)/shard_map/dot_general | solution.py:58
  252.1 0.7 fusion.21
  (1 shorter events, 0.0 us)
Async XLA Ops:
  6.5 232.5 %all-reduce.2.cloned.1.call-start = ((), (), s32[]{:S(2)}) async-start(), calls=%async_computation | async-start | bytes 4718592 | tf_op jit(solution)/shard_map/psum | solution.py:46
  20.5 5.2 %copy-start = (bf16[137,128,128]{2,0,1:T(8,128)(2,1)}, bf16[137,128,128]{2,0,1:T(8,128)(2,1)S(1)}, u32[]{:S(2)}) copy-start(bf16[137,128,128]{2,0,1:T(8,128)(2,1)S(1)} %multiply_convert_fusion) | copy-start | bytes 13467652
  30.9 15.8 %collective-permute-start.2 = (bf16[137,128,1]{1,0,2:T(8,128)(2,1)S(1)}, bf16[137,128,1]{1,0,2:T(8,128)(2,1)S(1)}, u32[]{:S(2)}, u32[]{:S(2)}) collective-permute-start(bf16[137,128,1]{1,0,2:T(8,128)(2,1)S(1)} %copy.26), channel_id=1, source_target_pairs={{0,1},{1,2},{2,3},{3,4},{4,5},{5,6},{6,7},{7,8},{8,9},{9,10},{10,1... | collective-permute-start | bytes 105224 | tf_op jit(solution)/shard_map/ppermute | solution.py:14
  39.1 11.6 %collective-permute-start.3 = (bf16[137,128,1]{1,0,2:T(8,128)(2,1)S(1)}, bf16[137,128,1]{1,0,2:T(8,128)(2,1)S(1)}, u32[]{:S(2)}, u32[]{:S(2)}) collective-permute-start(bf16[137,128,1]{1,0,2:T(8,128)(2,1)S(1)} %copy.28), channel_id=1, source_target_pairs={{1,0},{2,1},{3,2},{4,3},{5,4},{6,5},{7,6},{8,7},{9,8},{10,9},{11,1... | collective-permute-start | bytes 105224 | tf_op jit(solution)/shard_map/ppermute | solution.py:15
  40.0 14.7 %collective-permute-start = (bf16[137,1,128]{2,0,1:T(8,128)(2,1)S(1)}, bf16[137,1,128]{2,0,1:T(8,128)(2,1)S(1)}, u32[]{:S(2)}, u32[]{:S(2)}) collective-permute-start(bf16[137,1,128]{2,0,1:T(8,128)(2,1)S(1)} %get-tuple-element.7), channel_id=1, source_target_pairs={{0,16},{16,32},{32,48},{48,64},{64,80},{80,96},{96,112},{1,17},{17... | collective-permute-start | bytes 105224 | tf_op jit(solution)/shard_map/ppermute | solution.py:14
  45.2 9.5 %copy-start.3 = (f32[137]{0:T(256)S(1)}, f32[137]{0:T(256)}, u32[]{:S(2)}) copy-start(f32[137]{0:T(256)} %param.9) | copy-start | bytes 1648
  45.2 9.5 %collective-permute-start.1 = (bf16[137,1,128]{2,0,1:T(8,128)(2,1)S(1)}, bf16[137,1,128]{2,0,1:T(8,128)(2,1)S(1)}, u32[]{:S(2)}, u32[]{:S(2)}) collective-permute-start(bf16[137,1,128]{2,0,1:T(8,128)(2,1)S(1)} %get-tuple-element.8), channel_id=1, source_target_pairs={{16,0},{32,16},{48,32},{64,48},{80,64},{96,80},{112,96},{17,1},{33... | collective-permute-start | bytes 105224 | tf_op jit(solution)/shard_map/ppermute | solution.py:15
  73.7 6.2 %copy-start.2 = (s32[128,128]{1,0:T(8,128)S(1)}, s32[128,128]{1,0:T(8,128)}, u32[]{:S(2)}) copy-start(s32[128,128]{1,0:T(8,128)} %param.10) | copy-start | bytes 196612
  77.8 2.1 copy-start.1
  77.8 3.7 %copy-start.4 = (s32[1,1,128]{2,1,0:T(1,128)S(1)}, s32[1,1,128]{2,1,0:T(1,128)}, u32[]{:S(2)}) copy-start(s32[1,1,128]{2,1,0:T(1,128)} %param.11) | copy-start | bytes 1540
Sparse Core Ops, SparseCore 0:
  84.4 154.6 all-reduce.1
where the time goes:
time: 260 us
  waiting for transfers between devices  85.2 us (33%)
  blocking collectives  67.9 us (26%)
  other arithmetic  32.5 us (12%)
  local copies, waits for them, and re-layouts  32.5 us (12%)
  matrix products  18.1 us (7%)
  between operations  13.5 us (5%)
  starting transfers between devices  9.84 us (4%)
    psum x1, waiting for transfers between devices, shards(): totals, counts = lax.psum((part_totals, part_counts), ('lat', 'lon'))  85.1 us
    psum x1, blocking collectives, shards(): totals, counts = lax.psum((part_totals, part_counts), ('lat', 'lon'))  67.9 us
    reduce_sum x1, other arithmetic, shards(): own_term = jnp.sum(weights[:, None] * values_f32 * values_f32, axis=0)  16.9 us
    convert_element_type x1, other arithmetic, shards(): transport = (humidity.astype(jnp.float32) * wind_speed).astype(jnp.bfloat16)  14 us
    slice x3, local copies, waits for them, and re-layouts, extended(): last = lax.slice_in_dim(x, length - width, length, axis=dim)  11.1 us
    ppermute x2, starting transfers between devices, extended(): before = lax.ppermute(last, axis, up)  8.29 us
    unnamed x12, local copies, waits for them, and re-layouts  7.16 us
    dot_general x1, matrix products, shards(): lax.dot_general(values_f32, weighted, (((0,), (0,)), ((), ())), precision...  7.09 us
  transfers between devices with their start and end apart: 5, of which 1 were waited for; matrix products, arithmetic and copies ran while one was open for 6% of the time, Pallas kernels for 0%

commit v1 on v0

v1 whole, which is shorter than its diff:
```python
import jax
import jax.numpy as jnp
from jax import lax
from jax.experimental import pallas as pl
from jax.experimental.pallas import tpu as pltpu
from jax.sharding import PartitionSpec as P

F32 = jnp.float32
BF16 = jnp.bfloat16
LEV = 137
KP = 152
N = 128
CHUNKS = ((0, 8), (8, 16), (24, 24), (48, 24), (72, 24), (96, 24), (120, 8), (128, 9))
NT = (((1,), (1,)), ((), ()))
NN = (((1,), (0,)), ((), ()))


def iota(shape, dim):
    return lax.broadcasted_iota(jnp.int32, shape, dim)


def dot(a, b, dims):
    return lax.dot_general(a, b, dims, preferred_element_type=F32)


def column(row, rows):
    shape = (rows, row.shape[1])
    return jnp.sum(jnp.where(iota(shape, 0) == iota(shape, 1), row, 0.0), axis=1, keepdims=True)


def ends():
    shape = (16, N)
    first = (iota(shape, 0) == 0) & (iota(shape, 1) == 0)
    last = (iota(shape, 0) == 1) & (iota(shape, 1) == N - 1)
    return jnp.where(first | last, 1.0, 0.0).astype(BF16)


def halos(r0, r1, rc, ro):
    i, j = lax.axis_index("lat"), lax.axis_index("lon")
    i_even, j_even = lax.rem(i, 2) == 0, lax.rem(j, 2) == 0
    r0, r1, rc, ro = (r[...].astype(F32) for r in (r0, r1, rc, ro))
    north = jnp.where(i == 0, 0.0, jnp.where(i_even, r1, r0))
    south = jnp.where(i == 7, 0.0, jnp.where(i_even, r0, r1))
    west = jnp.where(j_even, ro, rc)
    east = jnp.where(j_even, rc, ro)
    return north, south, west, east


def transport_kernel(h_hbm, u_hbm, v_hbm, t_ref, s0_ref, s1_ref, c0_ref, c1_ref, hb, ub, vb, cols, sems):
    copies = []
    for c, (a, n) in enumerate(CHUNKS):
        row = []
        for m, (src, dst) in enumerate(((h_hbm, hb), (u_hbm, ub), (v_hbm, vb))):
            copy = pltpu.make_async_copy(src.at[pl.ds(a, n)], dst.at[pl.ds(a, n)], sems.at[c, m])
            copy.start()
            row.append(copy)
        copies.append(row)
    zeros = jnp.zeros((N, N), F32)
    for k in range(LEV, KP):
        t_ref[pl.ds(KP + k, N, stride=KP), :] = zeros
    blank = jnp.zeros((KP, N), F32)
    t_ref[pl.ds(0, KP), :] = blank
    t_ref[pl.ds((N + 1) * KP, KP), :] = blank
    cols[...] = jnp.zeros((3, N, N), BF16)
    lane = iota((N, N), 1)

    def level(k):
        parts = []
        for b in range(0, N, 32):
            rows = pl.ds(b, 32)
            u = ub[k, rows, :].astype(F32)
            v = vb[k, rows, :].astype(F32)
            x = u * u + v * v + 1.0
            t = (hb[k, rows, :].astype(F32) * (x * lax.rsqrt(x))).astype(BF16)
            t_ref[pl.ds((1 + b) * KP + k, 32, stride=KP), :] = t.astype(F32)
            parts.append(t)
        return jnp.concatenate(parts, axis=0)

    def group(k, size):
        ends = level(k)
        for q in range(1, size):
            moved = pltpu.roll(level(k + q), 2 * q, 1)
            ends = jnp.where((lane == 2 * q) | (lane == 2 * q - 1), moved, ends)
        shift = 2 * lax.rem(k, 64)
        mine = lax.rem(lane - shift + N + 1, N) < 2 * size
        block = lax.div(k, 64)
        cols[block] = jnp.where(mine, pltpu.roll(ends, shift, 1), cols[block])

    for (a, n), row in zip(CHUNKS, copies):
        for copy in row:
            copy.wait()

        def groups(g, _, a=a):
            group(a + 8 * g, 8)
            return 0

        lax.fori_loop(0, n // 8, groups, 0)
        if n % 8:
            group(a + n - n % 8, n % 8)
    i_even = lax.rem(lax.axis_index("lat"), 2) == 0
    j_even = lax.rem(lax.axis_index("lon"), 2) == 0

    def row_at(top):
        start = pl.multiple_of(jnp.where(top, KP, N * KP), 8)
        return t_ref[pl.ds(start, KP), :].astype(BF16)

    k, at = iota((KP, 3 * N), 0), iota((KP, 3 * N), 1)
    left_at = 2 * k
    right_at = jnp.where(lax.rem(k, 64) == 0, 2 * k + N - 1, 2 * k - 1)
    packed = jnp.concatenate([cols[0], cols[1], cols[2]], axis=1)

    def col_at(left):
        pick = jnp.where(at == jnp.where(left, left_at, right_at), 1.0, 0.0).astype(BF16)
        return dot(pick, packed, NT).astype(BF16)

    s0_ref[...] = row_at(jnp.logical_not(i_even))
    s1_ref[...] = row_at(i_even)
    c0_ref[...] = col_at(jnp.logical_not(j_even))
    c1_ref[...] = col_at(j_even)


def sums_kernel(t_ref, lab_ref, t0_ref, west_ref, east_ref):
    lab = lab_ref[...]
    lane = iota((N, N), 1)
    west_ref[...] = jnp.where(lane == 0, -1, pltpu.roll(lab, 1, 1))
    east_ref[...] = jnp.where(lane == N - 1, -1, pltpu.roll(lab, N - 1, 1))
    ids = iota((N, N), 0)
    t0_ref[...] = jnp.zeros((KP, N), F32)

    def patch_row(q):
        base = pl.multiple_of((1 + 4 * q) * KP, 8)
        x = [t_ref[pl.ds(base + m * KP, KP), :] for m in range(-1, 5)]
        whole = x[1] + x[2] + x[3] + x[4]
        step = jnp.where(iota((KP, N), 0) == LEV, 32.0, (x[0] - x[4]) + (x[5] - x[1]))
        left = jnp.concatenate([whole.astype(BF16), step.astype(BF16)], axis=1)
        r = pl.ds(4 * q, 1)
        here = jnp.where(lab_ref[r, :] == ids, 0.125, 0.0)
        west = jnp.where(west_ref[r, :] == ids, 0.125, 0.0)
        east = jnp.where(east_ref[r, :] == ids, 0.125, 0.0)
        spread = 6.0 * here + (west + east)
        return left, jnp.concatenate([spread.astype(BF16), here.astype(BF16)], axis=1)

    def patch_rows(i, _):
        pairs = [patch_row(16 * i + m) for m in range(16)]
        left, right = (jnp.concatenate(p, axis=1) for p in zip(*pairs))
        t0_ref[...] += dot(left, right, NT)
        return 0

    lax.fori_loop(0, N // 64, patch_rows, 0)


def pack_kernel(t0_ref, r0, r1, rc, ro, lab_ref, gl_ref, pay_ref):
    north, south, west, east = halos(r0, r1, rc, ro)
    lab = lab_ref[...].astype(F32)
    ids = iota((N, N), 0).astype(F32)
    sides = dot(ends(), lab.astype(BF16), NT)

    def marks(row):
        return jnp.where(row == ids, 0.125, 0.0)

    left = jnp.concatenate([north, south, west, east], axis=1).astype(BF16)
    right = jnp.concatenate(
        [marks(lab[0:1]), marks(lab[N - 1 : N]), marks(sides[0:1]), marks(sides[1:2])], axis=1
    ).astype(BF16)
    total = t0_ref[...] + dot(left, right, NT)
    count = total[LEV : LEV + 1] * (1.0 / 32.0)
    count_hi = jnp.floor(count * 0.125)
    gl = gl_ref[...].astype(F32)
    gl_hi = jnp.floor(gl * (1.0 / 64.0))
    row = iota((KP, N), 0)
    for m, extra in enumerate((count_hi, count - 8.0 * count_hi, gl_hi, gl - 64.0 * gl_hi)):
        total = jnp.where(row == LEV + m, extra, total)
    pay_ref[...] = total.astype(BF16)


def smooth_kernel(t_ref, r0, r1, rc, ro, w_ref, s_ref, root_ref):
    north, south, west, east = halos(r0, r1, rc, ro)
    low = iota((KP, N), 1) < 64
    sides = (
        jnp.where(low, west, pltpu.roll(east, 64, 1)).astype(BF16),
        jnp.where(low, pltpu.roll(west, 64, 1), east).astype(BF16),
    )
    root_ref[...] = jnp.sqrt(column(w_ref[...], KP)) + jnp.zeros((KP, N), F32)
    a, c = iota((2 * N, N), 0), iota((2 * N, N), 1)
    band = jnp.where(a == c, 0.5, jnp.where(jnp.abs(a - c) == 1, 0.125, 0.0))
    side = jnp.where(c == jnp.where(a < N + 64, 0, N - 1), 0.125, 0.0)
    right = jnp.where(a < N, band, side).astype(BF16)
    lane = lax.rem(iota((1, N), 1), 64)

    def at(r):
        return pl.ds(pl.multiple_of(r * KP, 8), KP)

    for half in range(2):

        def rows(i, _, half=half):
            top = 64 * half + 32 * i
            lefts = []
            for m in range(32):
                mine = jnp.where(lane == 32 * i + m, 1.0, 0.0).astype(BF16)
                lefts.append(jnp.concatenate([t_ref[at(top + m + 1), :].astype(BF16), sides[half] * mine], axis=1))
            across = dot(jnp.concatenate(lefts, axis=0), right, NN)
            for m in range(32):
                along = t_ref[at(top + m), :] + t_ref[at(top + m + 2), :]
                s_ref[at(top + m), :] = (across[m * KP : (m + 1) * KP] + 0.125 * along) * root_ref[...]
            return 0

        lax.fori_loop(0, 2, rows, 0)
    s_ref[at(0), :] += 0.125 * north * root_ref[...]
    s_ref[at(N - 1), :] += 0.125 * south * root_ref[...]


def final_kernel(p0, p1, p2, p3, s_ref, lab_ref, gl_ref, w_ref, out_ref, e_ref):
    own = column(gl_ref[...].astype(F32), N) + jnp.zeros((N, N), F32)
    lefts, rights = [], []
    for p in (p0, p1, p2, p3):
        pay = p[...]
        gl = pay[LEV + 2 : LEV + 3].astype(F32) * 64.0 + pay[LEV + 3 : LEV + 4].astype(F32)
        lefts.append(pay)
        rights.append(jnp.where(own == gl, 1.0, 0.0).astype(BF16))
    total = dot(jnp.concatenate(lefts, axis=1), jnp.concatenate(rights, axis=1), NT)
    count = 256.0 * total[LEV : LEV + 1] + 32.0 * total[LEV + 1 : LEV + 2]
    root = jnp.sqrt(column(w_ref[...], KP))
    profile = root * (total / jnp.maximum(count, 1.0))
    energy = jnp.sum(profile * profile, axis=0, keepdims=True)
    row = iota((KP, N), 0)
    table = jnp.where(row == LEV, energy, profile)
    hi = table.astype(BF16)
    left = jnp.concatenate([hi, (table - hi.astype(F32)).astype(BF16)], axis=1)
    ids = iota((N, N), 0)

    def patch_row(q):
        mark = jnp.where(lab_ref[pl.ds(4 * q, 1), :] == ids, 1.0, 0.0).astype(BF16)
        placed = dot(left, jnp.concatenate([mark, mark], axis=0), NN)
        e = placed[LEV : LEV + 1]
        placed = jnp.where(row == LEV, 0.0, placed)
        for m in range(4):
            r = 4 * q + m
            d = s_ref[pl.ds(pl.multiple_of(r * KP, 8), KP), :] - placed
            out_ref[pl.ds(r, 1), :] = jnp.sum(d * d, axis=0, keepdims=True)
            e_ref[pl.ds(r, 1), :] = e

    def patch_rows(i, _):
        for m in range(16):
            patch_row(16 * i + m)
        return 0

    lax.fori_loop(0, N // 64, patch_rows, 0)
    out_ref[...] = jnp.sqrt(out_ref[...] / e_ref[...])


def params(mib):
    return pltpu.CompilerParams(vmem_limit_bytes=mib * 1024 * 1024)


def cost(flops, moved):
    return pl.CostEstimate(flops=flops, bytes_accessed=moved, transcendentals=0)


def shards(humidity, wind_u, wind_v, weights, labels, global_labels):
    vmem = pl.BlockSpec(memory_space=pltpu.VMEM)
    anywhere = pl.BlockSpec(memory_space=pl.ANY)
    edge = pltpu.VMEM((KP, N), BF16)
    gl = global_labels.reshape(1, N)
    w = weights.reshape(1, LEV)
    t, s0, s1, c0, c1 = pl.pallas_call(
        transport_kernel,
        out_shape=(pltpu.VMEM(((N + 2) * KP, N), F32), edge, edge, edge, edge),
        in_specs=[anywhere] * 3,
        out_specs=[vmem] * 5,
        scratch_shapes=[pltpu.VMEM((LEV, N, N), BF16)] * 3
        + [pltpu.VMEM((3, N, N), BF16), pltpu.SemaphoreType.DMA((len(CHUNKS), 3))],
        compiler_params=params(18),
        cost_estimate=cost(30_000_000, 23_000_000),
        name="transport",
    )(*(pltpu.with_memory_space_constraint(x, pltpu.HBM) for x in (humidity, wind_u, wind_v)))
    r1 = lax.ppermute(s1, "lat", [(i, (i + 1) % 8 if i % 2 else (i - 1) % 8) for i in range(8)])
    r0 = lax.ppermute(s0, "lat", [(i, i ^ 1) for i in range(8)])
    ro = lax.ppermute(c1, "lon", [(j, (j + 1) % 16 if j % 2 else (j - 1) % 16) for j in range(16)])
    rc = lax.ppermute(c0, "lon", [(j, j ^ 1) for j in range(16)])
    t0 = pl.pallas_call(
        sums_kernel,
        out_shape=pltpu.VMEM((KP, N), F32),
        in_specs=[vmem] * 2,
        out_specs=vmem,
        scratch_shapes=[pltpu.VMEM((N, N), jnp.int32)] * 2,
        compiler_params=params(8),
        cost_estimate=cost(600_000_000, 9_500_000),
        name="sums",
    )(t, labels)
    pay = pl.pallas_call(
        pack_kernel,
        out_shape=edge,
        in_specs=[vmem] * 7,
        out_specs=vmem,
        compiler_params=params(8),
        cost_estimate=cost(20_000_000, 300_000),
        name="pack",
    )(t0, r0, r1, rc, ro, labels, gl)
    p2 = lax.ppermute(pay, "lat", [(i, (i + 4) % 8) for i in range(8)])
    p1 = lax.ppermute(pay, "lon", [(j, j ^ 1) for j in range(16)])
    p3 = lax.ppermute(p2, "lon", [(j, j ^ 1) for j in range(16)])
    s = pl.pallas_call(
        smooth_kernel,
        out_shape=pltpu.VMEM((N * KP, N), F32),
        in_specs=[vmem] * 6,
        out_specs=vmem,
        scratch_shapes=[pltpu.VMEM((KP, N), F32)],
        compiler_params=params(16),
        cost_estimate=cost(1_200_000_000, 19_000_000),
        name="smooth",
    )(t, r0, r1, rc, ro, w)
    return pl.pallas_call(
        final_kernel,
        out_shape=jax.ShapeDtypeStruct((N, N), F32),
        in_specs=[vmem] * 8,
        out_specs=vmem,
        scratch_shapes=[pltpu.VMEM((N, N), F32)],
        compiler_params=params(8),
        cost_estimate=cost(300_000_000, 9_500_000),
        name="final",
    )(pay, p1, p2, p3, s, labels, gl, w)


def solution(mesh):
    return jax.shard_map(
        shards,
        mesh=mesh,
        in_specs=(
            P(None, "lat", "lon"),
            P(None, "lat", "lon"),
            P(None, "lat", "lon"),
            P(),
            P("lat", "lon"),
            P("lat", "lon", None),
        ),
        out_specs=P("lat", "lon"),
        check_vma=False,
    )
```

time: 260 us -> 33.5 us (0.13)
  waiting for transfers between devices: 85.2 us -> 1.72 us
  blocking collectives: 67.9 us -> 0 us
  other arithmetic: 32.5 us -> 0 us
  local copies, waits for them, and re-layouts: 32.5 us -> 0.01 us
  matrix products: 18.1 us -> 0 us
  Pallas kernels: 0 us -> 15.9 us
  between operations: 13.5 us -> 0.07 us
  starting transfers between devices: 9.84 us -> 15.7 us
    psum x1 -> x0, waiting for transfers between devices: 85.1 us -> none  [shards(): totals, counts = lax.psum((part_totals, part_counts), ('lat', 'lon'))]
    psum x1 -> x0, blocking collectives: 67.9 us -> none  [shards(): totals, counts = lax.psum((part_totals, part_counts), ('lat', 'lon'))]
    dot_general x6 -> x0, matrix products: 18.1 us -> none  [the longest x1 7.09 us: shards(): lax.dot_general(values_f32, weighted, (((0,), (0,)), ((), ())), precision...]
    reduce_sum x2 -> x0, other arithmetic: 17.8 us -> none  [the longest x1 16.9 us: shards(): own_term = jnp.sum(weights[:, None] * values_f32 * values_f32, axis=0)]
    slice x4 -> x0, local copies, waits for them, and re-layouts: 16.2 us -> none  [the longest x3 11.1 us: extended(): last = lax.slice_in_dim(x, length - width, length, axis=dim)]
    pallas_call x0 -> x5, Pallas kernels: none -> 15.9 us  [the longest x1 7.47 us: shards(): pl.pallas_call(transport_kernel, out_shape=(pltpu.VMEM(((N + 2) * KP, N),...]
    convert_element_type x1 -> x0, other arithmetic: 14 us -> none  [shards(): transport = (humidity.astype(jnp.float32) * wind_speed).astype(jnp.bfloat16)]
    ppermute x2 -> x0, local copies, waits for them, and re-layouts: 7.96 us -> none  [the longest x1 4.05 us: extended(): before = lax.ppermute(last, axis, up)]
  transfers between devices with their start and end apart: 5 -> 7, of which waited for: 1 -> 2; matrix products, arithmetic and copies ran while one was open for 6% -> 0% of each run, Pallas kernels for 0% -> 16%
where the time goes in v1:
time: 33.5 us; the launch traced here: 33.4 us
  Pallas kernels  15.9 us (47%)
  starting transfers between devices  15.7 us (47%)
  waiting for transfers between devices  1.72 us (5%)
    pallas_call x1, Pallas kernels, shards(): pl.pallas_call(transport_kernel, out_shape=(pltpu.VMEM(((N + 2) * KP, N),...  7.47 us
    ppermute x1, starting transfers between devices, shards(): r0 = lax.ppermute(s0, 'lat', [(i, i ^ 1) for i in range(8)])  4.51 us
    pallas_call x1, Pallas kernels, shards(): pl.pallas_call(smooth_kernel, out_shape=pltpu.VMEM((N * KP, N), F32), in_...  3.51 us
    ppermute x1, starting transfers between devices, shards(): p3 = lax.ppermute(p2, 'lon', [(j, j ^ 1) for j in range(16)])  3.15 us
    pallas_call x1, Pallas kernels, shards(): pl.pallas_call(final_kernel, out_shape=jax.ShapeDtypeStruct((N, N), F32),...  2.79 us
    ppermute x1, starting transfers between devices, shards(): lax.ppermute(s1, 'lat', [(i, (i + 1) % 8 if i % 2 else (i - 1) % 8) for i...  2.54 us
    ppermute x1, starting transfers between devices, shards(): p1 = lax.ppermute(pay, 'lon', [(j, j ^ 1) for j in range(16)])  2.39 us
    pallas_call x1, Pallas kernels, shards(): pl.pallas_call(sums_kernel, out_shape=pltpu.VMEM((KP, N), F32), in_specs=...  1.85 us
  transfers between devices with their start and end apart: 7, of which 2 were waited for; matrix products, arithmetic and copies ran while one was open for 0% of the time, Pallas kernels for 16%

profile of v1, /device:TPU:1, one launch (start us, length us, event | category | flops | bytes accessed | tf_op | source)
XLA Modules:
  0.0 33.4 jit_solution(8650360330558176187)
XLA Ops:
  0.0 0.0 copy-start
  0.0 7.5 %transport.1 = (f32[19760,128]{1,0:T(8,128)S(1)}, bf16[152,128]{1,0:T(8,128)(2,1)S(1)}, bf16[152,128]{1,0:T(8,128)(2,1)S(1)}, bf16[152,128]{1,0:T(8,128)(2,1)S(1)}, bf16[152,128]{1,0:T(8,128)(2,1)S(1)}) custom-call(bf16[137,128,128]{2,1,0:T(8,128)(2,1)} %h_hbm.1, bf16[137,128,128]{2,1,0:T(8,128)(2,1)} %u_hbm.1, bf16[137,128,128]{2,1,0:T(8,128)(2,1)} %v_hbm.1), custom_call_target="tpu_custom_call" | custom-call | flops 30000000 | bytes 23000000 | tf_op jit(solution)/shard_map/transport/pallas_call | solution.py:265
  7.5 4.5 %collective-permute-start = (bf16[152,128]{1,0:T(8,128)(2,1)S(1)}, bf16[152,128]{1,0:T(8,128)(2,1)S(1)}, u32[]{:S(2)}, u32[]{:S(2)}) collective-permute-start(bf16[152,128]{1,0:T(8,128)(2,1)S(1)} %get-tuple-element.11), channel_id=1, source_target_pairs={{0,16},{16,0},{32,48},{48,32},{64,80},{80,64},{96,112},{112,96},{1... | collective-permute-start | bytes 116744 | tf_op jit(solution)/shard_map/ppermute | solution.py:277
  12.0 2.5 %collective-permute-start.1 = (bf16[152,128]{1,0:T(8,128)(2,1)S(1)}, bf16[152,128]{1,0:T(8,128)(2,1)S(1)}, u32[]{:S(2)}, u32[]{:S(2)}) collective-permute-start(bf16[152,128]{1,0:T(8,128)(2,1)S(1)} %get-tuple-element.12), channel_id=1, source_target_pairs={{0,112},{16,32},{32,16},{48,64},{64,48},{80,96},{96,80},{112,0},{1... | collective-permute-start | bytes 116744 | tf_op jit(solution)/shard_map/ppermute | solution.py:276
  14.5 1.0 %collective-permute-start.2 = (bf16[152,128]{1,0:T(8,128)(2,1)S(1)}, bf16[152,128]{1,0:T(8,128)(2,1)S(1)}, u32[]{:S(2)}, u32[]{:S(2)}) collective-permute-start(bf16[152,128]{1,0:T(8,128)(2,1)S(1)} %get-tuple-element.13), channel_id=1, source_target_pairs={{0,1},{1,0},{2,3},{3,2},{4,5},{5,4},{6,7},{7,6},{8,9},{9,8},{10,11... | collective-permute-start | bytes 116744 | tf_op jit(solution)/shard_map/ppermute | solution.py:279
  15.5 1.1 %collective-permute-start.3 = (bf16[152,128]{1,0:T(8,128)(2,1)S(1)}, bf16[152,128]{1,0:T(8,128)(2,1)S(1)}, u32[]{:S(2)}, u32[]{:S(2)}) collective-permute-start(bf16[152,128]{1,0:T(8,128)(2,1)S(1)} %get-tuple-element.14), channel_id=1, source_target_pairs={{0,15},{1,2},{2,1},{3,4},{4,3},{5,6},{6,5},{7,8},{8,7},{9,10},{10,... | collective-permute-start | bytes 116744 | tf_op jit(solution)/shard_map/ppermute | solution.py:278
  16.6 0.0 copy-done
  16.6 0.0 copy-start.2
  16.6 0.0 copy-start.1
  16.6 1.8 %sums.1.t0_ref = f32[152,128]{1,0:T(8,128)S(1)} custom-call(f32[19760,128]{1,0:T(8,128)S(1)} %get-tuple-element.10.t_ref, s32[128,128]{1,0:T(8,128)S(1)} %copy-done), custom_call_target="tpu_custom_call" | custom-call | flops 600000000 | bytes 9500000 | tf_op jit(solution)/shard_map/sums/pallas_call | solution.py:280
  18.4 0.0 collective-permute-done.r0
  18.4 0.0 collective-permute-done.1.r1
  18.5 0.0 collective-permute-done.2.rc
  18.5 0.7 %collective-permute-done.3.ro = bf16[152,128]{1,0:T(8,128)(2,1)S(1)} collective-permute-done((bf16[152,128]{1,0:T(8,128)(2,1)S(1)}, bf16[152,128]{1,0:T(8,128)(2,1)S(1)}, u32[]{:S(2)}, u32[]{:S(2)}) %collective-permute-start.3) | collective-permute-done | bytes 38944 | tf_op jit(solution)/shard_map/ppermute | solution.py:278
  19.2 0.0 copy-done.2
  19.2 0.3 pack.1.p0
  19.5 1.0 %collective-permute-start.5 = (bf16[152,128]{1,0:T(8,128)(2,1)S(1)}, bf16[152,128]{1,0:T(8,128)(2,1)S(1)}, u32[]{:S(2)}, u32[]{:S(2)}) collective-permute-start(bf16[152,128]{1,0:T(8,128)(2,1)S(1)} %pack.1.p0), channel_id=1, source_target_pairs={{0,64},{16,80},{32,96},{48,112},{64,0},{80,16},{96,32},{112,48},{1... | collective-permute-start | bytes 116744 | tf_op jit(solution)/shard_map/ppermute | solution.py:299
  20.6 2.4 %collective-permute-start.4 = (bf16[152,128]{1,0:T(8,128)(2,1)S(1)}, bf16[152,128]{1,0:T(8,128)(2,1)S(1)}, u32[]{:S(2)}, u32[]{:S(2)}) collective-permute-start(bf16[152,128]{1,0:T(8,128)(2,1)S(1)} %pack.1.p0), channel_id=1, source_target_pairs={{0,1},{1,0},{2,3},{3,2},{4,5},{5,4},{6,7},{7,6},{8,9},{9,8},{10,11... | collective-permute-start | bytes 116744 | tf_op jit(solution)/shard_map/ppermute | solution.py:300
  23.0 1.0 %collective-permute-done.5.p2 = bf16[152,128]{1,0:T(8,128)(2,1)S(1)} collective-permute-done((bf16[152,128]{1,0:T(8,128)(2,1)S(1)}, bf16[152,128]{1,0:T(8,128)(2,1)S(1)}, u32[]{:S(2)}, u32[]{:S(2)}) %collective-permute-start.5) | collective-permute-done | bytes 38944 | tf_op jit(solution)/shard_map/ppermute | solution.py:299
  23.9 3.2 %collective-permute-start.6 = (bf16[152,128]{1,0:T(8,128)(2,1)S(1)}, bf16[152,128]{1,0:T(8,128)(2,1)S(1)}, u32[]{:S(2)}, u32[]{:S(2)}) collective-permute-start(bf16[152,128]{1,0:T(8,128)(2,1)S(1)} %collective-permute-done.5.p2), channel_id=1, source_target_pairs={{0,1},{1,0},{2,3},{3,2},{4,5},{5,4},{6,7},{7,6},{8,9},{9,8},{10,11... | collective-permute-start | bytes 116744 | tf_op jit(solution)/shard_map/ppermute | solution.py:301
  27.1 0.0 copy-done.1
  27.1 3.5 %smooth.1.s_ref = f32[19456,128]{1,0:T(8,128)S(1)} custom-call(f32[19760,128]{1,0:T(8,128)S(1)} %get-tuple-element.10.t_ref, bf16[152,128]{1,0:T(8,128)(2,1)S(1)} %collective-permute-done.r0, bf16[152,128]{1,0:T(8,128)(2,1)S(1)} %collective-permute-done.1.r1, bf16[152,128]{1,0:T(8,128)(2,1)S(1)} %collective-permute-done.2.rc, ...), custom_call_target="tpu_custom_call" | custom-call | flops 1200000000 | bytes 19000000 | tf_op jit(solution)/shard_map/smooth/pallas_call | solution.py:302
  30.6 0.0 collective-permute-done.4.p1
  30.6 0.0 collective-permute-done.6.p3
  30.6 2.8 %final.1 = f32[128,128]{1,0:T(8,128)} custom-call(bf16[152,128]{1,0:T(8,128)(2,1)S(1)} %pack.1.p0, bf16[152,128]{1,0:T(8,128)(2,1)S(1)} %collective-permute-done.4.p1, bf16[152,128]{1,0:T(8,128)(2,1)S(1)} %collective-permute-done.5.p2, bf16[152,128]{1,0:T(8,128)(2,1)S(1)} %collective-permute-done.6.p3, f32[19456,128]{1,0:T(8,128)S(1)} %smooth.1.s_ref, ...), custom_call_target="tpu_custom_call" | custom-call | flops 300000000 | bytes 9500000 | tf_op jit(solution)/shard_map/final/pallas_call | solution.py:312
Async XLA Ops:
  0.0 16.6 %copy-start = (s32[128,128]{1,0:T(8,128)S(1)}, s32[128,128]{1,0:T(8,128)}, u32[]{:S(2)}) copy-start(s32[128,128]{1,0:T(8,128)} %lab_ref.5) | copy-start | bytes 196612
  7.5 11.0 %collective-permute-start = (bf16[152,128]{1,0:T(8,128)(2,1)S(1)}, bf16[152,128]{1,0:T(8,128)(2,1)S(1)}, u32[]{:S(2)}, u32[]{:S(2)}) collective-permute-start(bf16[152,128]{1,0:T(8,128)(2,1)S(1)} %get-tuple-element.11), channel_id=1, source_target_pairs={{0,16},{16,0},{32,48},{48,32},{64,80},{80,64},{96,112},{112,96},{1... | collective-permute-start | bytes 116744 | tf_op jit(solution)/shard_map/ppermute | solution.py:277
  12.0 6.5 %collective-permute-start.1 = (bf16[152,128]{1,0:T(8,128)(2,1)S(1)}, bf16[152,128]{1,0:T(8,128)(2,1)S(1)}, u32[]{:S(2)}, u32[]{:S(2)}) collective-permute-start(bf16[152,128]{1,0:T(8,128)(2,1)S(1)} %get-tuple-element.12), channel_id=1, source_target_pairs={{0,112},{16,32},{32,16},{48,64},{64,48},{80,96},{96,80},{112,0},{1... | collective-permute-start | bytes 116744 | tf_op jit(solution)/shard_map/ppermute | solution.py:276
  14.5 3.9 %collective-permute-start.2 = (bf16[152,128]{1,0:T(8,128)(2,1)S(1)}, bf16[152,128]{1,0:T(8,128)(2,1)S(1)}, u32[]{:S(2)}, u32[]{:S(2)}) collective-permute-start(bf16[152,128]{1,0:T(8,128)(2,1)S(1)} %get-tuple-element.13), channel_id=1, source_target_pairs={{0,1},{1,0},{2,3},{3,2},{4,5},{5,4},{6,7},{7,6},{8,9},{9,8},{10,11... | collective-permute-start | bytes 116744 | tf_op jit(solution)/shard_map/ppermute | solution.py:279
  15.5 3.7 %collective-permute-start.3 = (bf16[152,128]{1,0:T(8,128)(2,1)S(1)}, bf16[152,128]{1,0:T(8,128)(2,1)S(1)}, u32[]{:S(2)}, u32[]{:S(2)}) collective-permute-start(bf16[152,128]{1,0:T(8,128)(2,1)S(1)} %get-tuple-element.14), channel_id=1, source_target_pairs={{0,15},{1,2},{2,1},{3,4},{4,3},{5,6},{6,5},{7,8},{8,7},{9,10},{10,... | collective-permute-start | bytes 116744 | tf_op jit(solution)/shard_map/ppermute | solution.py:278
  16.6 2.6 %copy-start.2 = (s32[1,1,128]{2,1,0:T(1,128)S(1)}, s32[1,1,128]{2,1,0:T(1,128)}, u32[]{:S(2)}) copy-start(s32[1,1,128]{2,1,0:T(1,128)} %param.11) | copy-start | bytes 1540
  16.6 10.5 %copy-start.1 = (f32[137]{0:T(256)S(1)}, f32[137]{0:T(256)}, u32[]{:S(2)}) copy-start(f32[137]{0:T(256)} %param.9) | copy-start | bytes 1648
  19.5 4.4 %collective-permute-start.5 = (bf16[152,128]{1,0:T(8,128)(2,1)S(1)}, bf16[152,128]{1,0:T(8,128)(2,1)S(1)}, u32[]{:S(2)}, u32[]{:S(2)}) collective-permute-start(bf16[152,128]{1,0:T(8,128)(2,1)S(1)} %pack.1.p0), channel_id=1, source_target_pairs={{0,64},{16,80},{32,96},{48,112},{64,0},{80,16},{96,32},{112,48},{1... | collective-permute-start | bytes 116744 | tf_op jit(solution)/shard_map/ppermute | solution.py:299
  20.6 10.0 %collective-permute-start.4 = (bf16[152,128]{1,0:T(8,128)(2,1)S(1)}, bf16[152,128]{1,0:T(8,128)(2,1)S(1)}, u32[]{:S(2)}, u32[]{:S(2)}) collective-permute-start(bf16[152,128]{1,0:T(8,128)(2,1)S(1)} %pack.1.p0), channel_id=1, source_target_pairs={{0,1},{1,0},{2,3},{3,2},{4,5},{5,4},{6,7},{7,6},{8,9},{9,8},{10,11... | collective-permute-start | bytes 116744 | tf_op jit(solution)/shard_map/ppermute | solution.py:300
  23.9 6.7 %collective-permute-start.6 = (bf16[152,128]{1,0:T(8,128)(2,1)S(1)}, bf16[152,128]{1,0:T(8,128)(2,1)S(1)}, u32[]{:S(2)}, u32[]{:S(2)}) collective-permute-start(bf16[152,128]{1,0:T(8,128)(2,1)S(1)} %collective-permute-done.5.p2), channel_id=1, source_target_pairs={{0,1},{1,0},{2,3},{3,2},{4,5},{5,4},{6,7},{7,6},{8,9},{9,8},{10,11... | collective-permute-start | bytes 116744 | tf_op jit(solution)/shard_map/ppermute | solution.py:301

commit v2 on v1

--- a/solution.py
+++ b/solution.py
@@ -1,3 +1,5 @@
+import functools
+
 import jax
 import jax.numpy as jnp
 from jax import lax
@@ -68,12 +70,11 @@
         parts = []
         for b in range(0, N, 32):
             rows = pl.ds(b, 32)
-            u = ub[k, rows, :].astype(F32)
-            v = vb[k, rows, :].astype(F32)
-            x = u * u + v * v + 1.0
-            t = (hb[k, rows, :].astype(F32) * (x * lax.rsqrt(x))).astype(BF16)
-            t_ref[pl.ds((1 + b) * KP + k, 32, stride=KP), :] = t.astype(F32)
-            parts.append(t)
+            u, v = ub[k, rows, :], vb[k, rows, :]
+            x = (u * u + v * v).astype(F32) + 1.0
+            t = hb[k, rows, :].astype(F32) * (x * lax.rsqrt(x))
+            t_ref[pl.ds((1 + b) * KP + k, 32, stride=KP), :] = t
+            parts.append(t.astype(BF16))
         return jnp.concatenate(parts, axis=0)
 
     def group(k, size):
@@ -124,21 +125,25 @@
     lane = iota((N, N), 1)
     west_ref[...] = jnp.where(lane == 0, -1, pltpu.roll(lab, 1, 1))
     east_ref[...] = jnp.where(lane == N - 1, -1, pltpu.roll(lab, N - 1, 1))
-    ids = iota((N, N), 0)
+    ids = iota((N, N), 0).astype(F32).astype(BF16)
     t0_ref[...] = jnp.zeros((KP, N), F32)
+    last = iota((8, N), 0) + (LEV - LEV % 8)
 
     def patch_row(q):
         base = pl.multiple_of((1 + 4 * q) * KP, 8)
         x = [t_ref[pl.ds(base + m * KP, KP), :] for m in range(-1, 5)]
         whole = x[1] + x[2] + x[3] + x[4]
-        step = jnp.where(iota((KP, N), 0) == LEV, 32.0, (x[0] - x[4]) + (x[5] - x[1]))
+        step = (x[0] - x[4]) + (x[5] - x[1])
+        step = jnp.concatenate([step[: LEV - LEV % 8], jnp.where(last == LEV, 32.0, step[LEV - LEV % 8 : KP - 8]), step[KP - 8 :]], axis=0)
         left = jnp.concatenate([whole.astype(BF16), step.astype(BF16)], axis=1)
-        r = pl.ds(4 * q, 1)
-        here = jnp.where(lab_ref[r, :] == ids, 0.125, 0.0)
-        west = jnp.where(west_ref[r, :] == ids, 0.125, 0.0)
-        east = jnp.where(east_ref[r, :] == ids, 0.125, 0.0)
-        spread = 6.0 * here + (west + east)
-        return left, jnp.concatenate([spread.astype(BF16), here.astype(BF16)], axis=1)
+
+        def marks(ref):
+            row = ref[pl.ds(4 * q, 1), :].astype(F32).astype(BF16)
+            return jnp.where(row == ids, BF16(0.125), BF16(0.0))
+
+        here = marks(lab_ref)
+        spread = here * BF16(6.0) + (marks(west_ref) + marks(east_ref))
+        return left, jnp.concatenate([spread, here], axis=1)
 
     def patch_rows(i, _):
         pairs = [patch_row(16 * i + m) for m in range(16)]
@@ -173,43 +178,43 @@
     pay_ref[...] = total.astype(BF16)
 
 
-def smooth_kernel(t_ref, r0, r1, rc, ro, w_ref, s_ref, root_ref):
+def smooth_kernel(half, t_ref, r0, r1, rc, ro, w_ref, s_ref, root_ref):
     north, south, west, east = halos(r0, r1, rc, ro)
     low = iota((KP, N), 1) < 64
-    sides = (
-        jnp.where(low, west, pltpu.roll(east, 64, 1)).astype(BF16),
-        jnp.where(low, pltpu.roll(west, 64, 1), east).astype(BF16),
-    )
-    root_ref[...] = jnp.sqrt(column(w_ref[...], KP)) + jnp.zeros((KP, N), F32)
+    if half == 0:
+        side = jnp.where(low, west, pltpu.roll(east, 64, 1)).astype(BF16)
+    else:
+        side = jnp.where(low, pltpu.roll(west, 64, 1), east).astype(BF16)
+    root_ref[...] = jnp.sqrt(column(w_ref[...], KP)) * 0.125 + jnp.zeros((KP, N), F32)
     a, c = iota((2 * N, N), 0), iota((2 * N, N), 1)
-    band = jnp.where(a == c, 0.5, jnp.where(jnp.abs(a - c) == 1, 0.125, 0.0))
-    side = jnp.where(c == jnp.where(a < N + 64, 0, N - 1), 0.125, 0.0)
-    right = jnp.where(a < N, band, side).astype(BF16)
+    band = jnp.where(a == c, 4.0, jnp.where(jnp.abs(a - c) == 1, 1.0, 0.0))
+    edge = jnp.where(c == jnp.where(a < N + 64, 0, N - 1), 1.0, 0.0)
+    right = jnp.where(a < N, band, edge).astype(BF16)
     lane = lax.rem(iota((1, N), 1), 64)
 
     def at(r):
         return pl.ds(pl.multiple_of(r * KP, 8), KP)
 
-    for half in range(2):
-
-        def rows(i, _, half=half):
-            top = 64 * half + 32 * i
-            lefts = []
-            for m in range(32):
-                mine = jnp.where(lane == 32 * i + m, 1.0, 0.0).astype(BF16)
-                lefts.append(jnp.concatenate([t_ref[at(top + m + 1), :].astype(BF16), sides[half] * mine], axis=1))
-            across = dot(jnp.concatenate(lefts, axis=0), right, NN)
-            for m in range(32):
-                along = t_ref[at(top + m), :] + t_ref[at(top + m + 2), :]
-                s_ref[at(top + m), :] = (across[m * KP : (m + 1) * KP] + 0.125 * along) * root_ref[...]
-            return 0
-
-        lax.fori_loop(0, 2, rows, 0)
-    s_ref[at(0), :] += 0.125 * north * root_ref[...]
-    s_ref[at(N - 1), :] += 0.125 * south * root_ref[...]
-
-
-def final_kernel(p0, p1, p2, p3, s_ref, lab_ref, gl_ref, w_ref, out_ref, e_ref):
+    def rows(i, _):
+        top = 64 * half + 32 * i
+        lefts = []
+        for m in range(32):
+            mine = jnp.where(lane == 32 * i + m, 1.0, 0.0).astype(BF16)
+            lefts.append(jnp.concatenate([t_ref[at(top + m + 1), :].astype(BF16), side * mine], axis=1))
+        across = dot(jnp.concatenate(lefts, axis=0), right, NN)
+        for m in range(32):
+            along = t_ref[at(top + m), :] + t_ref[at(top + m + 2), :]
+            s_ref[at(32 * i + m), :] = (across[m * KP : (m + 1) * KP] + along) * root_ref[...]
+        return 0
+
+    lax.fori_loop(0, 2, rows, 0)
+    if half == 0:
+        s_ref[at(0), :] += north * root_ref[...]
+    else:
+        s_ref[at(63), :] += south * root_ref[...]
+
+
+def final_kernel(p0, p1, p2, p3, s0_ref, s1_ref, lab_ref, gl_ref, w_ref, out_ref, e_ref):
     own = column(gl_ref[...].astype(F32), N) + jnp.zeros((N, N), F32)
     lefts, rights = [], []
     for p in (p0, p1, p2, p3):
@@ -222,30 +227,35 @@
     root = jnp.sqrt(column(w_ref[...], KP))
     profile = root * (total / jnp.maximum(count, 1.0))
     energy = jnp.sum(profile * profile, axis=0, keepdims=True)
-    row = iota((KP, N), 0)
-    table = jnp.where(row == LEV, energy, profile)
+    table = jnp.where(iota((KP, N), 0) == LEV, energy, profile)
     hi = table.astype(BF16)
     left = jnp.concatenate([hi, (table - hi.astype(F32)).astype(BF16)], axis=1)
-    ids = iota((N, N), 0)
-
-    def patch_row(q):
-        mark = jnp.where(lab_ref[pl.ds(4 * q, 1), :] == ids, 1.0, 0.0).astype(BF16)
+    ids = iota((N, N), 0).astype(F32).astype(BF16)
+    base = LEV - LEV % 8
+    inside = iota((8, N), 0) + base < LEV
+
+    def patch_row(q, s_ref, top):
+        row = lab_ref[pl.ds(4 * q, 1), :].astype(F32).astype(BF16)
+        mark = jnp.where(row == ids, BF16(1.0), BF16(0.0))
         placed = dot(left, jnp.concatenate([mark, mark], axis=0), NN)
         e = placed[LEV : LEV + 1]
-        placed = jnp.where(row == LEV, 0.0, placed)
+        placed = jnp.concatenate([placed[:base], jnp.where(inside, placed[base : base + 8], 0.0)], axis=0)
         for m in range(4):
             r = 4 * q + m
-            d = s_ref[pl.ds(pl.multiple_of(r * KP, 8), KP), :] - placed
+            d = s_ref[pl.ds((r - top) * KP, base + 8), :] - placed
             out_ref[pl.ds(r, 1), :] = jnp.sum(d * d, axis=0, keepdims=True)
             e_ref[pl.ds(r, 1), :] = e
 
-    def patch_rows(i, _):
-        for m in range(16):
-            patch_row(16 * i + m)
-        return 0
-
-    lax.fori_loop(0, N // 64, patch_rows, 0)
+    for half, s_ref in enumerate((s0_ref, s1_ref)):
+        for q in range(16 * half, 16 * half + 16):
+            patch_row(q, s_ref, 64 * half)
     out_ref[...] = jnp.sqrt(out_ref[...] / e_ref[...])
+
+
+def outer(i, j):
+    if i in (0, 7):
+        return 16 * i + (j ^ 1)
+    return 16 * (i + 1 if i % 2 else i - 1) + j
 
 
 def params(mib):
@@ -273,7 +283,7 @@
         cost_estimate=cost(30_000_000, 23_000_000),
         name="transport",
     )(*(pltpu.with_memory_space_constraint(x, pltpu.HBM) for x in (humidity, wind_u, wind_v)))
-    r1 = lax.ppermute(s1, "lat", [(i, (i + 1) % 8 if i % 2 else (i - 1) % 8) for i in range(8)])
+    r1 = lax.ppermute(s1, ("lat", "lon"), [(16 * i + j, outer(i, j)) for i in range(8) for j in range(16)])
     r0 = lax.ppermute(s0, "lat", [(i, i ^ 1) for i in range(8)])
     ro = lax.ppermute(c1, "lon", [(j, (j + 1) % 16 if j % 2 else (j - 1) % 16) for j in range(16)])
     rc = lax.ppermute(c0, "lon", [(j, j ^ 1) for j in range(16)])
@@ -299,26 +309,29 @@
     p2 = lax.ppermute(pay, "lat", [(i, (i + 4) % 8) for i in range(8)])
     p1 = lax.ppermute(pay, "lon", [(j, j ^ 1) for j in range(16)])
     p3 = lax.ppermute(p2, "lon", [(j, j ^ 1) for j in range(16)])
-    s = pl.pallas_call(
-        smooth_kernel,
-        out_shape=pltpu.VMEM((N * KP, N), F32),
-        in_specs=[vmem] * 6,
-        out_specs=vmem,
-        scratch_shapes=[pltpu.VMEM((KP, N), F32)],
-        compiler_params=params(16),
-        cost_estimate=cost(1_200_000_000, 19_000_000),
-        name="smooth",
-    )(t, r0, r1, rc, ro, w)
+    s0, s1 = (
+        pl.pallas_call(
+            functools.partial(smooth_kernel, half),
+            out_shape=pltpu.VMEM((N // 2 * KP, N), F32),
+            in_specs=[vmem] * 6,
+            out_specs=vmem,
+            scratch_shapes=[pltpu.VMEM((KP, N), F32)],
+            compiler_params=params(12),
+            cost_estimate=cost(600_000_000, 9_500_000),
+            name="smooth",
+        )(t, r0, r1, rc, ro, w)
+        for half in range(2)
+    )
     return pl.pallas_call(
         final_kernel,
         out_shape=jax.ShapeDtypeStruct((N, N), F32),
-        in_specs=[vmem] * 8,
+        in_specs=[vmem] * 9,
         out_specs=vmem,
         scratch_shapes=[pltpu.VMEM((N, N), F32)],
         compiler_params=params(8),
         cost_estimate=cost(300_000_000, 9_500_000),
         name="final",
-    )(pay, p1, p2, p3, s, labels, gl, w)
+    )(pay, p1, p2, p3, s0, s1, labels, gl, w)
 
 
 def solution(mesh):

time: 33.5 us -> 29.2 us (0.87)
  starting transfers between devices: 15.7 us -> 13 us
  waiting for transfers between devices: 1.72 us -> 0.79 us
  Pallas kernels: 15.9 us -> 15.3 us
    ppermute x1, starting transfers between devices: 3.15 us -> 0.13 us  [shards(): p3 = lax.ppermute(p2, 'lon', [(j, j ^ 1) for j in range(16)])]
    ppermute x1, starting transfers between devices: 1.04 us -> 3.86 us  [shards(): p2 = lax.ppermute(pay, 'lat', [(i, (i + 4) % 8) for i in range(8)])]
    ppermute x1, starting transfers between devices: 2.54 us -> 0.95 us  [shards(): lax.ppermute(s1, ('lat', 'lon'), [(16 * i + j, outer(i, j)) for i in rang...]
    ppermute x1, waiting for transfers between devices: 0.99 us -> 0.01 us  [shards(): p2 = lax.ppermute(pay, 'lat', [(i, (i + 4) % 8) for i in range(8)])]
    ppermute x1, starting transfers between devices: 0.96 us -> 0.01 us  [shards(): rc = lax.ppermute(c0, 'lon', [(j, j ^ 1) for j in range(16)])]
    pallas_call x1, Pallas kernels: 1.85 us -> 1.47 us  [shards(): pl.pallas_call(sums_kernel, out_shape=pltpu.VMEM((KP, N), F32), in_specs=...]
    pallas_call x1 -> x2, Pallas kernels: 3.51 us -> 3.62 us  [shards(): pl.pallas_call(functools.partial(smooth_kernel, half), out_shape=pltpu.VM...]
  transfers between devices with their start and end apart: 7 -> 7, of which waited for: 2 -> 1; matrix products, arithmetic and copies ran while one was open for 0% -> 0% of each run, Pallas kernels for 16% -> 17%
where the time goes in v2:
time: 29.2 us; the launch traced here: 29.1 us
  Pallas kernels  15.3 us (52%)
  starting transfers between devices  13 us (45%)
  waiting for transfers between devices  0.79 us (3%)
    pallas_call x1, Pallas kernels, shards(): pl.pallas_call(transport_kernel, out_shape=(pltpu.VMEM(((N + 2) * KP, N),...  7.2 us
    ppermute x1, starting transfers between devices, shards(): r0 = lax.ppermute(s0, 'lat', [(i, i ^ 1) for i in range(8)])  4.51 us
    ppermute x1, starting transfers between devices, shards(): p2 = lax.ppermute(pay, 'lat', [(i, (i + 4) % 8) for i in range(8)])  3.86 us
    pallas_call x2, Pallas kernels, shards(): pl.pallas_call(functools.partial(smooth_kernel, half), out_shape=pltpu.VM...  3.62 us
    pallas_call x1, Pallas kernels, shards(): pl.pallas_call(final_kernel, out_shape=jax.ShapeDtypeStruct((N, N), F32),...  2.63 us
    ppermute x1, starting transfers between devices, shards(): p1 = lax.ppermute(pay, 'lon', [(j, j ^ 1) for j in range(16)])  2.39 us
    pallas_call x1, Pallas kernels, shards(): pl.pallas_call(sums_kernel, out_shape=pltpu.VMEM((KP, N), F32), in_specs=...  1.47 us
    ppermute x1, starting transfers between devices, shards(): lax.ppermute(c1, 'lon', [(j, (j + 1) % 16 if j % 2 else (j - 1) % 16) for...  1.13 us
  transfers between devices with their start and end apart: 7, of which 1 were waited for; matrix products, arithmetic and copies ran while one was open for 0% of the time, Pallas kernels for 17%

profile of v2, /device:TPU:1, one launch (start us, length us, event | category | flops | bytes accessed | tf_op | source)
XLA Modules:
  0.0 29.1 jit_solution(8351480613020791349)
XLA Ops:
  0.0 0.0 copy-start
  0.0 7.2 %transport.1 = (f32[19760,128]{1,0:T(8,128)S(1)}, bf16[152,128]{1,0:T(8,128)(2,1)S(1)}, bf16[152,128]{1,0:T(8,128)(2,1)S(1)}, bf16[152,128]{1,0:T(8,128)(2,1)S(1)}, bf16[152,128]{1,0:T(8,128)(2,1)S(1)}) custom-call(bf16[137,128,128]{2,1,0:T(8,128)(2,1)} %h_hbm.1, bf16[137,128,128]{2,1,0:T(8,128)(2,1)} %u_hbm.1, bf16[137,128,128]{2,1,0:T(8,128)(2,1)} %v_hbm.1), custom_call_target="tpu_custom_call" | custom-call | flops 30000000 | bytes 23000000 | tf_op jit(solution)/shard_map/transport/pallas_call | solution.py:275
  7.2 4.5 %collective-permute-start = (bf16[152,128]{1,0:T(8,128)(2,1)S(1)}, bf16[152,128]{1,0:T(8,128)(2,1)S(1)}, u32[]{:S(2)}, u32[]{:S(2)}) collective-permute-start(bf16[152,128]{1,0:T(8,128)(2,1)S(1)} %get-tuple-element.11), channel_id=1, source_target_pairs={{0,16},{16,0},{32,48},{48,32},{64,80},{80,64},{96,112},{112,96},{1... | collective-permute-start | bytes 116744 | tf_op jit(solution)/shard_map/ppermute | solution.py:287
  11.7 1.0 %collective-permute-start.1 = (bf16[152,128]{1,0:T(8,128)(2,1)S(1)}, bf16[152,128]{1,0:T(8,128)(2,1)S(1)}, u32[]{:S(2)}, u32[]{:S(2)}) collective-permute-start(bf16[152,128]{1,0:T(8,128)(2,1)S(1)} %get-tuple-element.12), channel_id=1, source_target_pairs={{0,1},{1,0},{2,3},{3,2},{4,5},{5,4},{6,7},{7,6},{8,9},{9,8},{10,11... | collective-permute-start | bytes 116744 | tf_op jit(solution)/shard_map/ppermute | solution.py:286
  12.7 0.0 collective-permute-start.2
  12.7 1.1 %collective-permute-start.3 = (bf16[152,128]{1,0:T(8,128)(2,1)S(1)}, bf16[152,128]{1,0:T(8,128)(2,1)S(1)}, u32[]{:S(2)}, u32[]{:S(2)}) collective-permute-start(bf16[152,128]{1,0:T(8,128)(2,1)S(1)} %get-tuple-element.14), channel_id=1, source_target_pairs={{0,15},{1,2},{2,1},{3,4},{4,3},{5,6},{6,5},{7,8},{8,7},{9,10},{10,... | collective-permute-start | bytes 116744 | tf_op jit(solution)/shard_map/ppermute | solution.py:288
  13.8 0.0 copy-done
  13.8 0.0 copy-start.2
  13.8 0.0 copy-start.1
  13.8 1.5 %sums.1.t0_ref = f32[152,128]{1,0:T(8,128)S(1)} custom-call(f32[19760,128]{1,0:T(8,128)S(1)} %get-tuple-element.10.t_ref, s32[128,128]{1,0:T(8,128)S(1)} %copy-done), custom_call_target="tpu_custom_call" | custom-call | flops 600000000 | bytes 9500000 | tf_op jit(solution)/shard_map/sums/pallas_call | solution.py:290
  15.3 0.0 collective-permute-done.r0
  15.3 0.0 collective-permute-done.1.r1
  15.3 0.0 collective-permute-done.2.rc
  15.3 0.8 %collective-permute-done.3.ro = bf16[152,128]{1,0:T(8,128)(2,1)S(1)} collective-permute-done((bf16[152,128]{1,0:T(8,128)(2,1)S(1)}, bf16[152,128]{1,0:T(8,128)(2,1)S(1)}, u32[]{:S(2)}, u32[]{:S(2)}) %collective-permute-start.3) | collective-permute-done | bytes 38944 | tf_op jit(solution)/shard_map/ppermute | solution.py:288
  16.1 0.0 copy-done.2
  16.1 0.3 %pack.1.p0 = bf16[152,128]{1,0:T(8,128)(2,1)S(1)} custom-call(f32[152,128]{1,0:T(8,128)S(1)} %sums.1.t0_ref, bf16[152,128]{1,0:T(8,128)(2,1)S(1)} %collective-permute-done.r0, bf16[152,128]{1,0:T(8,128)(2,1)S(1)} %collective-permute-done.1.r1, bf16[152,128]{1,0:T(8,128)(2,1)S(1)} %collective-permute-done.2.rc, ...), custom_call_target="tpu_custom_call" | custom-call | flops 20000000 | bytes 300000 | tf_op jit(solution)/shard_map/pack/pallas_call | solution.py:300
  16.4 3.9 %collective-permute-start.5 = (bf16[152,128]{1,0:T(8,128)(2,1)S(1)}, bf16[152,128]{1,0:T(8,128)(2,1)S(1)}, u32[]{:S(2)}, u32[]{:S(2)}) collective-permute-start(bf16[152,128]{1,0:T(8,128)(2,1)S(1)} %pack.1.p0), channel_id=1, source_target_pairs={{0,64},{16,80},{32,96},{48,112},{64,0},{80,16},{96,32},{112,48},{1... | collective-permute-start | bytes 116744 | tf_op jit(solution)/shard_map/ppermute | solution.py:309
  20.3 2.4 %collective-permute-start.4 = (bf16[152,128]{1,0:T(8,128)(2,1)S(1)}, bf16[152,128]{1,0:T(8,128)(2,1)S(1)}, u32[]{:S(2)}, u32[]{:S(2)}) collective-permute-start(bf16[152,128]{1,0:T(8,128)(2,1)S(1)} %pack.1.p0), channel_id=1, source_target_pairs={{0,1},{1,0},{2,3},{3,2},{4,5},{5,4},{6,7},{7,6},{8,9},{9,8},{10,11... | collective-permute-start | bytes 116744 | tf_op jit(solution)/shard_map/ppermute | solution.py:310
  22.7 0.0 copy-done.1
  22.7 1.8 %smooth.3.s1_ref = f32[9728,128]{1,0:T(8,128)S(1)} custom-call(f32[19760,128]{1,0:T(8,128)S(1)} %get-tuple-element.10.t_ref, bf16[152,128]{1,0:T(8,128)(2,1)S(1)} %collective-permute-done.r0, bf16[152,128]{1,0:T(8,128)(2,1)S(1)} %collective-permute-done.1.r1, bf16[152,128]{1,0:T(8,128)(2,1)S(1)} %collective-permute-done.2.rc, ...), custom_call_target="tpu_custom_call" | custom-call | flops 600000000 | bytes 9500000 | tf_op jit(solution)/shard_map/smooth/pallas_call | solution.py:313
  24.5 0.0 collective-permute-done.5.p2
  24.5 0.1 collective-permute-start.6
  24.6 1.8 %smooth.2.s0_ref = f32[9728,128]{1,0:T(8,128)S(1)} custom-call(f32[19760,128]{1,0:T(8,128)S(1)} %get-tuple-element.10.t_ref, bf16[152,128]{1,0:T(8,128)(2,1)S(1)} %collective-permute-done.r0, bf16[152,128]{1,0:T(8,128)(2,1)S(1)} %collective-permute-done.1.r1, bf16[152,128]{1,0:T(8,128)(2,1)S(1)} %collective-permute-done.2.rc, ...), custom_call_target="tpu_custom_call" | custom-call | flops 600000000 | bytes 9500000 | tf_op jit(solution)/shard_map/smooth/pallas_call | solution.py:313
  26.5 0.0 collective-permute-done.4.p1
  26.5 0.0 collective-permute-done.6.p3
  26.5 2.6 %final.1 = f32[128,128]{1,0:T(8,128)} custom-call(bf16[152,128]{1,0:T(8,128)(2,1)S(1)} %pack.1.p0, bf16[152,128]{1,0:T(8,128)(2,1)S(1)} %collective-permute-done.4.p1, bf16[152,128]{1,0:T(8,128)(2,1)S(1)} %collective-permute-done.5.p2, bf16[152,128]{1,0:T(8,128)(2,1)S(1)} %collective-permute-done.6.p3, f32[9728,128]{1,0:T(8,128)S(1)} %smooth.2.s0_ref, ...), custom_call_target="tpu_custom_call" | custom-call | flops 300000000 | bytes 9500000 | tf_op jit(solution)/shard_map/final/pallas_call | solution.py:325
Async XLA Ops:
  0.0 13.8 %copy-start = (s32[128,128]{1,0:T(8,128)S(1)}, s32[128,128]{1,0:T(8,128)}, u32[]{:S(2)}) copy-start(s32[128,128]{1,0:T(8,128)} %lab_ref.5) | copy-start | bytes 196612
  7.2 8.1 %collective-permute-start = (bf16[152,128]{1,0:T(8,128)(2,1)S(1)}, bf16[152,128]{1,0:T(8,128)(2,1)S(1)}, u32[]{:S(2)}, u32[]{:S(2)}) collective-permute-start(bf16[152,128]{1,0:T(8,128)(2,1)S(1)} %get-tuple-element.11), channel_id=1, source_target_pairs={{0,16},{16,0},{32,48},{48,32},{64,80},{80,64},{96,112},{112,96},{1... | collective-permute-start | bytes 116744 | tf_op jit(solution)/shard_map/ppermute | solution.py:287
  11.7 3.6 %collective-permute-start.1 = (bf16[152,128]{1,0:T(8,128)(2,1)S(1)}, bf16[152,128]{1,0:T(8,128)(2,1)S(1)}, u32[]{:S(2)}, u32[]{:S(2)}) collective-permute-start(bf16[152,128]{1,0:T(8,128)(2,1)S(1)} %get-tuple-element.12), channel_id=1, source_target_pairs={{0,1},{1,0},{2,3},{3,2},{4,5},{5,4},{6,7},{7,6},{8,9},{9,8},{10,11... | collective-permute-start | bytes 116744 | tf_op jit(solution)/shard_map/ppermute | solution.py:286
  12.7 2.6 %collective-permute-start.2 = (bf16[152,128]{1,0:T(8,128)(2,1)S(1)}, bf16[152,128]{1,0:T(8,128)(2,1)S(1)}, u32[]{:S(2)}, u32[]{:S(2)}) collective-permute-start(bf16[152,128]{1,0:T(8,128)(2,1)S(1)} %get-tuple-element.13), channel_id=1, source_target_pairs={{0,1},{1,0},{2,3},{3,2},{4,5},{5,4},{6,7},{7,6},{8,9},{9,8},{10,11... | collective-permute-start | bytes 116744 | tf_op jit(solution)/shard_map/ppermute | solution.py:289
  12.7 3.4 %collective-permute-start.3 = (bf16[152,128]{1,0:T(8,128)(2,1)S(1)}, bf16[152,128]{1,0:T(8,128)(2,1)S(1)}, u32[]{:S(2)}, u32[]{:S(2)}) collective-permute-start(bf16[152,128]{1,0:T(8,128)(2,1)S(1)} %get-tuple-element.14), channel_id=1, source_target_pairs={{0,15},{1,2},{2,1},{3,4},{4,3},{5,6},{6,5},{7,8},{8,7},{9,10},{10,... | collective-permute-start | bytes 116744 | tf_op jit(solution)/shard_map/ppermute | solution.py:288
  13.8 2.3 %copy-start.2 = (s32[1,1,128]{2,1,0:T(1,128)S(1)}, s32[1,1,128]{2,1,0:T(1,128)}, u32[]{:S(2)}) copy-start(s32[1,1,128]{2,1,0:T(1,128)} %param.11) | copy-start | bytes 1540
  13.8 8.9 %copy-start.1 = (f32[137]{0:T(256)S(1)}, f32[137]{0:T(256)}, u32[]{:S(2)}) copy-start(f32[137]{0:T(256)} %param.9) | copy-start | bytes 1648
  16.4 8.1 %collective-permute-start.5 = (bf16[152,128]{1,0:T(8,128)(2,1)S(1)}, bf16[152,128]{1,0:T(8,128)(2,1)S(1)}, u32[]{:S(2)}, u32[]{:S(2)}) collective-permute-start(bf16[152,128]{1,0:T(8,128)(2,1)S(1)} %pack.1.p0), channel_id=1, source_target_pairs={{0,64},{16,80},{32,96},{48,112},{64,0},{80,16},{96,32},{112,48},{1... | collective-permute-start | bytes 116744 | tf_op jit(solution)/shard_map/ppermute | solution.py:309
  20.3 6.2 %collective-permute-start.4 = (bf16[152,128]{1,0:T(8,128)(2,1)S(1)}, bf16[152,128]{1,0:T(8,128)(2,1)S(1)}, u32[]{:S(2)}, u32[]{:S(2)}) collective-permute-start(bf16[152,128]{1,0:T(8,128)(2,1)S(1)} %pack.1.p0), channel_id=1, source_target_pairs={{0,1},{1,0},{2,3},{3,2},{4,5},{5,4},{6,7},{7,6},{8,9},{9,8},{10,11... | collective-permute-start | bytes 116744 | tf_op jit(solution)/shard_map/ppermute | solution.py:310
  24.5 2.0 %collective-permute-start.6 = (bf16[152,128]{1,0:T(8,128)(2,1)S(1)}, bf16[152,128]{1,0:T(8,128)(2,1)S(1)}, u32[]{:S(2)}, u32[]{:S(2)}) collective-permute-start(bf16[152,128]{1,0:T(8,128)(2,1)S(1)} %collective-permute-done.5.p2), channel_id=1, source_target_pairs={{0,1},{1,0},{2,3},{3,2},{4,5},{5,4},{6,7},{7,6},{8,9},{9,8},{10,11... | collective-permute-start | bytes 116744 | tf_op jit(solution)/shard_map/ppermute | solution.py:311

commit v3 on v2

--- a/solution.py
+++ b/solution.py
@@ -10,6 +10,7 @@
 F32 = jnp.float32
 BF16 = jnp.bfloat16
 LEV = 137
+KA = 144
 KP = 152
 N = 128
 CHUNKS = ((0, 8), (8, 16), (24, 24), (48, 24), (72, 24), (96, 24), (120, 8), (128, 9))
@@ -48,7 +49,7 @@
     return north, south, west, east
 
 
-def transport_kernel(h_hbm, u_hbm, v_hbm, t_ref, s0_ref, s1_ref, c0_ref, c1_ref, hb, ub, vb, cols, sems):
+def transport_kernel(h_hbm, u_hbm, v_hbm, t_ref, s0_ref, s1_ref, c0_ref, c1_ref, hb, ub, vb, cols, near, picks, sems):
     copies = []
     for c, (a, n) in enumerate(CHUNKS):
         row = []
@@ -58,13 +59,20 @@
             row.append(copy)
         copies.append(row)
     zeros = jnp.zeros((N, N), F32)
-    for k in range(LEV, KP):
+    for k in range(LEV, KA):
         t_ref[pl.ds(KP + k, N, stride=KP), :] = zeros
-    blank = jnp.zeros((KP, N), F32)
-    t_ref[pl.ds(0, KP), :] = blank
-    t_ref[pl.ds((N + 1) * KP, KP), :] = blank
+    blank = jnp.zeros((KA, N), F32)
+    t_ref[pl.ds(0, KA), :] = blank
+    t_ref[pl.ds((N + 1) * KP, KA), :] = blank
     cols[...] = jnp.zeros((3, N, N), BF16)
     lane = iota((N, N), 1)
+    i_even = lax.rem(lax.axis_index("lat"), 2) == 0
+    j_even = lax.rem(lax.axis_index("lon"), 2) == 0
+    k, at = iota((KA, 3 * N), 0), iota((KA, 3 * N), 1)
+    left_at = 2 * k
+    right_at = jnp.where(lax.rem(k, 64) == 0, 2 * k + N - 1, 2 * k - 1)
+    picks[0] = jnp.where(at == jnp.where(j_even, right_at, left_at), 1.0, 0.0).astype(BF16)
+    picks[1] = jnp.where(at == jnp.where(j_even, left_at, right_at), 1.0, 0.0).astype(BF16)
 
     def level(k):
         parts = []
@@ -82,59 +90,60 @@
         for q in range(1, size):
             moved = pltpu.roll(level(k + q), 2 * q, 1)
             ends = jnp.where((lane == 2 * q) | (lane == 2 * q - 1), moved, ends)
+        near[...] = ends
+
+    def merge(k, size):
         shift = 2 * lax.rem(k, 64)
         mine = lax.rem(lane - shift + N + 1, N) < 2 * size
         block = lax.div(k, 64)
-        cols[block] = jnp.where(mine, pltpu.roll(ends, shift, 1), cols[block])
+        cols[block] = jnp.where(mine, pltpu.roll(near[...], shift, 1), cols[block])
 
     for (a, n), row in zip(CHUNKS, copies):
         for copy in row:
             copy.wait()
 
         def groups(g, _, a=a):
+            merge(a + 8 * g - 8, 8)
             group(a + 8 * g, 8)
             return 0
 
-        lax.fori_loop(0, n // 8, groups, 0)
+        if a == 0:
+            group(0, 8)
+        lax.fori_loop(1 if a == 0 else 0, n // 8, groups, 0)
         if n % 8:
-            group(a + n - n % 8, n % 8)
-    i_even = lax.rem(lax.axis_index("lat"), 2) == 0
-    j_even = lax.rem(lax.axis_index("lon"), 2) == 0
+            end = a + n - n % 8
+            merge(end - 8, 8)
+            group(end, n % 8)
+            merge(end, n % 8)
 
     def row_at(top):
         start = pl.multiple_of(jnp.where(top, KP, N * KP), 8)
-        return t_ref[pl.ds(start, KP), :].astype(BF16)
-
-    k, at = iota((KP, 3 * N), 0), iota((KP, 3 * N), 1)
-    left_at = 2 * k
-    right_at = jnp.where(lax.rem(k, 64) == 0, 2 * k + N - 1, 2 * k - 1)
+        return t_ref[pl.ds(start, KA), :].astype(BF16)
+
     packed = jnp.concatenate([cols[0], cols[1], cols[2]], axis=1)
-
-    def col_at(left):
-        pick = jnp.where(at == jnp.where(left, left_at, right_at), 1.0, 0.0).astype(BF16)
-        return dot(pick, packed, NT).astype(BF16)
-
     s0_ref[...] = row_at(jnp.logical_not(i_even))
     s1_ref[...] = row_at(i_even)
-    c0_ref[...] = col_at(jnp.logical_not(j_even))
-    c1_ref[...] = col_at(j_even)
-
-
-def sums_kernel(t_ref, lab_ref, t0_ref, west_ref, east_ref):
+    c0_ref[...] = dot(picks[0], packed, NT).astype(BF16)
+    c1_ref[...] = dot(picks[1], packed, NT).astype(BF16)
+
+
+def sums_kernel(t_ref, lab_ref, gl_ref, w_ref, t0_ref, root_ref, own_ref, west_ref, east_ref):
+    root_ref[...] = jnp.sqrt(column(w_ref[...], KA)) * 0.125 + jnp.zeros((KA, N), F32)
+    own_ref[...] = column(gl_ref[...].astype(F32), N) + jnp.zeros((N, N), F32)
     lab = lab_ref[...]
     lane = iota((N, N), 1)
     west_ref[...] = jnp.where(lane == 0, -1, pltpu.roll(lab, 1, 1))
     east_ref[...] = jnp.where(lane == N - 1, -1, pltpu.roll(lab, N - 1, 1))
     ids = iota((N, N), 0).astype(F32).astype(BF16)
-    t0_ref[...] = jnp.zeros((KP, N), F32)
+    t0_ref[...] = jnp.zeros((KA, N), F32)
     last = iota((8, N), 0) + (LEV - LEV % 8)
 
     def patch_row(q):
         base = pl.multiple_of((1 + 4 * q) * KP, 8)
-        x = [t_ref[pl.ds(base + m * KP, KP), :] for m in range(-1, 5)]
+        x = [t_ref[pl.ds(base + m * KP, KA), :] for m in range(-1, 5)]
         whole = x[1] + x[2] + x[3] + x[4]
         step = (x[0] - x[4]) + (x[5] - x[1])
-        step = jnp.concatenate([step[: LEV - LEV % 8], jnp.where(last == LEV, 32.0, step[LEV - LEV % 8 : KP - 8]), step[KP - 8 :]], axis=0)
+        step = jnp.concatenate([step[: LEV - LEV % 8], jnp.where(last == LEV, 32.0, step[LEV - LEV % 8 :])], axis=0)
         left = jnp.concatenate([whole.astype(BF16), step.astype(BF16)], axis=1)
 
         def marks(ref):
@@ -172,20 +181,19 @@
     count_hi = jnp.floor(count * 0.125)
     gl = gl_ref[...].astype(F32)
     gl_hi = jnp.floor(gl * (1.0 / 64.0))
-    row = iota((KP, N), 0)
+    row = iota((KA, N), 0)
     for m, extra in enumerate((count_hi, count - 8.0 * count_hi, gl_hi, gl - 64.0 * gl_hi)):
         total = jnp.where(row == LEV + m, extra, total)
     pay_ref[...] = total.astype(BF16)
 
 
-def smooth_kernel(half, t_ref, r0, r1, rc, ro, w_ref, s_ref, root_ref):
+def smooth_kernel(half, t_ref, r0, r1, rc, ro, root_ref, s_ref, square_ref):
     north, south, west, east = halos(r0, r1, rc, ro)
-    low = iota((KP, N), 1) < 64
+    low = iota((KA, N), 1) < 64
     if half == 0:
-        side = jnp.where(low, west, pltpu.roll(east, 64, 1)).astype(BF16)
+        outside, side = north, jnp.where(low, west, pltpu.roll(east, 64, 1)).astype(BF16)
     else:
-        side = jnp.where(low, pltpu.roll(west, 64, 1), east).astype(BF16)
-    root_ref[...] = jnp.sqrt(column(w_ref[...], KP)) * 0.125 + jnp.zeros((KP, N), F32)
+        outside, side = south, jnp.where(low, pltpu.roll(west, 64, 1), east).astype(BF16)
     a, c = iota((2 * N, N), 0), iota((2 * N, N), 1)
     band = jnp.where(a == c, 4.0, jnp.where(jnp.abs(a - c) == 1, 1.0, 0.0))
     edge = jnp.where(c == jnp.where(a < N + 64, 0, N - 1), 1.0, 0.0)
@@ -193,7 +201,10 @@
     lane = lax.rem(iota((1, N), 1), 64)
 
     def at(r):
-        return pl.ds(pl.multiple_of(r * KP, 8), KP)
+        return pl.ds(pl.multiple_of(r * KP, 8), KA)
+
+    def to(r):
+        return pl.ds(pl.multiple_of(r * KA, 8), KA)
 
     def rows(i, _):
         top = 64 * half + 32 * i
@@ -204,18 +215,18 @@
         across = dot(jnp.concatenate(lefts, axis=0), right, NN)
         for m in range(32):
             along = t_ref[at(top + m), :] + t_ref[at(top + m + 2), :]
-            s_ref[at(32 * i + m), :] = (across[m * KP : (m + 1) * KP] + along) * root_ref[...]
+            if m == (0 if half == 0 else 31):
+                along = along + jnp.where(i == half, outside, 0.0)
+            s = (across[m * KA : (m + 1) * KA] + along) * root_ref[...]
+            s_ref[to(32 * i + m), :] = s
+            square_ref[pl.ds(32 * i + m, 1), :] = jnp.sum(s * s, axis=0, keepdims=True)
         return 0
 
     lax.fori_loop(0, 2, rows, 0)
-    if half == 0:
-        s_ref[at(0), :] += north * root_ref[...]
-    else:
-        s_ref[at(63), :] += south * root_ref[...]
-
-
-def final_kernel(p0, p1, p2, p3, s0_ref, s1_ref, lab_ref, gl_ref, w_ref, out_ref, e_ref):
-    own = column(gl_ref[...].astype(F32), N) + jnp.zeros((N, N), F32)
+
+
+def final_kernel(p0, p1, p2, p3, s0_ref, s1_ref, square0, square1, lab_ref, own_ref, root_ref, out_ref, e_ref):
+    own = own_ref[...]
     lefts, rights = [], []
     for p in (p0, p1, p2, p3):
         pay = p[...]
@@ -224,32 +235,34 @@
         rights.append(jnp.where(own == gl, 1.0, 0.0).astype(BF16))
     total = dot(jnp.concatenate(lefts, axis=1), jnp.concatenate(rights, axis=1), NT)
     count = 256.0 * total[LEV : LEV + 1] + 32.0 * total[LEV + 1 : LEV + 2]
-    root = jnp.sqrt(column(w_ref[...], KP))
-    profile = root * (total / jnp.maximum(count, 1.0))
+    profile = root_ref[...] * (total * (8.0 / jnp.maximum(count, 1.0)))
+    hi = profile.astype(BF16).astype(F32)
+    lo = (profile - hi).astype(BF16).astype(F32)
+    profile = hi + lo
     energy = jnp.sum(profile * profile, axis=0, keepdims=True)
-    table = jnp.where(iota((KP, N), 0) == LEV, energy, profile)
-    hi = table.astype(BF16)
-    left = jnp.concatenate([hi, (table - hi.astype(F32)).astype(BF16)], axis=1)
+    energy_hi = energy.astype(BF16).astype(F32)
+    row = iota((KA, N), 0)
+    hi = jnp.where(row == LEV, energy_hi, hi).astype(BF16)
+    lo = jnp.where(row == LEV, energy - energy_hi, lo).astype(BF16)
+    left = jnp.concatenate([hi, lo], axis=1)
     ids = iota((N, N), 0).astype(F32).astype(BF16)
-    base = LEV - LEV % 8
-    inside = iota((8, N), 0) + base < LEV
 
     def patch_row(q, s_ref, top):
         row = lab_ref[pl.ds(4 * q, 1), :].astype(F32).astype(BF16)
         mark = jnp.where(row == ids, BF16(1.0), BF16(0.0))
         placed = dot(left, jnp.concatenate([mark, mark], axis=0), NN)
-        e = placed[LEV : LEV + 1]
-        placed = jnp.concatenate([placed[:base], jnp.where(inside, placed[base : base + 8], 0.0)], axis=0)
+        e_ref[pl.ds(4 * q, 4), :] = placed[LEV : LEV + 1] + jnp.zeros((4, N), F32)
         for m in range(4):
             r = 4 * q + m
-            d = s_ref[pl.ds((r - top) * KP, base + 8), :] - placed
-            out_ref[pl.ds(r, 1), :] = jnp.sum(d * d, axis=0, keepdims=True)
-            e_ref[pl.ds(r, 1), :] = e
+            cross = s_ref[pl.ds((r - top) * KA, KA), :] * placed
+            out_ref[pl.ds(r, 1), :] = jnp.sum(cross, axis=0, keepdims=True)
 
     for half, s_ref in enumerate((s0_ref, s1_ref)):
         for q in range(16 * half, 16 * half + 16):
             patch_row(q, s_ref, 64 * half)
-    out_ref[...] = jnp.sqrt(out_ref[...] / e_ref[...])
+    e = e_ref[...]
+    square = jnp.concatenate([square0[...], square1[...]], axis=0)
+    out_ref[...] = jnp.sqrt(jnp.maximum(square - 2.0 * out_ref[...] + e, 0.0) / e)
 
 
 def outer(i, j):
@@ -269,7 +282,7 @@
 def shards(humidity, wind_u, wind_v, weights, labels, global_labels):
     vmem = pl.BlockSpec(memory_space=pltpu.VMEM)
     anywhere = pl.BlockSpec(memory_space=pl.ANY)
-    edge = pltpu.VMEM((KP, N), BF16)
+    edge = pltpu.VMEM((KA, N), BF16)
     gl = global_labels.reshape(1, N)
     w = weights.reshape(1, LEV)
     t, s0, s1, c0, c1 = pl.pallas_call(
@@ -278,7 +291,8 @@
         in_specs=[anywhere] * 3,
         out_specs=[vmem] * 5,
         scratch_shapes=[pltpu.VMEM((LEV, N, N), BF16)] * 3
-        + [pltpu.VMEM((3, N, N), BF16), pltpu.SemaphoreType.DMA((len(CHUNKS), 3))],
+        + [pltpu.VMEM((3, N, N), BF16), pltpu.VMEM((N, N), BF16), pltpu.VMEM((2, KA, 3 * N), BF16)]
+        + [pltpu.SemaphoreType.DMA((len(CHUNKS), 3))],
         compiler_params=params(18),
         cost_estimate=cost(30_000_000, 23_000_000),
         name="transport",
@@ -287,16 +301,16 @@
     r0 = lax.ppermute(s0, "lat", [(i, i ^ 1) for i in range(8)])
     ro = lax.ppermute(c1, "lon", [(j, (j + 1) % 16 if j % 2 else (j - 1) % 16) for j in range(16)])
     rc = lax.ppermute(c0, "lon", [(j, j ^ 1) for j in range(16)])
-    t0 = pl.pallas_call(
+    t0, root, own = pl.pallas_call(
         sums_kernel,
-        out_shape=pltpu.VMEM((KP, N), F32),
-        in_specs=[vmem] * 2,
-        out_specs=vmem,
+        out_shape=(pltpu.VMEM((KA, N), F32), pltpu.VMEM((KA, N), F32), pltpu.VMEM((N, N), F32)),
+        in_specs=[vmem] * 4,
+        out_specs=[vmem] * 3,
         scratch_shapes=[pltpu.VMEM((N, N), jnp.int32)] * 2,
         compiler_params=params(8),
         cost_estimate=cost(600_000_000, 9_500_000),
         name="sums",
-    )(t, labels)
+    )(t, labels, gl, w)
     pay = pl.pallas_call(
         pack_kernel,
         out_shape=edge,
@@ -309,29 +323,28 @@
     p2 = lax.ppermute(pay, "lat", [(i, (i + 4) % 8) for i in range(8)])
     p1 = lax.ppermute(pay, "lon", [(j, j ^ 1) for j in range(16)])
     p3 = lax.ppermute(p2, "lon", [(j, j ^ 1) for j in range(16)])
-    s0, s1 = (
+    (s0, square0), (s1, square1) = (
         pl.pallas_call(
             functools.partial(smooth_kernel, half),
-            out_shape=pltpu.VMEM((N // 2 * KP, N), F32),
+            out_shape=(pltpu.VMEM((N // 2 * KA, N), F32), pltpu.VMEM((N // 2, N), F32)),
             in_specs=[vmem] * 6,
-            out_specs=vmem,
-            scratch_shapes=[pltpu.VMEM((KP, N), F32)],
+            out_specs=[vmem] * 2,
             compiler_params=params(12),
             cost_estimate=cost(600_000_000, 9_500_000),
             name="smooth",
-        )(t, r0, r1, rc, ro, w)
+        )(t, r0, r1, rc, ro, root)
         for half in range(2)
     )
     return pl.pallas_call(
         final_kernel,
         out_shape=jax.ShapeDtypeStruct((N, N), F32),
-        in_specs=[vmem] * 9,
+        in_specs=[vmem] * 11,
         out_specs=vmem,
         scratch_shapes=[pltpu.VMEM((N, N), F32)],
         compiler_params=params(8),
         cost_estimate=cost(300_000_000, 9_500_000),
         name="final",
-    )(pay, p1, p2, p3, s0, s1, labels, gl, w)
+    )(pay, p1, p2, p3, s0, s1, square0, square1, labels, own, root)
 
 
 def solution(mesh):

time: 29.2 us -> 27.7 us (0.949)
  Pallas kernels: 15.3 us -> 13.6 us
    pallas_call x1, Pallas kernels: 7.2 us -> 6.27 us  [shards(): pl.pallas_call(transport_kernel, out_shape=(pltpu.VMEM(((N + 2) * KP, N),...]
    pallas_call x1, Pallas kernels: 2.63 us -> 2.22 us  [shards(): pl.pallas_call(final_kernel, out_shape=jax.ShapeDtypeStruct((N, N), F32),...]
where the time goes in v3:
time: 27.7 us; the launch traced here: 27.6 us
  Pallas kernels  13.6 us (49%)
  starting transfers between devices  13.1 us (47%)
  waiting for transfers between devices  0.77 us (3%)
    pallas_call x1, Pallas kernels, shards(): pl.pallas_call(transport_kernel, out_shape=(pltpu.VMEM(((N + 2) * KP, N),...  6.27 us
    ppermute x1, starting transfers between devices, shards(): r0 = lax.ppermute(s0, 'lat', [(i, i ^ 1) for i in range(8)])  4.5 us
    ppermute x1, starting transfers between devices, shards(): p2 = lax.ppermute(pay, 'lat', [(i, (i + 4) % 8) for i in range(8)])  3.86 us
    pallas_call x2, Pallas kernels, shards(): pl.pallas_call(functools.partial(smooth_kernel, half), out_shape=(pltpu.V...  3.34 us
    ppermute x1, starting transfers between devices, shards(): p1 = lax.ppermute(pay, 'lon', [(j, j ^ 1) for j in range(16)])  2.38 us
    pallas_call x1, Pallas kernels, shards(): pl.pallas_call(final_kernel, out_shape=jax.ShapeDtypeStruct((N, N), F32),...  2.22 us
    pallas_call x1, Pallas kernels, shards(): pl.pallas_call(sums_kernel, out_shape=(pltpu.VMEM((KA, N), F32), pltpu.VM...  1.46 us
    ppermute x1, starting transfers between devices, shards(): lax.ppermute(c1, 'lon', [(j, (j + 1) % 16 if j % 2 else (j - 1) % 16) for...  1.13 us
  transfers between devices with their start and end apart: 7, of which 1 were waited for; matrix products, arithmetic and copies ran while one was open for 0% of the time, Pallas kernels for 17%

profile of v3, /device:TPU:1, one launch (start us, length us, event | category | flops | bytes accessed | tf_op | source)
XLA Modules:
  0.0 27.6 jit_solution(751330492840389800)
XLA Ops:
  0.0 0.0 copy-start.1
  0.0 0.0 copy-start.2
  0.0 0.0 copy-start
  0.0 6.3 %transport.1 = (f32[19760,128]{1,0:T(8,128)S(1)}, bf16[144,128]{1,0:T(8,128)(2,1)S(1)}, bf16[144,128]{1,0:T(8,128)(2,1)S(1)}, bf16[144,128]{1,0:T(8,128)(2,1)S(1)}, bf16[144,128]{1,0:T(8,128)(2,1)S(1)}) custom-call(bf16[137,128,128]{2,1,0:T(8,128)(2,1)} %h_hbm.1, bf16[137,128,128]{2,1,0:T(8,128)(2,1)} %u_hbm.1, bf16[137,128,128]{2,1,0:T(8,128)(2,1)} %v_hbm.1), custom_call_target="tpu_custom_call" | custom-call | flops 30000000 | bytes 23000000 | tf_op jit(solution)/shard_map/transport/pallas_call | solution.py:288
  6.3 4.5 %collective-permute-start = (bf16[144,128]{1,0:T(8,128)(2,1)S(1)}, bf16[144,128]{1,0:T(8,128)(2,1)S(1)}, u32[]{:S(2)}, u32[]{:S(2)}) collective-permute-start(bf16[144,128]{1,0:T(8,128)(2,1)S(1)} %get-tuple-element.19), channel_id=1, source_target_pairs={{0,16},{16,0},{32,48},{48,32},{64,80},{80,64},{96,112},{112,96},{1... | collective-permute-start | bytes 110600 | tf_op jit(solution)/shard_map/ppermute | solution.py:301
  10.8 1.0 %collective-permute-start.1 = (bf16[144,128]{1,0:T(8,128)(2,1)S(1)}, bf16[144,128]{1,0:T(8,128)(2,1)S(1)}, u32[]{:S(2)}, u32[]{:S(2)}) collective-permute-start(bf16[144,128]{1,0:T(8,128)(2,1)S(1)} %get-tuple-element.20), channel_id=1, source_target_pairs={{0,1},{1,0},{2,3},{3,2},{4,5},{5,4},{6,7},{7,6},{8,9},{9,8},{10,11... | collective-permute-start | bytes 110600 | tf_op jit(solution)/shard_map/ppermute | solution.py:300
  11.7 0.0 collective-permute-start.2
  11.8 1.1 %collective-permute-start.3 = (bf16[144,128]{1,0:T(8,128)(2,1)S(1)}, bf16[144,128]{1,0:T(8,128)(2,1)S(1)}, u32[]{:S(2)}, u32[]{:S(2)}) collective-permute-start(bf16[144,128]{1,0:T(8,128)(2,1)S(1)} %get-tuple-element.22), channel_id=1, source_target_pairs={{0,15},{1,2},{2,1},{3,4},{4,3},{5,6},{6,5},{7,8},{8,7},{9,10},{10,... | collective-permute-start | bytes 110600 | tf_op jit(solution)/shard_map/ppermute | solution.py:302
  12.9 0.0 copy-done.1
  12.9 0.0 copy-done.2
  12.9 0.0 copy-done
  12.9 1.5 %sums.1 = (f32[144,128]{1,0:T(8,128)S(1)}, f32[144,128]{1,0:T(8,128)S(1)}, f32[128,128]{1,0:T(8,128)S(1)}) custom-call(f32[19760,128]{1,0:T(8,128)S(1)} %get-tuple-element.17.t_ref, s32[128,128]{1,0:T(8,128)S(1)} %copy-done, s32[1,128]{1,0:T(1,128)S(1)} %bitcast.2, f32[1,137]{1,0:T(1,128)S(1)} %bitcast.4), custom_call_target="tpu_custom_call" | custom-call | flops 600000000 | bytes 9500000 | tf_op jit(solution)/shard_map/sums/pallas_call | solution.py:304
  14.4 0.0 collective-permute-done.r0
  14.4 0.0 collective-permute-done.1.r1
  14.4 0.0 collective-permute-done.2.rc
  14.4 0.8 %collective-permute-done.3.ro = bf16[144,128]{1,0:T(8,128)(2,1)S(1)} collective-permute-done((bf16[144,128]{1,0:T(8,128)(2,1)S(1)}, bf16[144,128]{1,0:T(8,128)(2,1)S(1)}, u32[]{:S(2)}, u32[]{:S(2)}) %collective-permute-start.3) | collective-permute-done | bytes 36896 | tf_op jit(solution)/shard_map/ppermute | solution.py:302
  15.1 0.3 %pack.1.p0 = bf16[144,128]{1,0:T(8,128)(2,1)S(1)} custom-call(f32[144,128]{1,0:T(8,128)S(1)} %get-tuple-element.18.t0_ref, bf16[144,128]{1,0:T(8,128)(2,1)S(1)} %collective-permute-done.r0, bf16[144,128]{1,0:T(8,128)(2,1)S(1)} %collective-permute-done.1.r1, bf16[144,128]{1,0:T(8,128)(2,1)S(1)} %collective-permute-done.2.rc, ...), custom_call_target="tpu_custom_call" | custom-call | flops 20000000 | bytes 300000 | tf_op jit(solution)/shard_map/pack/pallas_call | solution.py:314
  15.5 3.9 %collective-permute-start.5 = (bf16[144,128]{1,0:T(8,128)(2,1)S(1)}, bf16[144,128]{1,0:T(8,128)(2,1)S(1)}, u32[]{:S(2)}, u32[]{:S(2)}) collective-permute-start(bf16[144,128]{1,0:T(8,128)(2,1)S(1)} %pack.1.p0), channel_id=1, source_target_pairs={{0,64},{16,80},{32,96},{48,112},{64,0},{80,16},{96,32},{112,48},{1... | collective-permute-start | bytes 110600 | tf_op jit(solution)/shard_map/ppermute | solution.py:323
  19.3 2.4 %collective-permute-start.4 = (bf16[144,128]{1,0:T(8,128)(2,1)S(1)}, bf16[144,128]{1,0:T(8,128)(2,1)S(1)}, u32[]{:S(2)}, u32[]{:S(2)}) collective-permute-start(bf16[144,128]{1,0:T(8,128)(2,1)S(1)} %pack.1.p0), channel_id=1, source_target_pairs={{0,1},{1,0},{2,3},{3,2},{4,5},{5,4},{6,7},{7,6},{8,9},{9,8},{10,11... | collective-permute-start | bytes 110600 | tf_op jit(solution)/shard_map/ppermute | solution.py:324
  21.7 1.7 %smooth.3 = (f32[9216,128]{1,0:T(8,128)S(1)}, f32[64,128]{1,0:T(8,128)S(1)}) custom-call(f32[19760,128]{1,0:T(8,128)S(1)} %get-tuple-element.17.t_ref, bf16[144,128]{1,0:T(8,128)(2,1)S(1)} %collective-permute-done.r0, bf16[144,128]{1,0:T(8,128)(2,1)S(1)} %collective-permute-done.1.r1, bf16[144,128]{1,0:T(8,128)(2,1)S(1)} %collective-permute-done.2.rc, ...), custom_call_target="tpu_custom_call" | custom-call | flops 600000000 | bytes 9500000 | tf_op jit(solution)/shard_map/smooth/pallas_call | solution.py:327
  23.4 0.0 collective-permute-done.5.p2
  23.4 0.3 collective-permute-start.6
  23.7 1.7 %smooth.2 = (f32[9216,128]{1,0:T(8,128)S(1)}, f32[64,128]{1,0:T(8,128)S(1)}) custom-call(f32[19760,128]{1,0:T(8,128)S(1)} %get-tuple-element.17.t_ref, bf16[144,128]{1,0:T(8,128)(2,1)S(1)} %collective-permute-done.r0, bf16[144,128]{1,0:T(8,128)(2,1)S(1)} %collective-permute-done.1.r1, bf16[144,128]{1,0:T(8,128)(2,1)S(1)} %collective-permute-done.2.rc, ...), custom_call_target="tpu_custom_call" | custom-call | flops 600000000 | bytes 9500000 | tf_op jit(solution)/shard_map/smooth/pallas_call | solution.py:327
  25.3 0.0 collective-permute-done.4.p1
  25.3 0.0 collective-permute-done.6.p3
  25.4 2.2 %final.1 = f32[128,128]{1,0:T(8,128)} custom-call(bf16[144,128]{1,0:T(8,128)(2,1)S(1)} %pack.1.p0, bf16[144,128]{1,0:T(8,128)(2,1)S(1)} %collective-permute-done.4.p1, bf16[144,128]{1,0:T(8,128)(2,1)S(1)} %collective-permute-done.5.p2, bf16[144,128]{1,0:T(8,128)(2,1)S(1)} %collective-permute-done.6.p3, f32[9216,128]{1,0:T(8,128)S(1)} %get-tuple-element.24.s0_ref, ...), custom_call_target="tpu_custom_call" | custom-call | flops 300000000 | bytes 9500000 | tf_op jit(solution)/shard_map/final/pallas_call | solution.py:338
Async XLA Ops:
  0.0 12.9 %copy-start.1 = (s32[1,1,128]{2,1,0:T(1,128)S(1)}, s32[1,1,128]{2,1,0:T(1,128)}, u32[]{:S(2)}) copy-start(s32[1,1,128]{2,1,0:T(1,128)} %param.11) | copy-start | bytes 1540
  0.0 12.9 %copy-start.2 = (f32[137]{0:T(256)S(1)}, f32[137]{0:T(256)}, u32[]{:S(2)}) copy-start(f32[137]{0:T(256)} %param.9) | copy-start | bytes 1648
  0.0 12.9 %copy-start = (s32[128,128]{1,0:T(8,128)S(1)}, s32[128,128]{1,0:T(8,128)}, u32[]{:S(2)}) copy-start(s32[128,128]{1,0:T(8,128)} %lab_ref.5) | copy-start | bytes 196612
  6.3 8.1 %collective-permute-start = (bf16[144,128]{1,0:T(8,128)(2,1)S(1)}, bf16[144,128]{1,0:T(8,128)(2,1)S(1)}, u32[]{:S(2)}, u32[]{:S(2)}) collective-permute-start(bf16[144,128]{1,0:T(8,128)(2,1)S(1)} %get-tuple-element.19), channel_id=1, source_target_pairs={{0,16},{16,0},{32,48},{48,32},{64,80},{80,64},{96,112},{112,96},{1... | collective-permute-start | bytes 110600 | tf_op jit(solution)/shard_map/ppermute | solution.py:301
  10.8 3.6 %collective-permute-start.1 = (bf16[144,128]{1,0:T(8,128)(2,1)S(1)}, bf16[144,128]{1,0:T(8,128)(2,1)S(1)}, u32[]{:S(2)}, u32[]{:S(2)}) collective-permute-start(bf16[144,128]{1,0:T(8,128)(2,1)S(1)} %get-tuple-element.20), channel_id=1, source_target_pairs={{0,1},{1,0},{2,3},{3,2},{4,5},{5,4},{6,7},{7,6},{8,9},{9,8},{10,11... | collective-permute-start | bytes 110600 | tf_op jit(solution)/shard_map/ppermute | solution.py:300
  11.7 2.6 %collective-permute-start.2 = (bf16[144,128]{1,0:T(8,128)(2,1)S(1)}, bf16[144,128]{1,0:T(8,128)(2,1)S(1)}, u32[]{:S(2)}, u32[]{:S(2)}) collective-permute-start(bf16[144,128]{1,0:T(8,128)(2,1)S(1)} %get-tuple-element.21), channel_id=1, source_target_pairs={{0,1},{1,0},{2,3},{3,2},{4,5},{5,4},{6,7},{7,6},{8,9},{9,8},{10,11... | collective-permute-start | bytes 110600 | tf_op jit(solution)/shard_map/ppermute | solution.py:303
  11.8 3.4 %collective-permute-start.3 = (bf16[144,128]{1,0:T(8,128)(2,1)S(1)}, bf16[144,128]{1,0:T(8,128)(2,1)S(1)}, u32[]{:S(2)}, u32[]{:S(2)}) collective-permute-start(bf16[144,128]{1,0:T(8,128)(2,1)S(1)} %get-tuple-element.22), channel_id=1, source_target_pairs={{0,15},{1,2},{2,1},{3,4},{4,3},{5,6},{6,5},{7,8},{8,7},{9,10},{10,... | collective-permute-start | bytes 110600 | tf_op jit(solution)/shard_map/ppermute | solution.py:302
  15.5 7.9 %collective-permute-start.5 = (bf16[144,128]{1,0:T(8,128)(2,1)S(1)}, bf16[144,128]{1,0:T(8,128)(2,1)S(1)}, u32[]{:S(2)}, u32[]{:S(2)}) collective-permute-start(bf16[144,128]{1,0:T(8,128)(2,1)S(1)} %pack.1.p0), channel_id=1, source_target_pairs={{0,64},{16,80},{32,96},{48,112},{64,0},{80,16},{96,32},{112,48},{1... | collective-permute-start | bytes 110600 | tf_op jit(solution)/shard_map/ppermute | solution.py:323
  19.3 6.0 %collective-permute-start.4 = (bf16[144,128]{1,0:T(8,128)(2,1)S(1)}, bf16[144,128]{1,0:T(8,128)(2,1)S(1)}, u32[]{:S(2)}, u32[]{:S(2)}) collective-permute-start(bf16[144,128]{1,0:T(8,128)(2,1)S(1)} %pack.1.p0), channel_id=1, source_target_pairs={{0,1},{1,0},{2,3},{3,2},{4,5},{5,4},{6,7},{7,6},{8,9},{9,8},{10,11... | collective-permute-start | bytes 110600 | tf_op jit(solution)/shard_map/ppermute | solution.py:324
  23.4 1.9 %collective-permute-start.6 = (bf16[144,128]{1,0:T(8,128)(2,1)S(1)}, bf16[144,128]{1,0:T(8,128)(2,1)S(1)}, u32[]{:S(2)}, u32[]{:S(2)}) collective-permute-start(bf16[144,128]{1,0:T(8,128)(2,1)S(1)} %collective-permute-done.5.p2), channel_id=1, source_target_pairs={{0,1},{1,0},{2,3},{3,2},{4,5},{5,4},{6,7},{7,6},{8,9},{9,8},{10,11... | collective-permute-start | bytes 110600 | tf_op jit(solution)/shard_map/ppermute | solution.py:325

commit v4 on v3

--- a/solution.py
+++ b/solution.py
@@ -1,5 +1,3 @@
-import functools
-
 import jax
 import jax.numpy as jnp
 from jax import lax
@@ -11,6 +9,7 @@
 BF16 = jnp.bfloat16
 LEV = 137
 KA = 144
+TOP = 88
 KP = 152
 N = 128
 CHUNKS = ((0, 8), (8, 16), (24, 24), (48, 24), (72, 24), (96, 24), (120, 8), (128, 9))
@@ -38,12 +37,17 @@
     return jnp.where(first | last, 1.0, 0.0).astype(BF16)
 
 
+def north_first():
+    i, j = lax.axis_index("lat"), lax.axis_index("lon")
+    return (lax.rem(i, 2) == 0) == (lax.rem(j, 4) < 2)
+
+
 def halos(r0, r1, rc, ro):
     i, j = lax.axis_index("lat"), lax.axis_index("lon")
-    i_even, j_even = lax.rem(i, 2) == 0, lax.rem(j, 2) == 0
+    first, j_even = north_first(), lax.rem(j, 2) == 0
     r0, r1, rc, ro = (r[...].astype(F32) for r in (r0, r1, rc, ro))
-    north = jnp.where(i == 0, 0.0, jnp.where(i_even, r1, r0))
-    south = jnp.where(i == 7, 0.0, jnp.where(i_even, r0, r1))
+    north = jnp.where(i == 0, 0.0, jnp.where(first, r0, r1))
+    south = jnp.where(i == 7, 0.0, jnp.where(first, r1, r0))
     west = jnp.where(j_even, ro, rc)
     east = jnp.where(j_even, rc, ro)
     return north, south, west, east
@@ -66,8 +70,7 @@
     t_ref[pl.ds((N + 1) * KP, KA), :] = blank
     cols[...] = jnp.zeros((3, N, N), BF16)
     lane = iota((N, N), 1)
-    i_even = lax.rem(lax.axis_index("lat"), 2) == 0
-    j_even = lax.rem(lax.axis_index("lon"), 2) == 0
+    first, j_even = north_first(), lax.rem(lax.axis_index("lon"), 2) == 0
     k, at = iota((KA, 3 * N), 0), iota((KA, 3 * N), 1)
     left_at = 2 * k
     right_at = jnp.where(lax.rem(k, 64) == 0, 2 * k + N - 1, 2 * k - 1)
@@ -121,15 +124,19 @@
         return t_ref[pl.ds(start, KA), :].astype(BF16)
 
     packed = jnp.concatenate([cols[0], cols[1], cols[2]], axis=1)
-    s0_ref[...] = row_at(jnp.logical_not(i_even))
-    s1_ref[...] = row_at(i_even)
+    s0_ref[...] = row_at(first)
+    s1_ref[...] = row_at(jnp.logical_not(first))
     c0_ref[...] = dot(picks[0], packed, NT).astype(BF16)
     c1_ref[...] = dot(picks[1], packed, NT).astype(BF16)
 
 
-def sums_kernel(t_ref, lab_ref, gl_ref, w_ref, t0_ref, root_ref, own_ref, west_ref, east_ref):
+def sums_kernel(t_ref, lab_ref, gl_ref, w_ref, t0_ref, root_ref, own_ref, band_ref, west_ref, east_ref):
     root_ref[...] = jnp.sqrt(column(w_ref[...], KA)) * 0.125 + jnp.zeros((KA, N), F32)
     own_ref[...] = column(gl_ref[...].astype(F32), N) + jnp.zeros((N, N), F32)
+    a, c = iota((2 * N, N), 0), iota((2 * N, N), 1)
+    band = jnp.where(a == c, 4.0, jnp.where(jnp.abs(a - c) == 1, 1.0, 0.0))
+    edge = jnp.where(c == jnp.where(a < N + 64, 0, N - 1), 1.0, 0.0)
+    band_ref[...] = jnp.where(a < N, band, edge).astype(BF16)
     lab = lab_ref[...]
     lane = iota((N, N), 1)
     west_ref[...] = jnp.where(lane == 0, -1, pltpu.roll(lab, 1, 1))
@@ -163,7 +170,7 @@
     lax.fori_loop(0, N // 64, patch_rows, 0)
 
 
-def pack_kernel(t0_ref, r0, r1, rc, ro, lab_ref, gl_ref, pay_ref):
+def pack_kernel(t0_ref, r0, r1, ro, rc, lab_ref, gl_ref, pay_ref):
     north, south, west, east = halos(r0, r1, rc, ro)
     lab = lab_ref[...].astype(F32)
     ids = iota((N, N), 0).astype(F32)
@@ -187,39 +194,50 @@
     pay_ref[...] = total.astype(BF16)
 
 
-def smooth_kernel(half, t_ref, r0, r1, rc, ro, root_ref, s_ref, square_ref):
+def smooth_rows(t_ref, side, root_ref, band_ref, s_ref, square_ref, row, count, to, extra=None):
+    lane = lax.rem(iota((1, N), 1), 64)
+
+    def at(r):
+        return pl.ds(pl.multiple_of(r * KP, 8), KA)
+
+    lefts = []
+    for m in range(count):
+        mine = jnp.where(lane == lax.rem(row + m, 64), 1.0, 0.0).astype(BF16)
+        lefts.append(jnp.concatenate([t_ref[at(row + m + 1), :].astype(BF16), side * mine], axis=1))
+    across = dot(jnp.concatenate(lefts, axis=0), band_ref[...], NN)
+    for m in range(count):
+        along = t_ref[at(row + m), :] + t_ref[at(row + m + 2), :]
+        if extra is not None and m == extra[0]:
+            along = along + extra[1]
+        s = (across[m * KA : (m + 1) * KA] + along) * root_ref[...]
+        s_ref[pl.ds(pl.multiple_of((to + m) * KA, 8), KA), :] = s
+        square_ref[pl.ds(to + m, 1), :] = jnp.sum(s * s, axis=0, keepdims=True)
+
+
+def smooth_top_kernel(t_ref, r0, r1, rc, ro, root_ref, band_ref, s_ref, square_ref, side_ref, south_ref):
     north, south, west, east = halos(r0, r1, rc, ro)
     low = iota((KA, N), 1) < 64
-    if half == 0:
-        outside, side = north, jnp.where(low, west, pltpu.roll(east, 64, 1)).astype(BF16)
-    else:
-        outside, side = south, jnp.where(low, pltpu.roll(west, 64, 1), east).astype(BF16)
-    a, c = iota((2 * N, N), 0), iota((2 * N, N), 1)
-    band = jnp.where(a == c, 4.0, jnp.where(jnp.abs(a - c) == 1, 1.0, 0.0))
-    edge = jnp.where(c == jnp.where(a < N + 64, 0, N - 1), 1.0, 0.0)
-    right = jnp.where(a < N, band, edge).astype(BF16)
-    lane = lax.rem(iota((1, N), 1), 64)
-
-    def at(r):
-        return pl.ds(pl.multiple_of(r * KP, 8), KA)
-
-    def to(r):
-        return pl.ds(pl.multiple_of(r * KA, 8), KA)
+    side_ref[...] = jnp.where(low, pltpu.roll(west, 64, 1), east).astype(BF16)
+    south_ref[...] = south
+    side = jnp.where(low, west, pltpu.roll(east, 64, 1)).astype(BF16)
 
     def rows(i, _):
-        top = 64 * half + 32 * i
-        lefts = []
-        for m in range(32):
-            mine = jnp.where(lane == 32 * i + m, 1.0, 0.0).astype(BF16)
-            lefts.append(jnp.concatenate([t_ref[at(top + m + 1), :].astype(BF16), side * mine], axis=1))
-        across = dot(jnp.concatenate(lefts, axis=0), right, NN)
-        for m in range(32):
-            along = t_ref[at(top + m), :] + t_ref[at(top + m + 2), :]
-            if m == (0 if half == 0 else 31):
-                along = along + jnp.where(i == half, outside, 0.0)
-            s = (across[m * KA : (m + 1) * KA] + along) * root_ref[...]
-            s_ref[to(32 * i + m), :] = s
-            square_ref[pl.ds(32 * i + m, 1), :] = jnp.sum(s * s, axis=0, keepdims=True)
+        beyond = jnp.where(i == 0, north, 0.0)
+        smooth_rows(t_ref, side, root_ref, band_ref, s_ref, square_ref, 32 * i, 32, 32 * i, (0, beyond))
+        return 0
+
+    lax.fori_loop(0, 2, rows, 0)
+    if TOP > 64:
+        smooth_rows(t_ref, side_ref[...], root_ref, band_ref, s_ref, square_ref, 64, TOP - 64, 64)
+
+
+def smooth_bottom_kernel(t_ref, side_ref, south_ref, root_ref, band_ref, s_ref, square_ref):
+    count = (N - TOP) // 2
+
+    def rows(i, _):
+        beyond = jnp.where(i == 1, south_ref[...], 0.0)
+        row = TOP + count * i
+        smooth_rows(t_ref, side_ref[...], root_ref, band_ref, s_ref, square_ref, row, count, count * i, (count - 1, beyond))
         return 0
 
     lax.fori_loop(0, 2, rows, 0)
@@ -257,18 +275,26 @@
             cross = s_ref[pl.ds((r - top) * KA, KA), :] * placed
             out_ref[pl.ds(r, 1), :] = jnp.sum(cross, axis=0, keepdims=True)
 
-    for half, s_ref in enumerate((s0_ref, s1_ref)):
-        for q in range(16 * half, 16 * half + 16):
-            patch_row(q, s_ref, 64 * half)
+    for q in range(N // 4):
+        if 4 * q < TOP:
+            patch_row(q, s0_ref, 0)
+        else:
+            patch_row(q, s1_ref, TOP)
     e = e_ref[...]
     square = jnp.concatenate([square0[...], square1[...]], axis=0)
     out_ref[...] = jnp.sqrt(jnp.maximum(square - 2.0 * out_ref[...] + e, 0.0) / e)
 
 
-def outer(i, j):
-    if i in (0, 7):
-        return 16 * i + (j ^ 1)
-    return 16 * (i + 1 if i % 2 else i - 1) + j
+def vertical(turn):
+    pairs = []
+    for i in range(8):
+        for j in range(16):
+            if (j % 4 < 2) == (turn == 0):
+                other = 16 * i + (j ^ 1) if i in (0, 7) else 16 * (i + 1 if i % 2 else i - 1) + j
+            else:
+                other = 16 * (i ^ 1) + j
+            pairs.append((16 * i + j, other))
+    return pairs
 
 
 def params(mib):
@@ -283,6 +309,7 @@
     vmem = pl.BlockSpec(memory_space=pltpu.VMEM)
     anywhere = pl.BlockSpec(memory_space=pl.ANY)
     edge = pltpu.VMEM((KA, N), BF16)
+    wide = pltpu.VMEM((KA, N), F32)
     gl = global_labels.reshape(1, N)
     w = weights.reshape(1, LEV)
     t, s0, s1, c0, c1 = pl.pallas_call(
@@ -297,15 +324,15 @@
         cost_estimate=cost(30_000_000, 23_000_000),
         name="transport",
     )(*(pltpu.with_memory_space_constraint(x, pltpu.HBM) for x in (humidity, wind_u, wind_v)))
-    r1 = lax.ppermute(s1, ("lat", "lon"), [(16 * i + j, outer(i, j)) for i in range(8) for j in range(16)])
-    r0 = lax.ppermute(s0, "lat", [(i, i ^ 1) for i in range(8)])
+    r0 = lax.ppermute(s0, ("lat", "lon"), vertical(0))
+    r1 = lax.ppermute(s1, ("lat", "lon"), vertical(1))
     ro = lax.ppermute(c1, "lon", [(j, (j + 1) % 16 if j % 2 else (j - 1) % 16) for j in range(16)])
     rc = lax.ppermute(c0, "lon", [(j, j ^ 1) for j in range(16)])
-    t0, root, own = pl.pallas_call(
+    t0, root, own, band = pl.pallas_call(
         sums_kernel,
-        out_shape=(pltpu.VMEM((KA, N), F32), pltpu.VMEM((KA, N), F32), pltpu.VMEM((N, N), F32)),
+        out_shape=(wide, wide, pltpu.VMEM((N, N), F32), pltpu.VMEM((2 * N, N), BF16)),
         in_specs=[vmem] * 4,
-        out_specs=[vmem] * 3,
+        out_specs=[vmem] * 4,
         scratch_shapes=[pltpu.VMEM((N, N), jnp.int32)] * 2,
         compiler_params=params(8),
         cost_estimate=cost(600_000_000, 9_500_000),
@@ -319,22 +346,28 @@
         compiler_params=params(8),
         cost_estimate=cost(20_000_000, 300_000),
         name="pack",
-    )(t0, r0, r1, rc, ro, labels, gl)
+    )(t0, r0, r1, ro, rc, labels, gl)
     p2 = lax.ppermute(pay, "lat", [(i, (i + 4) % 8) for i in range(8)])
     p1 = lax.ppermute(pay, "lon", [(j, j ^ 1) for j in range(16)])
     p3 = lax.ppermute(p2, "lon", [(j, j ^ 1) for j in range(16)])
-    (s0, square0), (s1, square1) = (
-        pl.pallas_call(
-            functools.partial(smooth_kernel, half),
-            out_shape=(pltpu.VMEM((N // 2 * KA, N), F32), pltpu.VMEM((N // 2, N), F32)),
-            in_specs=[vmem] * 6,
-            out_specs=[vmem] * 2,
-            compiler_params=params(12),
-            cost_estimate=cost(600_000_000, 9_500_000),
-            name="smooth",
-        )(t, r0, r1, rc, ro, root)
-        for half in range(2)
-    )
+    top0, square0, side, south = pl.pallas_call(
+        smooth_top_kernel,
+        out_shape=(pltpu.VMEM((TOP * KA, N), F32), pltpu.VMEM((TOP, N), F32), edge, wide),
+        in_specs=[vmem] * 7,
+        out_specs=[vmem] * 4,
+        compiler_params=params(12),
+        cost_estimate=cost(600_000_000, 9_500_000),
+        name="smooth_top",
+    )(t, r0, r1, rc, ro, root, band)
+    bottom, square1 = pl.pallas_call(
+        smooth_bottom_kernel,
+        out_shape=(pltpu.VMEM(((N - TOP) * KA, N), F32), pltpu.VMEM((N - TOP, N), F32)),
+        in_specs=[vmem] * 5,
+        out_specs=[vmem] * 2,
+        compiler_params=params(12),
+        cost_estimate=cost(600_000_000, 9_500_000),
+        name="smooth_bottom",
+    )(t, side, south, root, band)
     return pl.pallas_call(
         final_kernel,
         out_shape=jax.ShapeDtypeStruct((N, N), F32),
@@ -344,7 +377,7 @@
         compiler_params=params(8),
         cost_estimate=cost(300_000_000, 9_500_000),
         name="final",
-    )(pay, p1, p2, p3, s0, s1, square0, square1, labels, own, root)
+    )(pay, p1, p2, p3, top0, bottom, square0, square1, labels, own, root)
 
 
 def solution(mesh):

time: 27.7 us -> 27.3 us (0.986)
  waiting for transfers between devices: 0.77 us -> 0.02 us
    ppermute x1, starting transfers between devices: 0.01 us -> 2.7 us  [shards(): rc = lax.ppermute(c0, 'lon', [(j, j ^ 1) for j in range(16)])]
    ppermute x1, starting transfers between devices: 3.86 us -> 2.19 us  [shards(): p2 = lax.ppermute(pay, 'lat', [(i, (i + 4) % 8) for i in range(8)])]
    ppermute x1, waiting for transfers between devices: 0.75 us -> 0.01 us  [shards(): lax.ppermute(c1, 'lon', [(j, (j + 1) % 16 if j % 2 else (j - 1) % 16) for...]
    ppermute x2, starting transfers between devices: 5.46 us -> 4.89 us  [the longest x1 3.4 us: shards(): r1 = lax.ppermute(s1, ('lat', 'lon'), vertical(1))]
    ppermute x1, starting transfers between devices: 2.38 us -> 2.09 us  [shards(): p1 = lax.ppermute(pay, 'lon', [(j, j ^ 1) for j in range(16)])]
  transfers between devices with their start and end apart: 7 -> 7, of which waited for: 1 -> 0; matrix products, arithmetic and copies ran while one was open for 0% -> 0% of each run, Pallas kernels for 17% -> 18%
where the time goes in v4:
time: 27.3 us; the launch traced here: 27.2 us
  Pallas kernels  13.8 us (51%)
  starting transfers between devices  13.3 us (49%)
    pallas_call x1, Pallas kernels, shards(): pl.pallas_call(transport_kernel, out_shape=(pltpu.VMEM(((N + 2) * KP, N),...  6.27 us
    ppermute x1, starting transfers between devices, shards(): r1 = lax.ppermute(s1, ('lat', 'lon'), vertical(1))  3.4 us
    ppermute x1, starting transfers between devices, shards(): rc = lax.ppermute(c0, 'lon', [(j, j ^ 1) for j in range(16)])  2.7 us
    pallas_call x1, Pallas kernels, shards(): pl.pallas_call(smooth_top_kernel, out_shape=(pltpu.VMEM((TOP * KA, N), F3...  2.34 us
    ppermute x1, starting transfers between devices, shards(): p2 = lax.ppermute(pay, 'lat', [(i, (i + 4) % 8) for i in range(8)])  2.19 us
    pallas_call x1, Pallas kernels, shards(): pl.pallas_call(final_kernel, out_shape=jax.ShapeDtypeStruct((N, N), F32),...  2.18 us
    ppermute x1, starting transfers between devices, shards(): p1 = lax.ppermute(pay, 'lon', [(j, j ^ 1) for j in range(16)])  2.09 us
    ppermute x1, starting transfers between devices, shards(): r0 = lax.ppermute(s0, ('lat', 'lon'), vertical(0))  1.49 us
  transfers between devices with their start and end apart: 7, of which 0 were waited for; matrix products, arithmetic and copies ran while one was open for 0% of the time, Pallas kernels for 18%

profile of v4, /device:TPU:1, one launch (start us, length us, event | category | flops | bytes accessed | tf_op | source)
XLA Modules:
  0.0 27.2 jit_solution(17132439470270433649)
XLA Ops:
  0.0 0.0 copy-start
  0.0 0.0 copy-start.1
  0.0 0.0 copy-start.2
  0.0 6.3 %transport.1 = (f32[19760,128]{1,0:T(8,128)S(1)}, bf16[144,128]{1,0:T(8,128)(2,1)S(1)}, bf16[144,128]{1,0:T(8,128)(2,1)S(1)}, bf16[144,128]{1,0:T(8,128)(2,1)S(1)}, bf16[144,128]{1,0:T(8,128)(2,1)S(1)}) custom-call(bf16[137,128,128]{2,1,0:T(8,128)(2,1)} %h_hbm.1, bf16[137,128,128]{2,1,0:T(8,128)(2,1)} %u_hbm.1, bf16[137,128,128]{2,1,0:T(8,128)(2,1)} %v_hbm.1), custom_call_target="tpu_custom_call" | custom-call | flops 30000000 | bytes 23000000 | tf_op jit(solution)/shard_map/transport/pallas_call | solution.py:315
  6.3 1.5 %collective-permute-start = (bf16[144,128]{1,0:T(8,128)(2,1)S(1)}, bf16[144,128]{1,0:T(8,128)(2,1)S(1)}, u32[]{:S(2)}, u32[]{:S(2)}) collective-permute-start(bf16[144,128]{1,0:T(8,128)(2,1)S(1)} %get-tuple-element.22), channel_id=1, source_target_pairs={{0,1},{1,0},{2,18},{3,19},{4,5},{5,4},{6,22},{7,23},{8,9},{9,8},{1... | collective-permute-start | bytes 110600 | tf_op jit(solution)/shard_map/ppermute | solution.py:327
  7.8 3.4 %collective-permute-start.1 = (bf16[144,128]{1,0:T(8,128)(2,1)S(1)}, bf16[144,128]{1,0:T(8,128)(2,1)S(1)}, u32[]{:S(2)}, u32[]{:S(2)}) collective-permute-start(bf16[144,128]{1,0:T(8,128)(2,1)S(1)} %get-tuple-element.23), channel_id=1, source_target_pairs={{0,16},{1,17},{2,3},{3,2},{4,20},{5,21},{6,7},{7,6},{8,24},{9,25},... | collective-permute-start | bytes 110600 | tf_op jit(solution)/shard_map/ppermute | solution.py:328
  11.2 1.2 %collective-permute-start.2 = (bf16[144,128]{1,0:T(8,128)(2,1)S(1)}, bf16[144,128]{1,0:T(8,128)(2,1)S(1)}, u32[]{:S(2)}, u32[]{:S(2)}) collective-permute-start(bf16[144,128]{1,0:T(8,128)(2,1)S(1)} %get-tuple-element.24), channel_id=1, source_target_pairs={{0,15},{1,2},{2,1},{3,4},{4,3},{5,6},{6,5},{7,8},{8,7},{9,10},{10,... | collective-permute-start | bytes 110600 | tf_op jit(solution)/shard_map/ppermute | solution.py:329
  12.4 2.7 %collective-permute-start.3 = (bf16[144,128]{1,0:T(8,128)(2,1)S(1)}, bf16[144,128]{1,0:T(8,128)(2,1)S(1)}, u32[]{:S(2)}, u32[]{:S(2)}) collective-permute-start(bf16[144,128]{1,0:T(8,128)(2,1)S(1)} %get-tuple-element.25), channel_id=1, source_target_pairs={{0,1},{1,0},{2,3},{3,2},{4,5},{5,4},{6,7},{7,6},{8,9},{9,8},{10,11... | collective-permute-start | bytes 110600 | tf_op jit(solution)/shard_map/ppermute | solution.py:330
  15.1 0.0 copy-done
  15.1 0.0 copy-done.1
  15.1 0.0 copy-done.2
  15.1 1.5 %sums.1 = (f32[144,128]{1,0:T(8,128)S(1)}, f32[144,128]{1,0:T(8,128)S(1)}, f32[128,128]{1,0:T(8,128)S(1)}, bf16[256,128]{1,0:T(8,128)(2,1)S(1)}) custom-call(f32[19760,128]{1,0:T(8,128)S(1)} %get-tuple-element.20.t_ref, s32[128,128]{1,0:T(8,128)S(1)} %copy-done, s32[1,128]{1,0:T(1,128)S(1)} %bitcast.2, f32[1,137]{1,0:T(1,128)S(1)} %bitcast.4), custom_call_target="tpu_custom_call" | custom-call | flops 600000000 | bytes 9500000 | tf_op jit(solution)/shard_map/sums/pallas_call | solution.py:331
  16.6 0.0 collective-permute-done.r0
  16.6 0.0 collective-permute-done.1.r1
  16.6 0.0 collective-permute-done.2.ro
  16.6 0.0 collective-permute-done.3.rc
  16.6 0.3 %pack.1.p0 = bf16[144,128]{1,0:T(8,128)(2,1)S(1)} custom-call(f32[144,128]{1,0:T(8,128)S(1)} %get-tuple-element.21.t0_ref, bf16[144,128]{1,0:T(8,128)(2,1)S(1)} %collective-permute-done.r0, bf16[144,128]{1,0:T(8,128)(2,1)S(1)} %collective-permute-done.1.r1, bf16[144,128]{1,0:T(8,128)(2,1)S(1)} %collective-permute-done.2.ro, ...), custom_call_target="tpu_custom_call" | custom-call | flops 20000000 | bytes 300000 | tf_op jit(solution)/shard_map/pack/pallas_call | solution.py:341
  16.9 2.2 %collective-permute-start.5 = (bf16[144,128]{1,0:T(8,128)(2,1)S(1)}, bf16[144,128]{1,0:T(8,128)(2,1)S(1)}, u32[]{:S(2)}, u32[]{:S(2)}) collective-permute-start(bf16[144,128]{1,0:T(8,128)(2,1)S(1)} %pack.1.p0), channel_id=1, source_target_pairs={{0,64},{16,80},{32,96},{48,112},{64,0},{80,16},{96,32},{112,48},{1... | collective-permute-start | bytes 110600 | tf_op jit(solution)/shard_map/ppermute | solution.py:350
  19.1 2.1 %collective-permute-start.4 = (bf16[144,128]{1,0:T(8,128)(2,1)S(1)}, bf16[144,128]{1,0:T(8,128)(2,1)S(1)}, u32[]{:S(2)}, u32[]{:S(2)}) collective-permute-start(bf16[144,128]{1,0:T(8,128)(2,1)S(1)} %pack.1.p0), channel_id=1, source_target_pairs={{0,1},{1,0},{2,3},{3,2},{4,5},{5,4},{6,7},{7,6},{8,9},{9,8},{10,11... | collective-permute-start | bytes 110600 | tf_op jit(solution)/shard_map/ppermute | solution.py:351
  21.2 2.3 %smooth_top.1 = (f32[12672,128]{1,0:T(8,128)S(1)}, f32[88,128]{1,0:T(8,128)S(1)}, bf16[144,128]{1,0:T(8,128)(2,1)S(1)}, f32[144,128]{1,0:T(8,128)S(1)}) custom-call(f32[19760,128]{1,0:T(8,128)S(1)} %get-tuple-element.20.t_ref, bf16[144,128]{1,0:T(8,128)(2,1)S(1)} %collective-permute-done.r0, bf16[144,128]{1,0:T(8,128)(2,1)S(1)} %collective-permute-done.1.r1, ...), custom_call_target="tpu_custom_call" | custom-call | flops 600000000 | bytes 9500000 | tf_op jit(solution)/shard_map/smooth_top/pallas_call | solution.py:353
  23.6 0.0 collective-permute-done.5.p2
  23.6 0.2 collective-permute-start.6
  23.8 1.2 %smooth_bottom.1 = (f32[5760,128]{1,0:T(8,128)S(1)}, f32[40,128]{1,0:T(8,128)S(1)}) custom-call(f32[19760,128]{1,0:T(8,128)S(1)} %get-tuple-element.20.t_ref, bf16[144,128]{1,0:T(8,128)(2,1)S(1)} %get-tuple-element.29.side_ref, f32[144,128]{1,0:T(8,128)S(1)} %get-tuple-element.30.south_ref, f32[144,128]{1,0:T(8,128)S(1)} %get-tuple-element.26.root_ref, ...), custom_call_target="tpu_custom_call" | custom-call | flops 600000000 | bytes 9500000 | tf_op jit(solution)/shard_map/smooth_bottom/pallas_call | solution.py:362
  25.0 0.0 collective-permute-done.4.p1
  25.0 0.0 collective-permute-done.6.p3
  25.0 2.2 %final.1 = f32[128,128]{1,0:T(8,128)} custom-call(bf16[144,128]{1,0:T(8,128)(2,1)S(1)} %pack.1.p0, bf16[144,128]{1,0:T(8,128)(2,1)S(1)} %collective-permute-done.4.p1, bf16[144,128]{1,0:T(8,128)(2,1)S(1)} %collective-permute-done.5.p2, bf16[144,128]{1,0:T(8,128)(2,1)S(1)} %collective-permute-done.6.p3, f32[12672,128]{1,0:T(8,128)S(1)} %get-tuple-element.28.s0_ref, ...), custom_call_target="tpu_custom_call" | custom-call | flops 300000000 | bytes 9500000 | tf_op jit(solution)/shard_map/final/pallas_call | solution.py:371
Async XLA Ops:
  0.0 15.1 %copy-start = (s32[128,128]{1,0:T(8,128)S(1)}, s32[128,128]{1,0:T(8,128)}, u32[]{:S(2)}) copy-start(s32[128,128]{1,0:T(8,128)} %lab_ref.5) | copy-start | bytes 196612
  0.0 15.1 %copy-start.1 = (s32[1,1,128]{2,1,0:T(1,128)S(1)}, s32[1,1,128]{2,1,0:T(1,128)}, u32[]{:S(2)}) copy-start(s32[1,1,128]{2,1,0:T(1,128)} %param.11) | copy-start | bytes 1540
  0.0 15.1 %copy-start.2 = (f32[137]{0:T(256)S(1)}, f32[137]{0:T(256)}, u32[]{:S(2)}) copy-start(f32[137]{0:T(256)} %param.9) | copy-start | bytes 1648
  6.3 10.3 %collective-permute-start = (bf16[144,128]{1,0:T(8,128)(2,1)S(1)}, bf16[144,128]{1,0:T(8,128)(2,1)S(1)}, u32[]{:S(2)}, u32[]{:S(2)}) collective-permute-start(bf16[144,128]{1,0:T(8,128)(2,1)S(1)} %get-tuple-element.22), channel_id=1, source_target_pairs={{0,1},{1,0},{2,18},{3,19},{4,5},{5,4},{6,22},{7,23},{8,9},{9,8},{1... | collective-permute-start | bytes 110600 | tf_op jit(solution)/shard_map/ppermute | solution.py:327
  7.8 8.8 %collective-permute-start.1 = (bf16[144,128]{1,0:T(8,128)(2,1)S(1)}, bf16[144,128]{1,0:T(8,128)(2,1)S(1)}, u32[]{:S(2)}, u32[]{:S(2)}) collective-permute-start(bf16[144,128]{1,0:T(8,128)(2,1)S(1)} %get-tuple-element.23), channel_id=1, source_target_pairs={{0,16},{1,17},{2,3},{3,2},{4,20},{5,21},{6,7},{7,6},{8,24},{9,25},... | collective-permute-start | bytes 110600 | tf_op jit(solution)/shard_map/ppermute | solution.py:328
  11.2 5.4 %collective-permute-start.2 = (bf16[144,128]{1,0:T(8,128)(2,1)S(1)}, bf16[144,128]{1,0:T(8,128)(2,1)S(1)}, u32[]{:S(2)}, u32[]{:S(2)}) collective-permute-start(bf16[144,128]{1,0:T(8,128)(2,1)S(1)} %get-tuple-element.24), channel_id=1, source_target_pairs={{0,15},{1,2},{2,1},{3,4},{4,3},{5,6},{6,5},{7,8},{8,7},{9,10},{10,... | collective-permute-start | bytes 110600 | tf_op jit(solution)/shard_map/ppermute | solution.py:329
  12.4 4.2 %collective-permute-start.3 = (bf16[144,128]{1,0:T(8,128)(2,1)S(1)}, bf16[144,128]{1,0:T(8,128)(2,1)S(1)}, u32[]{:S(2)}, u32[]{:S(2)}) collective-permute-start(bf16[144,128]{1,0:T(8,128)(2,1)S(1)} %get-tuple-element.25), channel_id=1, source_target_pairs={{0,1},{1,0},{2,3},{3,2},{4,5},{5,4},{6,7},{7,6},{8,9},{9,8},{10,11... | collective-permute-start | bytes 110600 | tf_op jit(solution)/shard_map/ppermute | solution.py:330
  16.9 6.6 %collective-permute-start.5 = (bf16[144,128]{1,0:T(8,128)(2,1)S(1)}, bf16[144,128]{1,0:T(8,128)(2,1)S(1)}, u32[]{:S(2)}, u32[]{:S(2)}) collective-permute-start(bf16[144,128]{1,0:T(8,128)(2,1)S(1)} %pack.1.p0), channel_id=1, source_target_pairs={{0,64},{16,80},{32,96},{48,112},{64,0},{80,16},{96,32},{112,48},{1... | collective-permute-start | bytes 110600 | tf_op jit(solution)/shard_map/ppermute | solution.py:350
  19.1 5.8 %collective-permute-start.4 = (bf16[144,128]{1,0:T(8,128)(2,1)S(1)}, bf16[144,128]{1,0:T(8,128)(2,1)S(1)}, u32[]{:S(2)}, u32[]{:S(2)}) collective-permute-start(bf16[144,128]{1,0:T(8,128)(2,1)S(1)} %pack.1.p0), channel_id=1, source_target_pairs={{0,1},{1,0},{2,3},{3,2},{4,5},{5,4},{6,7},{7,6},{8,9},{9,8},{10,11... | collective-permute-start | bytes 110600 | tf_op jit(solution)/shard_map/ppermute | solution.py:351
  23.6 1.4 %collective-permute-start.6 = (bf16[144,128]{1,0:T(8,128)(2,1)S(1)}, bf16[144,128]{1,0:T(8,128)(2,1)S(1)}, u32[]{:S(2)}, u32[]{:S(2)}) collective-permute-start(bf16[144,128]{1,0:T(8,128)(2,1)S(1)} %collective-permute-done.5.p2), channel_id=1, source_target_pairs={{0,1},{1,0},{2,3},{3,2},{4,5},{5,4},{6,7},{7,6},{8,9},{9,8},{10,11... | collective-permute-start | bytes 110600 | tf_op jit(solution)/shard_map/ppermute | solution.py:352

commit v5 on v4

--- a/solution.py
+++ b/solution.py
@@ -130,7 +130,7 @@
     c1_ref[...] = dot(picks[1], packed, NT).astype(BF16)
 
 
-def sums_kernel(t_ref, lab_ref, gl_ref, w_ref, t0_ref, root_ref, own_ref, band_ref, west_ref, east_ref):
+def sums_kernel(t_ref, lab_ref, gl_ref, w_ref, t0_ref, root_ref, own_ref, band_ref, marks_ref, west_ref, east_ref):
     root_ref[...] = jnp.sqrt(column(w_ref[...], KA)) * 0.125 + jnp.zeros((KA, N), F32)
     own_ref[...] = column(gl_ref[...].astype(F32), N) + jnp.zeros((N, N), F32)
     a, c = iota((2 * N, N), 0), iota((2 * N, N), 1)
@@ -168,30 +168,35 @@
         return 0
 
     lax.fori_loop(0, N // 64, patch_rows, 0)
-
-
-def pack_kernel(t0_ref, r0, r1, ro, rc, lab_ref, gl_ref, pay_ref):
-    north, south, west, east = halos(r0, r1, rc, ro)
-    lab = lab_ref[...].astype(F32)
-    ids = iota((N, N), 0).astype(F32)
-    sides = dot(ends(), lab.astype(BF16), NT)
-
-    def marks(row):
-        return jnp.where(row == ids, 0.125, 0.0)
-
-    left = jnp.concatenate([north, south, west, east], axis=1).astype(BF16)
-    right = jnp.concatenate(
-        [marks(lab[0:1]), marks(lab[N - 1 : N]), marks(sides[0:1]), marks(sides[1:2])], axis=1
-    ).astype(BF16)
-    total = t0_ref[...] + dot(left, right, NT)
-    count = total[LEV : LEV + 1] * (1.0 / 32.0)
+    total = t0_ref[LEV - LEV % 8 :, :]
+    count = total[LEV % 8 : LEV % 8 + 1] * (1.0 / 32.0)
     count_hi = jnp.floor(count * 0.125)
     gl = gl_ref[...].astype(F32)
     gl_hi = jnp.floor(gl * (1.0 / 64.0))
-    row = iota((KA, N), 0)
     for m, extra in enumerate((count_hi, count - 8.0 * count_hi, gl_hi, gl - 64.0 * gl_hi)):
-        total = jnp.where(row == LEV + m, extra, total)
-    pay_ref[...] = total.astype(BF16)
+        total = jnp.where(last == LEV + m, extra, total)
+    t0_ref[LEV - LEV % 8 :, :] = total
+
+    sides = dot(ends(), lab.astype(F32).astype(BF16), NT)
+    rows = iota((N, N), 0).astype(F32)
+
+    def edge_marks(row, there):
+        return jnp.where((row == rows) & there, 0.125, 0.0)
+
+    i, j = lax.axis_index("lat"), lax.axis_index("lon")
+    up, j_even = north_first(), lax.rem(j, 2) == 0
+    north = edge_marks(lab[0:1].astype(F32), i > 0)
+    south = edge_marks(lab[N - 1 : N].astype(F32), i < 7)
+    west, east = edge_marks(sides[0:1], True), edge_marks(sides[1:2], True)
+    marks_ref[...] = jnp.concatenate(
+        [jnp.where(up, north, south), jnp.where(up, south, north), jnp.where(j_even, west, east), jnp.where(j_even, east, west)],
+        axis=1,
+    ).astype(BF16)
+
+
+def pack_kernel(t0_ref, r0, r1, ro, rc, marks_ref, pay_ref):
+    left = jnp.concatenate([r0[...], r1[...], ro[...], rc[...]], axis=1)
+    pay_ref[...] = (t0_ref[...] + dot(left, marks_ref[...], NT)).astype(BF16)
 
 
 def smooth_rows(t_ref, side, root_ref, band_ref, s_ref, square_ref, row, count, to, extra=None):
@@ -328,11 +333,11 @@
     r1 = lax.ppermute(s1, ("lat", "lon"), vertical(1))
     ro = lax.ppermute(c1, "lon", [(j, (j + 1) % 16 if j % 2 else (j - 1) % 16) for j in range(16)])
     rc = lax.ppermute(c0, "lon", [(j, j ^ 1) for j in range(16)])
-    t0, root, own, band = pl.pallas_call(
+    t0, root, own, band, marks = pl.pallas_call(
         sums_kernel,
-        out_shape=(wide, wide, pltpu.VMEM((N, N), F32), pltpu.VMEM((2 * N, N), BF16)),
+        out_shape=(wide, wide, pltpu.VMEM((N, N), F32), pltpu.VMEM((2 * N, N), BF16), pltpu.VMEM((N, 4 * N), BF16)),
         in_specs=[vmem] * 4,
-        out_specs=[vmem] * 4,
+        out_specs=[vmem] * 5,
         scratch_shapes=[pltpu.VMEM((N, N), jnp.int32)] * 2,
         compiler_params=params(8),
         cost_estimate=cost(600_000_000, 9_500_000),
@@ -341,12 +346,12 @@
     pay = pl.pallas_call(
         pack_kernel,
         out_shape=edge,
-        in_specs=[vmem] * 7,
+        in_specs=[vmem] * 6,
         out_specs=vmem,
         compiler_params=params(8),
         cost_estimate=cost(20_000_000, 300_000),
         name="pack",
-    )(t0, r0, r1, ro, rc, labels, gl)
+    )(t0, r0, r1, ro, rc, marks)
     p2 = lax.ppermute(pay, "lat", [(i, (i + 4) % 8) for i in range(8)])
     p1 = lax.ppermute(pay, "lon", [(j, j ^ 1) for j in range(16)])
     p3 = lax.ppermute(p2, "lon", [(j, j ^ 1) for j in range(16)])

time: 27.3 us -> 27.1 us (level)
  transfers between devices with their start and end apart: 7 -> 7, of which waited for: 0 -> 0; matrix products, arithmetic and copies ran while one was open for 0% -> 0% of each run, Pallas kernels for 18% -> 19%
where the time goes in v5:
time: 27.1 us; the launch traced here: 27 us
  Pallas kernels  13.8 us (51%)
  starting transfers between devices  13.1 us (48%)
    pallas_call x1, Pallas kernels, shards(): pl.pallas_call(transport_kernel, out_shape=(pltpu.VMEM(((N + 2) * KP, N),...  6.27 us
    ppermute x1, starting transfers between devices, shards(): r1 = lax.ppermute(s1, ('lat', 'lon'), vertical(1))  3.4 us
    ppermute x1, starting transfers between devices, shards(): rc = lax.ppermute(c0, 'lon', [(j, j ^ 1) for j in range(16)])  2.7 us
    pallas_call x1, Pallas kernels, shards(): pl.pallas_call(smooth_top_kernel, out_shape=(pltpu.VMEM((TOP * KA, N), F3...  2.33 us
    ppermute x1, starting transfers between devices, shards(): p2 = lax.ppermute(pay, 'lat', [(i, (i + 4) % 8) for i in range(8)])  2.2 us
    pallas_call x1, Pallas kernels, shards(): pl.pallas_call(final_kernel, out_shape=jax.ShapeDtypeStruct((N, N), F32),...  2.19 us
    ppermute x1, starting transfers between devices, shards(): p1 = lax.ppermute(pay, 'lon', [(j, j ^ 1) for j in range(16)])  1.95 us
    pallas_call x1, Pallas kernels, shards(): pl.pallas_call(sums_kernel, out_shape=(wide, wide, pltpu.VMEM((N, N), F32...  1.61 us
  transfers between devices with their start and end apart: 7, of which 0 were waited for; matrix products, arithmetic and copies ran while one was open for 0% of the time, Pallas kernels for 19%

profile of v5, /device:TPU:1, one launch (start us, length us, event | category | flops | bytes accessed | tf_op | source)
XLA Modules:
  0.0 27.0 jit_solution(8578163931378512425)
XLA Ops:
  0.0 0.0 copy-start
  0.0 0.0 copy-start.2
  0.0 0.0 copy-start.1
  0.0 6.3 %transport.1 = (f32[19760,128]{1,0:T(8,128)S(1)}, bf16[144,128]{1,0:T(8,128)(2,1)S(1)}, bf16[144,128]{1,0:T(8,128)(2,1)S(1)}, bf16[144,128]{1,0:T(8,128)(2,1)S(1)}, bf16[144,128]{1,0:T(8,128)(2,1)S(1)}) custom-call(bf16[137,128,128]{2,1,0:T(8,128)(2,1)} %h_hbm.1, bf16[137,128,128]{2,1,0:T(8,128)(2,1)} %u_hbm.1, bf16[137,128,128]{2,1,0:T(8,128)(2,1)} %v_hbm.1), custom_call_target="tpu_custom_call" | custom-call | flops 30000000 | bytes 23000000 | tf_op jit(solution)/shard_map/transport/pallas_call | solution.py:320
  6.3 1.5 %collective-permute-start = (bf16[144,128]{1,0:T(8,128)(2,1)S(1)}, bf16[144,128]{1,0:T(8,128)(2,1)S(1)}, u32[]{:S(2)}, u32[]{:S(2)}) collective-permute-start(bf16[144,128]{1,0:T(8,128)(2,1)S(1)} %get-tuple-element.23), channel_id=1, source_target_pairs={{0,1},{1,0},{2,18},{3,19},{4,5},{5,4},{6,22},{7,23},{8,9},{9,8},{1... | collective-permute-start | bytes 110600 | tf_op jit(solution)/shard_map/ppermute | solution.py:332
  7.8 3.4 %collective-permute-start.1 = (bf16[144,128]{1,0:T(8,128)(2,1)S(1)}, bf16[144,128]{1,0:T(8,128)(2,1)S(1)}, u32[]{:S(2)}, u32[]{:S(2)}) collective-permute-start(bf16[144,128]{1,0:T(8,128)(2,1)S(1)} %get-tuple-element.24), channel_id=1, source_target_pairs={{0,16},{1,17},{2,3},{3,2},{4,20},{5,21},{6,7},{7,6},{8,24},{9,25},... | collective-permute-start | bytes 110600 | tf_op jit(solution)/shard_map/ppermute | solution.py:333
  11.2 1.2 %collective-permute-start.2 = (bf16[144,128]{1,0:T(8,128)(2,1)S(1)}, bf16[144,128]{1,0:T(8,128)(2,1)S(1)}, u32[]{:S(2)}, u32[]{:S(2)}) collective-permute-start(bf16[144,128]{1,0:T(8,128)(2,1)S(1)} %get-tuple-element.25), channel_id=1, source_target_pairs={{0,15},{1,2},{2,1},{3,4},{4,3},{5,6},{6,5},{7,8},{8,7},{9,10},{10,... | collective-permute-start | bytes 110600 | tf_op jit(solution)/shard_map/ppermute | solution.py:334
  12.4 2.7 %collective-permute-start.3 = (bf16[144,128]{1,0:T(8,128)(2,1)S(1)}, bf16[144,128]{1,0:T(8,128)(2,1)S(1)}, u32[]{:S(2)}, u32[]{:S(2)}) collective-permute-start(bf16[144,128]{1,0:T(8,128)(2,1)S(1)} %get-tuple-element.26), channel_id=1, source_target_pairs={{0,1},{1,0},{2,3},{3,2},{4,5},{5,4},{6,7},{7,6},{8,9},{9,8},{10,11... | collective-permute-start | bytes 110600 | tf_op jit(solution)/shard_map/ppermute | solution.py:335
  15.1 0.0 copy-done
  15.1 0.0 copy-done.2
  15.1 0.0 copy-done.1
  15.1 1.6 %sums.1 = (f32[144,128]{1,0:T(8,128)S(1)}, f32[144,128]{1,0:T(8,128)S(1)}, f32[128,128]{1,0:T(8,128)S(1)}, bf16[256,128]{1,0:T(8,128)(2,1)S(1)}, bf16[128,512]{1,0:T(8,128)(2,1)S(1)}) custom-call(f32[19760,128]{1,0:T(8,128)S(1)} %get-tuple-element.21.t_ref, s32[128,128]{1,0:T(8,128)S(1)} %copy-done, s32[1,128]{1,0:T(1,128)S(1)} %bitcast.3, f32[1,137]{1,0:T(1,128)S(1)} %bitcast.2), custom_call_target="tpu_custom_call" | custom-call | flops 600000000 | bytes 9500000 | tf_op jit(solution)/shard_map/sums/pallas_call | solution.py:336
  16.7 0.0 collective-permute-done.r0
  16.7 0.0 collective-permute-done.1.r1
  16.7 0.0 collective-permute-done.2.ro
  16.7 0.0 collective-permute-done.3.rc
  16.7 0.2 pack.1.p0
  17.0 2.2 %collective-permute-start.5 = (bf16[144,128]{1,0:T(8,128)(2,1)S(1)}, bf16[144,128]{1,0:T(8,128)(2,1)S(1)}, u32[]{:S(2)}, u32[]{:S(2)}) collective-permute-start(bf16[144,128]{1,0:T(8,128)(2,1)S(1)} %pack.1.p0), channel_id=1, source_target_pairs={{0,64},{16,80},{32,96},{48,112},{64,0},{80,16},{96,32},{112,48},{1... | collective-permute-start | bytes 110600 | tf_op jit(solution)/shard_map/ppermute | solution.py:355
  19.1 1.9 %collective-permute-start.4 = (bf16[144,128]{1,0:T(8,128)(2,1)S(1)}, bf16[144,128]{1,0:T(8,128)(2,1)S(1)}, u32[]{:S(2)}, u32[]{:S(2)}) collective-permute-start(bf16[144,128]{1,0:T(8,128)(2,1)S(1)} %pack.1.p0), channel_id=1, source_target_pairs={{0,1},{1,0},{2,3},{3,2},{4,5},{5,4},{6,7},{7,6},{8,9},{9,8},{10,11... | collective-permute-start | bytes 110600 | tf_op jit(solution)/shard_map/ppermute | solution.py:356
  21.1 2.3 %smooth_top.1 = (f32[12672,128]{1,0:T(8,128)S(1)}, f32[88,128]{1,0:T(8,128)S(1)}, bf16[144,128]{1,0:T(8,128)(2,1)S(1)}, f32[144,128]{1,0:T(8,128)S(1)}) custom-call(f32[19760,128]{1,0:T(8,128)S(1)} %get-tuple-element.21.t_ref, bf16[144,128]{1,0:T(8,128)(2,1)S(1)} %collective-permute-done.r0, bf16[144,128]{1,0:T(8,128)(2,1)S(1)} %collective-permute-done.1.r1, ...), custom_call_target="tpu_custom_call" | custom-call | flops 600000000 | bytes 9500000 | tf_op jit(solution)/shard_map/smooth_top/pallas_call | solution.py:358
  23.4 0.0 collective-permute-done.5.p2
  23.4 0.2 collective-permute-start.6
  23.7 1.2 %smooth_bottom.1 = (f32[5760,128]{1,0:T(8,128)S(1)}, f32[40,128]{1,0:T(8,128)S(1)}) custom-call(f32[19760,128]{1,0:T(8,128)S(1)} %get-tuple-element.21.t_ref, bf16[144,128]{1,0:T(8,128)(2,1)S(1)} %get-tuple-element.31.side_ref, f32[144,128]{1,0:T(8,128)S(1)} %get-tuple-element.32.south_ref, f32[144,128]{1,0:T(8,128)S(1)} %get-tuple-element.28.root_ref, ...), custom_call_target="tpu_custom_call" | custom-call | flops 600000000 | bytes 9500000 | tf_op jit(solution)/shard_map/smooth_bottom/pallas_call | solution.py:367
  24.8 0.0 collective-permute-done.4.p1
  24.8 0.0 collective-permute-done.6.p3
  24.8 2.2 %final.1 = f32[128,128]{1,0:T(8,128)} custom-call(bf16[144,128]{1,0:T(8,128)(2,1)S(1)} %pack.1.p0, bf16[144,128]{1,0:T(8,128)(2,1)S(1)} %collective-permute-done.4.p1, bf16[144,128]{1,0:T(8,128)(2,1)S(1)} %collective-permute-done.5.p2, bf16[144,128]{1,0:T(8,128)(2,1)S(1)} %collective-permute-done.6.p3, f32[12672,128]{1,0:T(8,128)S(1)} %get-tuple-element.30.s0_ref, ...), custom_call_target="tpu_custom_call" | custom-call | flops 300000000 | bytes 9500000 | tf_op jit(solution)/shard_map/final/pallas_call | solution.py:376
Async XLA Ops:
  0.0 15.1 %copy-start = (s32[128,128]{1,0:T(8,128)S(1)}, s32[128,128]{1,0:T(8,128)}, u32[]{:S(2)}) copy-start(s32[128,128]{1,0:T(8,128)} %lab_ref.3) | copy-start | bytes 196612
  0.0 15.1 %copy-start.2 = (s32[1,1,128]{2,1,0:T(1,128)S(1)}, s32[1,1,128]{2,1,0:T(1,128)}, u32[]{:S(2)}) copy-start(s32[1,1,128]{2,1,0:T(1,128)} %param.11) | copy-start | bytes 1540
  0.0 15.1 %copy-start.1 = (f32[137]{0:T(256)S(1)}, f32[137]{0:T(256)}, u32[]{:S(2)}) copy-start(f32[137]{0:T(256)} %param.9) | copy-start | bytes 1648
  6.3 10.4 %collective-permute-start = (bf16[144,128]{1,0:T(8,128)(2,1)S(1)}, bf16[144,128]{1,0:T(8,128)(2,1)S(1)}, u32[]{:S(2)}, u32[]{:S(2)}) collective-permute-start(bf16[144,128]{1,0:T(8,128)(2,1)S(1)} %get-tuple-element.23), channel_id=1, source_target_pairs={{0,1},{1,0},{2,18},{3,19},{4,5},{5,4},{6,22},{7,23},{8,9},{9,8},{1... | collective-permute-start | bytes 110600 | tf_op jit(solution)/shard_map/ppermute | solution.py:332
  7.8 8.9 %collective-permute-start.1 = (bf16[144,128]{1,0:T(8,128)(2,1)S(1)}, bf16[144,128]{1,0:T(8,128)(2,1)S(1)}, u32[]{:S(2)}, u32[]{:S(2)}) collective-permute-start(bf16[144,128]{1,0:T(8,128)(2,1)S(1)} %get-tuple-element.24), channel_id=1, source_target_pairs={{0,16},{1,17},{2,3},{3,2},{4,20},{5,21},{6,7},{7,6},{8,24},{9,25},... | collective-permute-start | bytes 110600 | tf_op jit(solution)/shard_map/ppermute | solution.py:333
  11.2 5.5 %collective-permute-start.2 = (bf16[144,128]{1,0:T(8,128)(2,1)S(1)}, bf16[144,128]{1,0:T(8,128)(2,1)S(1)}, u32[]{:S(2)}, u32[]{:S(2)}) collective-permute-start(bf16[144,128]{1,0:T(8,128)(2,1)S(1)} %get-tuple-element.25), channel_id=1, source_target_pairs={{0,15},{1,2},{2,1},{3,4},{4,3},{5,6},{6,5},{7,8},{8,7},{9,10},{10,... | collective-permute-start | bytes 110600 | tf_op jit(solution)/shard_map/ppermute | solution.py:334
  12.4 4.4 %collective-permute-start.3 = (bf16[144,128]{1,0:T(8,128)(2,1)S(1)}, bf16[144,128]{1,0:T(8,128)(2,1)S(1)}, u32[]{:S(2)}, u32[]{:S(2)}) collective-permute-start(bf16[144,128]{1,0:T(8,128)(2,1)S(1)} %get-tuple-element.26), channel_id=1, source_target_pairs={{0,1},{1,0},{2,3},{3,2},{4,5},{5,4},{6,7},{7,6},{8,9},{9,8},{10,11... | collective-permute-start | bytes 110600 | tf_op jit(solution)/shard_map/ppermute | solution.py:335
  17.0 6.5 %collective-permute-start.5 = (bf16[144,128]{1,0:T(8,128)(2,1)S(1)}, bf16[144,128]{1,0:T(8,128)(2,1)S(1)}, u32[]{:S(2)}, u32[]{:S(2)}) collective-permute-start(bf16[144,128]{1,0:T(8,128)(2,1)S(1)} %pack.1.p0), channel_id=1, source_target_pairs={{0,64},{16,80},{32,96},{48,112},{64,0},{80,16},{96,32},{112,48},{1... | collective-permute-start | bytes 110600 | tf_op jit(solution)/shard_map/ppermute | solution.py:355
  19.1 5.7 %collective-permute-start.4 = (bf16[144,128]{1,0:T(8,128)(2,1)S(1)}, bf16[144,128]{1,0:T(8,128)(2,1)S(1)}, u32[]{:S(2)}, u32[]{:S(2)}) collective-permute-start(bf16[144,128]{1,0:T(8,128)(2,1)S(1)} %pack.1.p0), channel_id=1, source_target_pairs={{0,1},{1,0},{2,3},{3,2},{4,5},{5,4},{6,7},{7,6},{8,9},{9,8},{10,11... | collective-permute-start | bytes 110600 | tf_op jit(solution)/shard_map/ppermute | solution.py:356
  23.4 1.4 %collective-permute-start.6 = (bf16[144,128]{1,0:T(8,128)(2,1)S(1)}, bf16[144,128]{1,0:T(8,128)(2,1)S(1)}, u32[]{:S(2)}, u32[]{:S(2)}) collective-permute-start(bf16[144,128]{1,0:T(8,128)(2,1)S(1)} %collective-permute-done.5.p2), channel_id=1, source_target_pairs={{0,1},{1,0},{2,3},{3,2},{4,5},{5,4},{6,7},{7,6},{8,9},{9,8},{10,11... | collective-permute-start | bytes 110600 | tf_op jit(solution)/shard_map/ppermute | solution.py:357

commit v6 on v5

--- a/solution.py
+++ b/solution.py
@@ -53,7 +53,7 @@
     return north, south, west, east
 
 
-def transport_kernel(h_hbm, u_hbm, v_hbm, t_ref, s0_ref, s1_ref, c0_ref, c1_ref, hb, ub, vb, cols, near, picks, sems):
+def transport_kernel(h_hbm, u_hbm, v_hbm, t_ref, s0_ref, s1_ref, c0_ref, c1_ref, band_ref, hb, ub, vb, cols, near, picks, sems):
     copies = []
     for c, (a, n) in enumerate(CHUNKS):
         row = []
@@ -77,6 +77,13 @@
     picks[0] = jnp.where(at == jnp.where(j_even, right_at, left_at), 1.0, 0.0).astype(BF16)
     picks[1] = jnp.where(at == jnp.where(j_even, left_at, right_at), 1.0, 0.0).astype(BF16)
 
+    a, c = iota((3 * N, 2 * N), 0), iota((3 * N, 2 * N), 1)
+    a_in, a_of, c_in, c_of = lax.rem(a, N), lax.div(a, N), lax.rem(c, N), lax.div(c, N)
+    band = jnp.where(a_in == c_in, 4.0, jnp.where(jnp.abs(a_in - c_in) == 1, 1.0, 0.0))
+    edge = jnp.where(c_in == jnp.where(a_in < 64, 0, N - 1), 1.0, 0.0)
+    edge = jnp.where(lax.rem(a, 2) == c_of, edge, 0.0)
+    band_ref[...] = jnp.where(a_of == 2, edge, jnp.where(a_of == c_of, band, 0.0)).astype(BF16)
+
     def level(k):
         parts = []
         for b in range(0, N, 32):
@@ -130,13 +137,9 @@
     c1_ref[...] = dot(picks[1], packed, NT).astype(BF16)
 
 
-def sums_kernel(t_ref, lab_ref, gl_ref, w_ref, t0_ref, root_ref, own_ref, band_ref, marks_ref, west_ref, east_ref):
+def sums_kernel(t_ref, lab_ref, gl_ref, w_ref, t0_ref, root_ref, own_ref, marks_ref, west_ref, east_ref):
     root_ref[...] = jnp.sqrt(column(w_ref[...], KA)) * 0.125 + jnp.zeros((KA, N), F32)
     own_ref[...] = column(gl_ref[...].astype(F32), N) + jnp.zeros((N, N), F32)
-    a, c = iota((2 * N, N), 0), iota((2 * N, N), 1)
-    band = jnp.where(a == c, 4.0, jnp.where(jnp.abs(a - c) == 1, 1.0, 0.0))
-    edge = jnp.where(c == jnp.where(a < N + 64, 0, N - 1), 1.0, 0.0)
-    band_ref[...] = jnp.where(a < N, band, edge).astype(BF16)
     lab = lab_ref[...]
     lane = iota((N, N), 1)
     west_ref[...] = jnp.where(lane == 0, -1, pltpu.roll(lab, 1, 1))
@@ -200,21 +203,23 @@
 
 
 def smooth_rows(t_ref, side, root_ref, band_ref, s_ref, square_ref, row, count, to, extra=None):
-    lane = lax.rem(iota((1, N), 1), 64)
+    pair = lax.div(lax.rem(iota((1, N), 1), 64), 2)
 
     def at(r):
         return pl.ds(pl.multiple_of(r * KP, 8), KA)
 
     lefts = []
-    for m in range(count):
-        mine = jnp.where(lane == lax.rem(row + m, 64), 1.0, 0.0).astype(BF16)
-        lefts.append(jnp.concatenate([t_ref[at(row + m + 1), :].astype(BF16), side * mine], axis=1))
+    for m in range(0, count, 2):
+        mine = jnp.where(pair == lax.div(lax.rem(row + m, 64), 2), 1.0, 0.0).astype(BF16)
+        two = [t_ref[at(row + m + n), :].astype(BF16) for n in (1, 2)]
+        lefts.append(jnp.concatenate([*two, side * mine], axis=1))
     across = dot(jnp.concatenate(lefts, axis=0), band_ref[...], NN)
     for m in range(count):
         along = t_ref[at(row + m), :] + t_ref[at(row + m + 2), :]
         if extra is not None and m == extra[0]:
             along = along + extra[1]
-        s = (across[m * KA : (m + 1) * KA] + along) * root_ref[...]
+        here = across[m // 2 * KA : (m // 2 + 1) * KA, m % 2 * N : (m % 2 + 1) * N]
+        s = (here + along) * root_ref[...]
         s_ref[pl.ds(pl.multiple_of((to + m) * KA, 8), KA), :] = s
         square_ref[pl.ds(to + m, 1), :] = jnp.sum(s * s, axis=0, keepdims=True)
 
@@ -317,11 +322,11 @@
     wide = pltpu.VMEM((KA, N), F32)
     gl = global_labels.reshape(1, N)
     w = weights.reshape(1, LEV)
-    t, s0, s1, c0, c1 = pl.pallas_call(
+    t, s0, s1, c0, c1, band = pl.pallas_call(
         transport_kernel,
-        out_shape=(pltpu.VMEM(((N + 2) * KP, N), F32), edge, edge, edge, edge),
+        out_shape=(pltpu.VMEM(((N + 2) * KP, N), F32), edge, edge, edge, edge, pltpu.VMEM((3 * N, 2 * N), BF16)),
         in_specs=[anywhere] * 3,
-        out_specs=[vmem] * 5,
+        out_specs=[vmem] * 6,
         scratch_shapes=[pltpu.VMEM((LEV, N, N), BF16)] * 3
         + [pltpu.VMEM((3, N, N), BF16), pltpu.VMEM((N, N), BF16), pltpu.VMEM((2, KA, 3 * N), BF16)]
         + [pltpu.SemaphoreType.DMA((len(CHUNKS), 3))],
@@ -333,11 +338,11 @@
     r1 = lax.ppermute(s1, ("lat", "lon"), vertical(1))
     ro = lax.ppermute(c1, "lon", [(j, (j + 1) % 16 if j % 2 else (j - 1) % 16) for j in range(16)])
     rc = lax.ppermute(c0, "lon", [(j, j ^ 1) for j in range(16)])
-    t0, root, own, band, marks = pl.pallas_call(
+    t0, root, own, marks = pl.pallas_call(
         sums_kernel,
-        out_shape=(wide, wide, pltpu.VMEM((N, N), F32), pltpu.VMEM((2 * N, N), BF16), pltpu.VMEM((N, 4 * N), BF16)),
+        out_shape=(wide, wide, pltpu.VMEM((N, N), F32), pltpu.VMEM((N, 4 * N), BF16)),
         in_specs=[vmem] * 4,
-        out_specs=[vmem] * 5,
+        out_specs=[vmem] * 4,
         scratch_shapes=[pltpu.VMEM((N, N), jnp.int32)] * 2,
         compiler_params=params(8),
         cost_estimate=cost(600_000_000, 9_500_000),

time: 27.1 us -> 27.1 us (level)
  no operation moved by 1% of the time
where the time goes in v6:
time: 27.1 us; the launch traced here: 27 us
  Pallas kernels  13.7 us (51%)
  starting transfers between devices  13.2 us (49%)
    pallas_call x1, Pallas kernels, shards(): pl.pallas_call(transport_kernel, out_shape=(pltpu.VMEM(((N + 2) * KP, N),...  6.27 us
    ppermute x1, starting transfers between devices, shards(): r1 = lax.ppermute(s1, ('lat', 'lon'), vertical(1))  3.4 us
    ppermute x1, starting transfers between devices, shards(): rc = lax.ppermute(c0, 'lon', [(j, j ^ 1) for j in range(16)])  2.7 us
    pallas_call x1, Pallas kernels, shards(): pl.pallas_call(smooth_top_kernel, out_shape=(pltpu.VMEM((TOP * KA, N), F3...  2.32 us
    ppermute x1, starting transfers between devices, shards(): p2 = lax.ppermute(pay, 'lat', [(i, (i + 4) % 8) for i in range(8)])  2.2 us
    pallas_call x1, Pallas kernels, shards(): pl.pallas_call(final_kernel, out_shape=jax.ShapeDtypeStruct((N, N), F32),...  2.19 us
    ppermute x1, starting transfers between devices, shards(): p1 = lax.ppermute(pay, 'lon', [(j, j ^ 1) for j in range(16)])  1.94 us
    pallas_call x1, Pallas kernels, shards(): pl.pallas_call(sums_kernel, out_shape=(wide, wide, pltpu.VMEM((N, N), F32...  1.62 us
  transfers between devices with their start and end apart: 7, of which 0 were waited for; matrix products, arithmetic and copies ran while one was open for 0% of the time, Pallas kernels for 19%

profile of v6, /device:TPU:1, one launch (start us, length us, event | category | flops | bytes accessed | tf_op | source)
XLA Modules:
  0.0 27.0 jit_solution(14042589072218276166)
XLA Ops:
  0.0 0.0 copy-start
  0.0 0.0 copy-start.2
  0.0 0.0 copy-start.1
  0.0 6.3 %transport.1 = (f32[19760,128]{1,0:T(8,128)S(1)}, bf16[144,128]{1,0:T(8,128)(2,1)S(1)}, bf16[144,128]{1,0:T(8,128)(2,1)S(1)}, bf16[144,128]{1,0:T(8,128)(2,1)S(1...) custom-call(bf16[137,128,128]{2,1,0:T(8,128)(2,1)} %h_hbm.1, bf16[137,128,128]{2,1,0:T(8,128)(2,1)} %u_hbm.1, ...), custom_call_target="tpu_custom_call" | custom-call | flops 30000000 | bytes 23000000 | tf_op jit(solution)/shard_map/transport/pallas_call | solution.py:325
  6.3 1.5 %collective-permute-start = (bf16[144,128]{1,0:T(8,128)(2,1)S(1)}, bf16[144,128]{1,0:T(8,128)(2,1)S(1)}, u32[]{:S(2)}, u32[]{:S(2)}) collective-permute-start(bf16[144,128]{1,0:T(8,128)(2,1)S(1)} %get-tuple-element.23), channel_id=1, source_target_pairs={{0,1},{1,0},{2,18},{3,19},{4,5},{5,4},{6,22},{7,23},{8,9},{9,8},{1... | collective-permute-start | bytes 110600 | tf_op jit(solution)/shard_map/ppermute | solution.py:337
  7.8 3.4 %collective-permute-start.1 = (bf16[144,128]{1,0:T(8,128)(2,1)S(1)}, bf16[144,128]{1,0:T(8,128)(2,1)S(1)}, u32[]{:S(2)}, u32[]{:S(2)}) collective-permute-start(bf16[144,128]{1,0:T(8,128)(2,1)S(1)} %get-tuple-element.24), channel_id=1, source_target_pairs={{0,16},{1,17},{2,3},{3,2},{4,20},{5,21},{6,7},{7,6},{8,24},{9,25},... | collective-permute-start | bytes 110600 | tf_op jit(solution)/shard_map/ppermute | solution.py:338
  11.2 1.2 %collective-permute-start.2 = (bf16[144,128]{1,0:T(8,128)(2,1)S(1)}, bf16[144,128]{1,0:T(8,128)(2,1)S(1)}, u32[]{:S(2)}, u32[]{:S(2)}) collective-permute-start(bf16[144,128]{1,0:T(8,128)(2,1)S(1)} %get-tuple-element.25), channel_id=1, source_target_pairs={{0,15},{1,2},{2,1},{3,4},{4,3},{5,6},{6,5},{7,8},{8,7},{9,10},{10,... | collective-permute-start | bytes 110600 | tf_op jit(solution)/shard_map/ppermute | solution.py:339
  12.4 2.7 %collective-permute-start.3 = (bf16[144,128]{1,0:T(8,128)(2,1)S(1)}, bf16[144,128]{1,0:T(8,128)(2,1)S(1)}, u32[]{:S(2)}, u32[]{:S(2)}) collective-permute-start(bf16[144,128]{1,0:T(8,128)(2,1)S(1)} %get-tuple-element.26), channel_id=1, source_target_pairs={{0,1},{1,0},{2,3},{3,2},{4,5},{5,4},{6,7},{7,6},{8,9},{9,8},{10,11... | collective-permute-start | bytes 110600 | tf_op jit(solution)/shard_map/ppermute | solution.py:340
  15.1 0.0 copy-done
  15.1 0.0 copy-done.2
  15.1 0.0 copy-done.1
  15.1 1.6 %sums.1 = (f32[144,128]{1,0:T(8,128)S(1)}, f32[144,128]{1,0:T(8,128)S(1)}, f32[128,128]{1,0:T(8,128)S(1)}, bf16[128,512]{1,0:T(8,128)(2,1)S(1)}) custom-call(f32[19760,128]{1,0:T(8,128)S(1)} %get-tuple-element.21.t_ref, s32[128,128]{1,0:T(8,128)S(1)} %copy-done, s32[1,128]{1,0:T(1,128)S(1)} %bitcast.3, f32[1,137]{1,0:T(1,128)S(1)} %bitcast.2), custom_call_target="tpu_custom_call" | custom-call | flops 600000000 | bytes 9500000 | tf_op jit(solution)/shard_map/sums/pallas_call | solution.py:341
  16.7 0.0 collective-permute-done.r0
  16.7 0.0 collective-permute-done.1.r1
  16.7 0.0 collective-permute-done.2.ro
  16.7 0.0 collective-permute-done.3.rc
  16.8 0.2 pack.1.p0
  17.0 2.2 %collective-permute-start.5 = (bf16[144,128]{1,0:T(8,128)(2,1)S(1)}, bf16[144,128]{1,0:T(8,128)(2,1)S(1)}, u32[]{:S(2)}, u32[]{:S(2)}) collective-permute-start(bf16[144,128]{1,0:T(8,128)(2,1)S(1)} %pack.1.p0), channel_id=1, source_target_pairs={{0,64},{16,80},{32,96},{48,112},{64,0},{80,16},{96,32},{112,48},{1... | collective-permute-start | bytes 110600 | tf_op jit(solution)/shard_map/ppermute | solution.py:360
  19.2 1.9 %collective-permute-start.4 = (bf16[144,128]{1,0:T(8,128)(2,1)S(1)}, bf16[144,128]{1,0:T(8,128)(2,1)S(1)}, u32[]{:S(2)}, u32[]{:S(2)}) collective-permute-start(bf16[144,128]{1,0:T(8,128)(2,1)S(1)} %pack.1.p0), channel_id=1, source_target_pairs={{0,1},{1,0},{2,3},{3,2},{4,5},{5,4},{6,7},{7,6},{8,9},{9,8},{10,11... | collective-permute-start | bytes 110600 | tf_op jit(solution)/shard_map/ppermute | solution.py:361
  21.1 2.3 %smooth_top.1 = (f32[12672,128]{1,0:T(8,128)S(1)}, f32[88,128]{1,0:T(8,128)S(1)}, bf16[144,128]{1,0:T(8,128)(2,1)S(1)}, f32[144,128]{1,0:T(8,128)S(1)}) custom-call(f32[19760,128]{1,0:T(8,128)S(1)} %get-tuple-element.21.t_ref, bf16[144,128]{1,0:T(8,128)(2,1)S(1)} %collective-permute-done.r0, bf16[144,128]{1,0:T(8,128)(2,1)S(1)} %collective-permute-done.1.r1, ...), custom_call_target="tpu_custom_call" | custom-call | flops 600000000 | bytes 9500000 | tf_op jit(solution)/shard_map/smooth_top/pallas_call | solution.py:363
  23.4 0.0 collective-permute-done.5.p2
  23.4 0.2 collective-permute-start.6
  23.7 1.1 %smooth_bottom.1 = (f32[5760,128]{1,0:T(8,128)S(1)}, f32[40,128]{1,0:T(8,128)S(1)}) custom-call(f32[19760,128]{1,0:T(8,128)S(1)} %get-tuple-element.21.t_ref, bf16[144,128]{1,0:T(8,128)(2,1)S(1)} %get-tuple-element.31.side_ref, f32[144,128]{1,0:T(8,128)S(1)} %get-tuple-element.32.south_ref, f32[144,128]{1,0:T(8,128)S(1)} %get-tuple-element.28.root_ref, ...), custom_call_target="tpu_custom_call" | custom-call | flops 600000000 | bytes 9500000 | tf_op jit(solution)/shard_map/smooth_bottom/pallas_call | solution.py:372
  24.8 0.0 collective-permute-done.4.p1
  24.8 0.0 collective-permute-done.6.p3
  24.8 2.2 %final.1 = f32[128,128]{1,0:T(8,128)} custom-call(bf16[144,128]{1,0:T(8,128)(2,1)S(1)} %pack.1.p0, bf16[144,128]{1,0:T(8,128)(2,1)S(1)} %collective-permute-done.4.p1, bf16[144,128]{1,0:T(8,128)(2,1)S(1)} %collective-permute-done.5.p2, bf16[144,128]{1,0:T(8,128)(2,1)S(1)} %collective-permute-done.6.p3, f32[12672,128]{1,0:T(8,128)S(1)} %get-tuple-element.30.s0_ref, ...), custom_call_target="tpu_custom_call" | custom-call | flops 300000000 | bytes 9500000 | tf_op jit(solution)/shard_map/final/pallas_call | solution.py:381
Async XLA Ops:
  0.0 15.1 %copy-start = (s32[128,128]{1,0:T(8,128)S(1)}, s32[128,128]{1,0:T(8,128)}, u32[]{:S(2)}) copy-start(s32[128,128]{1,0:T(8,128)} %lab_ref.3) | copy-start | bytes 196612
  0.0 15.1 %copy-start.2 = (s32[1,1,128]{2,1,0:T(1,128)S(1)}, s32[1,1,128]{2,1,0:T(1,128)}, u32[]{:S(2)}) copy-start(s32[1,1,128]{2,1,0:T(1,128)} %param.11) | copy-start | bytes 1540
  0.0 15.1 %copy-start.1 = (f32[137]{0:T(256)S(1)}, f32[137]{0:T(256)}, u32[]{:S(2)}) copy-start(f32[137]{0:T(256)} %param.9) | copy-start | bytes 1648
  6.3 10.4 %collective-permute-start = (bf16[144,128]{1,0:T(8,128)(2,1)S(1)}, bf16[144,128]{1,0:T(8,128)(2,1)S(1)}, u32[]{:S(2)}, u32[]{:S(2)}) collective-permute-start(bf16[144,128]{1,0:T(8,128)(2,1)S(1)} %get-tuple-element.23), channel_id=1, source_target_pairs={{0,1},{1,0},{2,18},{3,19},{4,5},{5,4},{6,22},{7,23},{8,9},{9,8},{1... | collective-permute-start | bytes 110600 | tf_op jit(solution)/shard_map/ppermute | solution.py:337
  7.8 8.9 %collective-permute-start.1 = (bf16[144,128]{1,0:T(8,128)(2,1)S(1)}, bf16[144,128]{1,0:T(8,128)(2,1)S(1)}, u32[]{:S(2)}, u32[]{:S(2)}) collective-permute-start(bf16[144,128]{1,0:T(8,128)(2,1)S(1)} %get-tuple-element.24), channel_id=1, source_target_pairs={{0,16},{1,17},{2,3},{3,2},{4,20},{5,21},{6,7},{7,6},{8,24},{9,25},... | collective-permute-start | bytes 110600 | tf_op jit(solution)/shard_map/ppermute | solution.py:338
  11.2 5.6 %collective-permute-start.2 = (bf16[144,128]{1,0:T(8,128)(2,1)S(1)}, bf16[144,128]{1,0:T(8,128)(2,1)S(1)}, u32[]{:S(2)}, u32[]{:S(2)}) collective-permute-start(bf16[144,128]{1,0:T(8,128)(2,1)S(1)} %get-tuple-element.25), channel_id=1, source_target_pairs={{0,15},{1,2},{2,1},{3,4},{4,3},{5,6},{6,5},{7,8},{8,7},{9,10},{10,... | collective-permute-start | bytes 110600 | tf_op jit(solution)/shard_map/ppermute | solution.py:339
  12.4 4.4 %collective-permute-start.3 = (bf16[144,128]{1,0:T(8,128)(2,1)S(1)}, bf16[144,128]{1,0:T(8,128)(2,1)S(1)}, u32[]{:S(2)}, u32[]{:S(2)}) collective-permute-start(bf16[144,128]{1,0:T(8,128)(2,1)S(1)} %get-tuple-element.26), channel_id=1, source_target_pairs={{0,1},{1,0},{2,3},{3,2},{4,5},{5,4},{6,7},{7,6},{8,9},{9,8},{10,11... | collective-permute-start | bytes 110600 | tf_op jit(solution)/shard_map/ppermute | solution.py:340
  17.0 6.5 %collective-permute-start.5 = (bf16[144,128]{1,0:T(8,128)(2,1)S(1)}, bf16[144,128]{1,0:T(8,128)(2,1)S(1)}, u32[]{:S(2)}, u32[]{:S(2)}) collective-permute-start(bf16[144,128]{1,0:T(8,128)(2,1)S(1)} %pack.1.p0), channel_id=1, source_target_pairs={{0,64},{16,80},{32,96},{48,112},{64,0},{80,16},{96,32},{112,48},{1... | collective-permute-start | bytes 110600 | tf_op jit(solution)/shard_map/ppermute | solution.py:360
  19.2 5.6 %collective-permute-start.4 = (bf16[144,128]{1,0:T(8,128)(2,1)S(1)}, bf16[144,128]{1,0:T(8,128)(2,1)S(1)}, u32[]{:S(2)}, u32[]{:S(2)}) collective-permute-start(bf16[144,128]{1,0:T(8,128)(2,1)S(1)} %pack.1.p0), channel_id=1, source_target_pairs={{0,1},{1,0},{2,3},{3,2},{4,5},{5,4},{6,7},{7,6},{8,9},{9,8},{10,11... | collective-permute-start | bytes 110600 | tf_op jit(solution)/shard_map/ppermute | solution.py:361
  23.4 1.4 %collective-permute-start.6 = (bf16[144,128]{1,0:T(8,128)(2,1)S(1)}, bf16[144,128]{1,0:T(8,128)(2,1)S(1)}, u32[]{:S(2)}, u32[]{:S(2)}) collective-permute-start(bf16[144,128]{1,0:T(8,128)(2,1)S(1)} %collective-permute-done.5.p2), channel_id=1, source_target_pairs={{0,1},{1,0},{2,3},{3,2},{4,5},{5,4},{6,7},{7,6},{8,9},{9,8},{10,11... | collective-permute-start | bytes 110600 | tf_op jit(solution)/shard_map/ppermute | solution.py:362

commit v7 on v6

--- a/solution.py
+++ b/solution.py
@@ -253,7 +253,7 @@
     lax.fori_loop(0, 2, rows, 0)
 
 
-def final_kernel(p0, p1, p2, p3, s0_ref, s1_ref, square0, square1, lab_ref, own_ref, root_ref, out_ref, e_ref):
+def final_kernel(p0, p1, p2, p3, s0_ref, s1_ref, square0, square1, lab_ref, own_ref, root_ref, out_ref, e_ref, cross_ref):
     own = own_ref[...]
     lefts, rights = [], []
     for p in (p0, p1, p2, p3):
@@ -283,7 +283,7 @@
         for m in range(4):
             r = 4 * q + m
             cross = s_ref[pl.ds((r - top) * KA, KA), :] * placed
-            out_ref[pl.ds(r, 1), :] = jnp.sum(cross, axis=0, keepdims=True)
+            cross_ref[pl.ds(8 * r, 8), :] = jnp.sum(cross.reshape(KA // 8, 8, N), axis=0)
 
     for q in range(N // 4):
         if 4 * q < TOP:
@@ -292,7 +292,8 @@
             patch_row(q, s1_ref, TOP)
     e = e_ref[...]
     square = jnp.concatenate([square0[...], square1[...]], axis=0)
-    out_ref[...] = jnp.sqrt(jnp.maximum(square - 2.0 * out_ref[...] + e, 0.0) / e)
+    cross = sum(cross_ref[pl.ds(m, N, stride=8), :] for m in range(8))
+    out_ref[...] = jnp.sqrt(jnp.maximum(square - 2.0 * cross + e, 0.0) / e)
 
 
 def vertical(turn):
@@ -383,7 +384,7 @@
         out_shape=jax.ShapeDtypeStruct((N, N), F32),
         in_specs=[vmem] * 11,
         out_specs=vmem,
-        scratch_shapes=[pltpu.VMEM((N, N), F32)],
+        scratch_shapes=[pltpu.VMEM((N, N), F32), pltpu.VMEM((8 * N, N), F32)],
         compiler_params=params(8),
         cost_estimate=cost(300_000_000, 9_500_000),
         name="final",

time: 27.1 us -> 27.1 us (level)
  no operation moved by 1% of the time
where the time goes in v7:
time: 27.1 us; the launch traced here: 27 us
  Pallas kernels  13.7 us (51%)
  starting transfers between devices  13.2 us (49%)
    pallas_call x1, Pallas kernels, shards(): pl.pallas_call(transport_kernel, out_shape=(pltpu.VMEM(((N + 2) * KP, N),...  6.27 us
    ppermute x1, starting transfers between devices, shards(): r1 = lax.ppermute(s1, ('lat', 'lon'), vertical(1))  3.4 us
    ppermute x1, starting transfers between devices, shards(): rc = lax.ppermute(c0, 'lon', [(j, j ^ 1) for j in range(16)])  2.7 us
    pallas_call x1, Pallas kernels, shards(): pl.pallas_call(smooth_top_kernel, out_shape=(pltpu.VMEM((TOP * KA, N), F3...  2.32 us
    ppermute x1, starting transfers between devices, shards(): p2 = lax.ppermute(pay, 'lat', [(i, (i + 4) % 8) for i in range(8)])  2.2 us
    pallas_call x1, Pallas kernels, shards(): pl.pallas_call(final_kernel, out_shape=jax.ShapeDtypeStruct((N, N), F32),...  2.14 us
    ppermute x1, starting transfers between devices, shards(): p1 = lax.ppermute(pay, 'lon', [(j, j ^ 1) for j in range(16)])  1.94 us
    pallas_call x1, Pallas kernels, shards(): pl.pallas_call(sums_kernel, out_shape=(wide, wide, pltpu.VMEM((N, N), F32...  1.62 us
  transfers between devices with their start and end apart: 7, of which 0 were waited for; matrix products, arithmetic and copies ran while one was open for 0% of the time, Pallas kernels for 19%

profile of v7, /device:TPU:1, one launch (start us, length us, event | category | flops | bytes accessed | tf_op | source)
XLA Modules:
  0.0 27.0 jit_solution(5689906997245385607)
XLA Ops:
  0.0 0.0 copy-start
  0.0 0.0 copy-start.2
  0.0 0.0 copy-start.1
  0.0 6.3 %transport.1 = (f32[19760,128]{1,0:T(8,128)S(1)}, bf16[144,128]{1,0:T(8,128)(2,1)S(1)}, bf16[144,128]{1,0:T(8,128)(2,1)S(1)}, bf16[144,128]{1,0:T(8,128)(2,1)S(1...) custom-call(bf16[137,128,128]{2,1,0:T(8,128)(2,1)} %h_hbm.1, bf16[137,128,128]{2,1,0:T(8,128)(2,1)} %u_hbm.1, ...), custom_call_target="tpu_custom_call" | custom-call | flops 30000000 | bytes 23000000 | tf_op jit(solution)/shard_map/transport/pallas_call | solution.py:326
  6.3 1.5 %collective-permute-start = (bf16[144,128]{1,0:T(8,128)(2,1)S(1)}, bf16[144,128]{1,0:T(8,128)(2,1)S(1)}, u32[]{:S(2)}, u32[]{:S(2)}) collective-permute-start(bf16[144,128]{1,0:T(8,128)(2,1)S(1)} %get-tuple-element.23), channel_id=1, source_target_pairs={{0,1},{1,0},{2,18},{3,19},{4,5},{5,4},{6,22},{7,23},{8,9},{9,8},{1... | collective-permute-start | bytes 110600 | tf_op jit(solution)/shard_map/ppermute | solution.py:338
  7.8 3.4 %collective-permute-start.1 = (bf16[144,128]{1,0:T(8,128)(2,1)S(1)}, bf16[144,128]{1,0:T(8,128)(2,1)S(1)}, u32[]{:S(2)}, u32[]{:S(2)}) collective-permute-start(bf16[144,128]{1,0:T(8,128)(2,1)S(1)} %get-tuple-element.24), channel_id=1, source_target_pairs={{0,16},{1,17},{2,3},{3,2},{4,20},{5,21},{6,7},{7,6},{8,24},{9,25},... | collective-permute-start | bytes 110600 | tf_op jit(solution)/shard_map/ppermute | solution.py:339
  11.2 1.2 %collective-permute-start.2 = (bf16[144,128]{1,0:T(8,128)(2,1)S(1)}, bf16[144,128]{1,0:T(8,128)(2,1)S(1)}, u32[]{:S(2)}, u32[]{:S(2)}) collective-permute-start(bf16[144,128]{1,0:T(8,128)(2,1)S(1)} %get-tuple-element.25), channel_id=1, source_target_pairs={{0,15},{1,2},{2,1},{3,4},{4,3},{5,6},{6,5},{7,8},{8,7},{9,10},{10,... | collective-permute-start | bytes 110600 | tf_op jit(solution)/shard_map/ppermute | solution.py:340
  12.4 2.7 %collective-permute-start.3 = (bf16[144,128]{1,0:T(8,128)(2,1)S(1)}, bf16[144,128]{1,0:T(8,128)(2,1)S(1)}, u32[]{:S(2)}, u32[]{:S(2)}) collective-permute-start(bf16[144,128]{1,0:T(8,128)(2,1)S(1)} %get-tuple-element.26), channel_id=1, source_target_pairs={{0,1},{1,0},{2,3},{3,2},{4,5},{5,4},{6,7},{7,6},{8,9},{9,8},{10,11... | collective-permute-start | bytes 110600 | tf_op jit(solution)/shard_map/ppermute | solution.py:341
  15.1 0.0 copy-done
  15.1 0.0 copy-done.2
  15.1 0.0 copy-done.1
  15.1 1.6 %sums.1 = (f32[144,128]{1,0:T(8,128)S(1)}, f32[144,128]{1,0:T(8,128)S(1)}, f32[128,128]{1,0:T(8,128)S(1)}, bf16[128,512]{1,0:T(8,128)(2,1)S(1)}) custom-call(f32[19760,128]{1,0:T(8,128)S(1)} %get-tuple-element.21.t_ref, s32[128,128]{1,0:T(8,128)S(1)} %copy-done, s32[1,128]{1,0:T(1,128)S(1)} %bitcast.3, f32[1,137]{1,0:T(1,128)S(1)} %bitcast.2), custom_call_target="tpu_custom_call" | custom-call | flops 600000000 | bytes 9500000 | tf_op jit(solution)/shard_map/sums/pallas_call | solution.py:342
  16.7 0.0 collective-permute-done.r0
  16.7 0.0 collective-permute-done.1.r1
  16.7 0.0 collective-permute-done.2.ro
  16.7 0.0 collective-permute-done.3.rc
  16.8 0.2 pack.1.p0
  17.0 2.2 %collective-permute-start.5 = (bf16[144,128]{1,0:T(8,128)(2,1)S(1)}, bf16[144,128]{1,0:T(8,128)(2,1)S(1)}, u32[]{:S(2)}, u32[]{:S(2)}) collective-permute-start(bf16[144,128]{1,0:T(8,128)(2,1)S(1)} %pack.1.p0), channel_id=1, source_target_pairs={{0,64},{16,80},{32,96},{48,112},{64,0},{80,16},{96,32},{112,48},{1... | collective-permute-start | bytes 110600 | tf_op jit(solution)/shard_map/ppermute | solution.py:361
  19.2 1.9 %collective-permute-start.4 = (bf16[144,128]{1,0:T(8,128)(2,1)S(1)}, bf16[144,128]{1,0:T(8,128)(2,1)S(1)}, u32[]{:S(2)}, u32[]{:S(2)}) collective-permute-start(bf16[144,128]{1,0:T(8,128)(2,1)S(1)} %pack.1.p0), channel_id=1, source_target_pairs={{0,1},{1,0},{2,3},{3,2},{4,5},{5,4},{6,7},{7,6},{8,9},{9,8},{10,11... | collective-permute-start | bytes 110600 | tf_op jit(solution)/shard_map/ppermute | solution.py:362
  21.1 2.3 %smooth_top.1 = (f32[12672,128]{1,0:T(8,128)S(1)}, f32[88,128]{1,0:T(8,128)S(1)}, bf16[144,128]{1,0:T(8,128)(2,1)S(1)}, f32[144,128]{1,0:T(8,128)S(1)}) custom-call(f32[19760,128]{1,0:T(8,128)S(1)} %get-tuple-element.21.t_ref, bf16[144,128]{1,0:T(8,128)(2,1)S(1)} %collective-permute-done.r0, bf16[144,128]{1,0:T(8,128)(2,1)S(1)} %collective-permute-done.1.r1, ...), custom_call_target="tpu_custom_call" | custom-call | flops 600000000 | bytes 9500000 | tf_op jit(solution)/shard_map/smooth_top/pallas_call | solution.py:364
  23.4 0.0 collective-permute-done.5.p2
  23.4 0.2 collective-permute-start.6
  23.7 1.1 %smooth_bottom.1 = (f32[5760,128]{1,0:T(8,128)S(1)}, f32[40,128]{1,0:T(8,128)S(1)}) custom-call(f32[19760,128]{1,0:T(8,128)S(1)} %get-tuple-element.21.t_ref, bf16[144,128]{1,0:T(8,128)(2,1)S(1)} %get-tuple-element.31.side_ref, f32[144,128]{1,0:T(8,128)S(1)} %get-tuple-element.32.south_ref, f32[144,128]{1,0:T(8,128)S(1)} %get-tuple-element.28.root_ref, ...), custom_call_target="tpu_custom_call" | custom-call | flops 600000000 | bytes 9500000 | tf_op jit(solution)/shard_map/smooth_bottom/pallas_call | solution.py:373
  24.8 0.0 collective-permute-done.4.p1
  24.8 0.0 collective-permute-done.6.p3
  24.8 2.1 %final.1 = f32[128,128]{1,0:T(8,128)} custom-call(bf16[144,128]{1,0:T(8,128)(2,1)S(1)} %pack.1.p0, bf16[144,128]{1,0:T(8,128)(2,1)S(1)} %collective-permute-done.4.p1, bf16[144,128]{1,0:T(8,128)(2,1)S(1)} %collective-permute-done.5.p2, bf16[144,128]{1,0:T(8,128)(2,1)S(1)} %collective-permute-done.6.p3, f32[12672,128]{1,0:T(8,128)S(1)} %get-tuple-element.30.s0_ref, ...), custom_call_target="tpu_custom_call" | custom-call | flops 300000000 | bytes 9500000 | tf_op jit(solution)/shard_map/final/pallas_call | solution.py:382
Async XLA Ops:
  0.0 15.1 %copy-start = (s32[128,128]{1,0:T(8,128)S(1)}, s32[128,128]{1,0:T(8,128)}, u32[]{:S(2)}) copy-start(s32[128,128]{1,0:T(8,128)} %lab_ref.3) | copy-start | bytes 196612
  0.0 15.1 %copy-start.2 = (s32[1,1,128]{2,1,0:T(1,128)S(1)}, s32[1,1,128]{2,1,0:T(1,128)}, u32[]{:S(2)}) copy-start(s32[1,1,128]{2,1,0:T(1,128)} %param.11) | copy-start | bytes 1540
  0.0 15.1 %copy-start.1 = (f32[137]{0:T(256)S(1)}, f32[137]{0:T(256)}, u32[]{:S(2)}) copy-start(f32[137]{0:T(256)} %param.9) | copy-start | bytes 1648
  6.3 10.4 %collective-permute-start = (bf16[144,128]{1,0:T(8,128)(2,1)S(1)}, bf16[144,128]{1,0:T(8,128)(2,1)S(1)}, u32[]{:S(2)}, u32[]{:S(2)}) collective-permute-start(bf16[144,128]{1,0:T(8,128)(2,1)S(1)} %get-tuple-element.23), channel_id=1, source_target_pairs={{0,1},{1,0},{2,18},{3,19},{4,5},{5,4},{6,22},{7,23},{8,9},{9,8},{1... | collective-permute-start | bytes 110600 | tf_op jit(solution)/shard_map/ppermute | solution.py:338
  7.8 8.9 %collective-permute-start.1 = (bf16[144,128]{1,0:T(8,128)(2,1)S(1)}, bf16[144,128]{1,0:T(8,128)(2,1)S(1)}, u32[]{:S(2)}, u32[]{:S(2)}) collective-permute-start(bf16[144,128]{1,0:T(8,128)(2,1)S(1)} %get-tuple-element.24), channel_id=1, source_target_pairs={{0,16},{1,17},{2,3},{3,2},{4,20},{5,21},{6,7},{7,6},{8,24},{9,25},... | collective-permute-start | bytes 110600 | tf_op jit(solution)/shard_map/ppermute | solution.py:339
  11.2 5.6 %collective-permute-start.2 = (bf16[144,128]{1,0:T(8,128)(2,1)S(1)}, bf16[144,128]{1,0:T(8,128)(2,1)S(1)}, u32[]{:S(2)}, u32[]{:S(2)}) collective-permute-start(bf16[144,128]{1,0:T(8,128)(2,1)S(1)} %get-tuple-element.25), channel_id=1, source_target_pairs={{0,15},{1,2},{2,1},{3,4},{4,3},{5,6},{6,5},{7,8},{8,7},{9,10},{10,... | collective-permute-start | bytes 110600 | tf_op jit(solution)/shard_map/ppermute | solution.py:340
  12.4 4.4 %collective-permute-start.3 = (bf16[144,128]{1,0:T(8,128)(2,1)S(1)}, bf16[144,128]{1,0:T(8,128)(2,1)S(1)}, u32[]{:S(2)}, u32[]{:S(2)}) collective-permute-start(bf16[144,128]{1,0:T(8,128)(2,1)S(1)} %get-tuple-element.26), channel_id=1, source_target_pairs={{0,1},{1,0},{2,3},{3,2},{4,5},{5,4},{6,7},{7,6},{8,9},{9,8},{10,11... | collective-permute-start | bytes 110600 | tf_op jit(solution)/shard_map/ppermute | solution.py:341
  17.0 6.5 %collective-permute-start.5 = (bf16[144,128]{1,0:T(8,128)(2,1)S(1)}, bf16[144,128]{1,0:T(8,128)(2,1)S(1)}, u32[]{:S(2)}, u32[]{:S(2)}) collective-permute-start(bf16[144,128]{1,0:T(8,128)(2,1)S(1)} %pack.1.p0), channel_id=1, source_target_pairs={{0,64},{16,80},{32,96},{48,112},{64,0},{80,16},{96,32},{112,48},{1... | collective-permute-start | bytes 110600 | tf_op jit(solution)/shard_map/ppermute | solution.py:361
  19.2 5.6 %collective-permute-start.4 = (bf16[144,128]{1,0:T(8,128)(2,1)S(1)}, bf16[144,128]{1,0:T(8,128)(2,1)S(1)}, u32[]{:S(2)}, u32[]{:S(2)}) collective-permute-start(bf16[144,128]{1,0:T(8,128)(2,1)S(1)} %pack.1.p0), channel_id=1, source_target_pairs={{0,1},{1,0},{2,3},{3,2},{4,5},{5,4},{6,7},{7,6},{8,9},{9,8},{10,11... | collective-permute-start | bytes 110600 | tf_op jit(solution)/shard_map/ppermute | solution.py:362
  23.4 1.4 %collective-permute-start.6 = (bf16[144,128]{1,0:T(8,128)(2,1)S(1)}, bf16[144,128]{1,0:T(8,128)(2,1)S(1)}, u32[]{:S(2)}, u32[]{:S(2)}) collective-permute-start(bf16[144,128]{1,0:T(8,128)(2,1)S(1)} %collective-permute-done.5.p2), channel_id=1, source_target_pairs={{0,1},{1,0},{2,3},{3,2},{4,5},{5,4},{6,7},{7,6},{8,9},{9,8},{10,11... | collective-permute-start | bytes 110600 | tf_op jit(solution)/shard_map/ppermute | solution.py:363

commit v8 on v7

--- a/solution.py
+++ b/solution.py
@@ -212,7 +212,10 @@
     for m in range(0, count, 2):
         mine = jnp.where(pair == lax.div(lax.rem(row + m, 64), 2), 1.0, 0.0).astype(BF16)
         two = [t_ref[at(row + m + n), :].astype(BF16) for n in (1, 2)]
-        lefts.append(jnp.concatenate([*two, side * mine], axis=1))
+        half = side
+        if side.shape[0] > KA:
+            half = side[pl.ds(pl.multiple_of(KA * lax.div(row + m, 64), 16), KA), :]
+        lefts.append(jnp.concatenate([*two, half * mine], axis=1))
     across = dot(jnp.concatenate(lefts, axis=0), band_ref[...], NN)
     for m in range(count):
         along = t_ref[at(row + m), :] + t_ref[at(row + m + 2), :]
@@ -224,21 +227,23 @@
         square_ref[pl.ds(to + m, 1), :] = jnp.sum(s * s, axis=0, keepdims=True)
 
 
-def smooth_top_kernel(t_ref, r0, r1, rc, ro, root_ref, band_ref, s_ref, square_ref, side_ref, south_ref):
+def smooth_top_kernel(t_ref, r0, r1, rc, ro, root_ref, band_ref, s_ref, square_ref, side_ref, south_ref, sides):
     north, south, west, east = halos(r0, r1, rc, ro)
     low = iota((KA, N), 1) < 64
     side_ref[...] = jnp.where(low, pltpu.roll(west, 64, 1), east).astype(BF16)
     south_ref[...] = south
     side = jnp.where(low, west, pltpu.roll(east, 64, 1)).astype(BF16)
 
+    sides[pl.ds(0, KA), :] = side
+    sides[pl.ds(KA, KA), :] = side_ref[...]
+    count = TOP // 2
+
     def rows(i, _):
         beyond = jnp.where(i == 0, north, 0.0)
-        smooth_rows(t_ref, side, root_ref, band_ref, s_ref, square_ref, 32 * i, 32, 32 * i, (0, beyond))
+        smooth_rows(t_ref, sides, root_ref, band_ref, s_ref, square_ref, count * i, count, count * i, (0, beyond))
         return 0
 
     lax.fori_loop(0, 2, rows, 0)
-    if TOP > 64:
-        smooth_rows(t_ref, side_ref[...], root_ref, band_ref, s_ref, square_ref, 64, TOP - 64, 64)
 
 
 def smooth_bottom_kernel(t_ref, side_ref, south_ref, root_ref, band_ref, s_ref, square_ref):
@@ -366,6 +371,7 @@
         out_shape=(pltpu.VMEM((TOP * KA, N), F32), pltpu.VMEM((TOP, N), F32), edge, wide),
         in_specs=[vmem] * 7,
         out_specs=[vmem] * 4,
+        scratch_shapes=[pltpu.VMEM((2 * KA, N), BF16)],
         compiler_params=params(12),
         cost_estimate=cost(600_000_000, 9_500_000),
         name="smooth_top",

time: 27.1 us -> 27.1 us (level)
  no operation moved by 1% of the time
where the time goes in v8:
time: 27.1 us; the launch traced here: 27 us
  Pallas kernels  13.6 us (50%)
  starting transfers between devices  13.2 us (49%)
    pallas_call x1, Pallas kernels, shards(): pl.pallas_call(transport_kernel, out_shape=(pltpu.VMEM(((N + 2) * KP, N),...  6.27 us
    ppermute x1, starting transfers between devices, shards(): r1 = lax.ppermute(s1, ('lat', 'lon'), vertical(1))  3.4 us
    ppermute x1, starting transfers between devices, shards(): rc = lax.ppermute(c0, 'lon', [(j, j ^ 1) for j in range(16)])  2.7 us
    pallas_call x1, Pallas kernels, shards(): pl.pallas_call(smooth_top_kernel, out_shape=(pltpu.VMEM((TOP * KA, N), F3...  2.27 us
    ppermute x1, starting transfers between devices, shards(): p2 = lax.ppermute(pay, 'lat', [(i, (i + 4) % 8) for i in range(8)])  2.2 us
    pallas_call x1, Pallas kernels, shards(): pl.pallas_call(final_kernel, out_shape=jax.ShapeDtypeStruct((N, N), F32),...  2.14 us
    ppermute x1, starting transfers between devices, shards(): p1 = lax.ppermute(pay, 'lon', [(j, j ^ 1) for j in range(16)])  1.94 us
    pallas_call x1, Pallas kernels, shards(): pl.pallas_call(sums_kernel, out_shape=(wide, wide, pltpu.VMEM((N, N), F32...  1.62 us
  transfers between devices with their start and end apart: 7, of which 0 were waited for; matrix products, arithmetic and copies ran while one was open for 0% of the time, Pallas kernels for 19%

profile of v8, /device:TPU:1, one launch (start us, length us, event | category | flops | bytes accessed | tf_op | source)
XLA Modules:
  0.0 27.0 jit_solution(2074915449782454759)
XLA Ops:
  0.0 0.0 copy-start
  0.0 0.0 copy-start.2
  0.0 0.0 copy-start.1
  0.0 6.3 %transport.1 = (f32[19760,128]{1,0:T(8,128)S(1)}, bf16[144,128]{1,0:T(8,128)(2,1)S(1)}, bf16[144,128]{1,0:T(8,128)(2,1)S(1)}, bf16[144,128]{1,0:T(8,128)(2,1)S(1...) custom-call(bf16[137,128,128]{2,1,0:T(8,128)(2,1)} %h_hbm.1, bf16[137,128,128]{2,1,0:T(8,128)(2,1)} %u_hbm.1, ...), custom_call_target="tpu_custom_call" | custom-call | flops 30000000 | bytes 23000000 | tf_op jit(solution)/shard_map/transport/pallas_call | solution.py:331
  6.3 1.5 %collective-permute-start = (bf16[144,128]{1,0:T(8,128)(2,1)S(1)}, bf16[144,128]{1,0:T(8,128)(2,1)S(1)}, u32[]{:S(2)}, u32[]{:S(2)}) collective-permute-start(bf16[144,128]{1,0:T(8,128)(2,1)S(1)} %get-tuple-element.23), channel_id=1, source_target_pairs={{0,1},{1,0},{2,18},{3,19},{4,5},{5,4},{6,22},{7,23},{8,9},{9,8},{1... | collective-permute-start | bytes 110600 | tf_op jit(solution)/shard_map/ppermute | solution.py:343
  7.8 3.4 %collective-permute-start.1 = (bf16[144,128]{1,0:T(8,128)(2,1)S(1)}, bf16[144,128]{1,0:T(8,128)(2,1)S(1)}, u32[]{:S(2)}, u32[]{:S(2)}) collective-permute-start(bf16[144,128]{1,0:T(8,128)(2,1)S(1)} %get-tuple-element.24), channel_id=1, source_target_pairs={{0,16},{1,17},{2,3},{3,2},{4,20},{5,21},{6,7},{7,6},{8,24},{9,25},... | collective-permute-start | bytes 110600 | tf_op jit(solution)/shard_map/ppermute | solution.py:344
  11.2 1.2 %collective-permute-start.2 = (bf16[144,128]{1,0:T(8,128)(2,1)S(1)}, bf16[144,128]{1,0:T(8,128)(2,1)S(1)}, u32[]{:S(2)}, u32[]{:S(2)}) collective-permute-start(bf16[144,128]{1,0:T(8,128)(2,1)S(1)} %get-tuple-element.25), channel_id=1, source_target_pairs={{0,15},{1,2},{2,1},{3,4},{4,3},{5,6},{6,5},{7,8},{8,7},{9,10},{10,... | collective-permute-start | bytes 110600 | tf_op jit(solution)/shard_map/ppermute | solution.py:345
  12.4 2.7 %collective-permute-start.3 = (bf16[144,128]{1,0:T(8,128)(2,1)S(1)}, bf16[144,128]{1,0:T(8,128)(2,1)S(1)}, u32[]{:S(2)}, u32[]{:S(2)}) collective-permute-start(bf16[144,128]{1,0:T(8,128)(2,1)S(1)} %get-tuple-element.26), channel_id=1, source_target_pairs={{0,1},{1,0},{2,3},{3,2},{4,5},{5,4},{6,7},{7,6},{8,9},{9,8},{10,11... | collective-permute-start | bytes 110600 | tf_op jit(solution)/shard_map/ppermute | solution.py:346
  15.1 0.0 copy-done
  15.1 0.0 copy-done.2
  15.1 0.0 copy-done.1
  15.1 1.6 %sums.1 = (f32[144,128]{1,0:T(8,128)S(1)}, f32[144,128]{1,0:T(8,128)S(1)}, f32[128,128]{1,0:T(8,128)S(1)}, bf16[128,512]{1,0:T(8,128)(2,1)S(1)}) custom-call(f32[19760,128]{1,0:T(8,128)S(1)} %get-tuple-element.21.t_ref, s32[128,128]{1,0:T(8,128)S(1)} %copy-done, s32[1,128]{1,0:T(1,128)S(1)} %bitcast.3, f32[1,137]{1,0:T(1,128)S(1)} %bitcast.2), custom_call_target="tpu_custom_call" | custom-call | flops 600000000 | bytes 9500000 | tf_op jit(solution)/shard_map/sums/pallas_call | solution.py:347
  16.7 0.0 collective-permute-done.r0
  16.7 0.0 collective-permute-done.1.r1
  16.7 0.0 collective-permute-done.2.ro
  16.7 0.0 collective-permute-done.3.rc
  16.8 0.2 pack.1.p0
  17.0 2.2 %collective-permute-start.5 = (bf16[144,128]{1,0:T(8,128)(2,1)S(1)}, bf16[144,128]{1,0:T(8,128)(2,1)S(1)}, u32[]{:S(2)}, u32[]{:S(2)}) collective-permute-start(bf16[144,128]{1,0:T(8,128)(2,1)S(1)} %pack.1.p0), channel_id=1, source_target_pairs={{0,64},{16,80},{32,96},{48,112},{64,0},{80,16},{96,32},{112,48},{1... | collective-permute-start | bytes 110600 | tf_op jit(solution)/shard_map/ppermute | solution.py:366
  19.2 1.9 %collective-permute-start.4 = (bf16[144,128]{1,0:T(8,128)(2,1)S(1)}, bf16[144,128]{1,0:T(8,128)(2,1)S(1)}, u32[]{:S(2)}, u32[]{:S(2)}) collective-permute-start(bf16[144,128]{1,0:T(8,128)(2,1)S(1)} %pack.1.p0), channel_id=1, source_target_pairs={{0,1},{1,0},{2,3},{3,2},{4,5},{5,4},{6,7},{7,6},{8,9},{9,8},{10,11... | collective-permute-start | bytes 110600 | tf_op jit(solution)/shard_map/ppermute | solution.py:367
  21.1 2.3 %smooth_top.1 = (f32[12672,128]{1,0:T(8,128)S(1)}, f32[88,128]{1,0:T(8,128)S(1)}, bf16[144,128]{1,0:T(8,128)(2,1)S(1)}, f32[144,128]{1,0:T(8,128)S(1)}) custom-call(f32[19760,128]{1,0:T(8,128)S(1)} %get-tuple-element.21.t_ref, bf16[144,128]{1,0:T(8,128)(2,1)S(1)} %collective-permute-done.r0, bf16[144,128]{1,0:T(8,128)(2,1)S(1)} %collective-permute-done.1.r1, ...), custom_call_target="tpu_custom_call" | custom-call | flops 600000000 | bytes 9500000 | tf_op jit(solution)/shard_map/smooth_top/pallas_call | solution.py:369
  23.4 0.0 collective-permute-done.5.p2
  23.4 0.3 %collective-permute-start.6 = (bf16[144,128]{1,0:T(8,128)(2,1)S(1)}, bf16[144,128]{1,0:T(8,128)(2,1)S(1)}, u32[]{:S(2)}, u32[]{:S(2)}) collective-permute-start(bf16[144,128]{1,0:T(8,128)(2,1)S(1)} %collective-permute-done.5.p2), channel_id=1, source_target_pairs={{0,1},{1,0},{2,3},{3,2},{4,5},{5,4},{6,7},{7,6},{8,9},{9,8},{10,11... | collective-permute-start | bytes 110600 | tf_op jit(solution)/shard_map/ppermute | solution.py:368
  23.7 1.1 %smooth_bottom.1 = (f32[5760,128]{1,0:T(8,128)S(1)}, f32[40,128]{1,0:T(8,128)S(1)}) custom-call(f32[19760,128]{1,0:T(8,128)S(1)} %get-tuple-element.21.t_ref, bf16[144,128]{1,0:T(8,128)(2,1)S(1)} %get-tuple-element.31.side_ref, f32[144,128]{1,0:T(8,128)S(1)} %get-tuple-element.32.south_ref, f32[144,128]{1,0:T(8,128)S(1)} %get-tuple-element.28.root_ref, ...), custom_call_target="tpu_custom_call" | custom-call | flops 600000000 | bytes 9500000 | tf_op jit(solution)/shard_map/smooth_bottom/pallas_call | solution.py:379
  24.8 0.0 collective-permute-done.4.p1
  24.8 0.0 collective-permute-done.6.p3
  24.8 2.1 %final.1 = f32[128,128]{1,0:T(8,128)} custom-call(bf16[144,128]{1,0:T(8,128)(2,1)S(1)} %pack.1.p0, bf16[144,128]{1,0:T(8,128)(2,1)S(1)} %collective-permute-done.4.p1, bf16[144,128]{1,0:T(8,128)(2,1)S(1)} %collective-permute-done.5.p2, bf16[144,128]{1,0:T(8,128)(2,1)S(1)} %collective-permute-done.6.p3, f32[12672,128]{1,0:T(8,128)S(1)} %get-tuple-element.30.s0_ref, ...), custom_call_target="tpu_custom_call" | custom-call | flops 300000000 | bytes 9500000 | tf_op jit(solution)/shard_map/final/pallas_call | solution.py:388
Async XLA Ops:
  0.0 15.1 %copy-start = (s32[128,128]{1,0:T(8,128)S(1)}, s32[128,128]{1,0:T(8,128)}, u32[]{:S(2)}) copy-start(s32[128,128]{1,0:T(8,128)} %lab_ref.3) | copy-start | bytes 196612
  0.0 15.1 %copy-start.2 = (s32[1,1,128]{2,1,0:T(1,128)S(1)}, s32[1,1,128]{2,1,0:T(1,128)}, u32[]{:S(2)}) copy-start(s32[1,1,128]{2,1,0:T(1,128)} %param.11) | copy-start | bytes 1540
  0.0 15.1 %copy-start.1 = (f32[137]{0:T(256)S(1)}, f32[137]{0:T(256)}, u32[]{:S(2)}) copy-start(f32[137]{0:T(256)} %param.9) | copy-start | bytes 1648
  6.3 10.4 %collective-permute-start = (bf16[144,128]{1,0:T(8,128)(2,1)S(1)}, bf16[144,128]{1,0:T(8,128)(2,1)S(1)}, u32[]{:S(2)}, u32[]{:S(2)}) collective-permute-start(bf16[144,128]{1,0:T(8,128)(2,1)S(1)} %get-tuple-element.23), channel_id=1, source_target_pairs={{0,1},{1,0},{2,18},{3,19},{4,5},{5,4},{6,22},{7,23},{8,9},{9,8},{1... | collective-permute-start | bytes 110600 | tf_op jit(solution)/shard_map/ppermute | solution.py:343
  7.8 8.9 %collective-permute-start.1 = (bf16[144,128]{1,0:T(8,128)(2,1)S(1)}, bf16[144,128]{1,0:T(8,128)(2,1)S(1)}, u32[]{:S(2)}, u32[]{:S(2)}) collective-permute-start(bf16[144,128]{1,0:T(8,128)(2,1)S(1)} %get-tuple-element.24), channel_id=1, source_target_pairs={{0,16},{1,17},{2,3},{3,2},{4,20},{5,21},{6,7},{7,6},{8,24},{9,25},... | collective-permute-start | bytes 110600 | tf_op jit(solution)/shard_map/ppermute | solution.py:344
  11.2 5.6 %collective-permute-start.2 = (bf16[144,128]{1,0:T(8,128)(2,1)S(1)}, bf16[144,128]{1,0:T(8,128)(2,1)S(1)}, u32[]{:S(2)}, u32[]{:S(2)}) collective-permute-start(bf16[144,128]{1,0:T(8,128)(2,1)S(1)} %get-tuple-element.25), channel_id=1, source_target_pairs={{0,15},{1,2},{2,1},{3,4},{4,3},{5,6},{6,5},{7,8},{8,7},{9,10},{10,... | collective-permute-start | bytes 110600 | tf_op jit(solution)/shard_map/ppermute | solution.py:345
  12.4 4.4 %collective-permute-start.3 = (bf16[144,128]{1,0:T(8,128)(2,1)S(1)}, bf16[144,128]{1,0:T(8,128)(2,1)S(1)}, u32[]{:S(2)}, u32[]{:S(2)}) collective-permute-start(bf16[144,128]{1,0:T(8,128)(2,1)S(1)} %get-tuple-element.26), channel_id=1, source_target_pairs={{0,1},{1,0},{2,3},{3,2},{4,5},{5,4},{6,7},{7,6},{8,9},{9,8},{10,11... | collective-permute-start | bytes 110600 | tf_op jit(solution)/shard_map/ppermute | solution.py:346
  17.0 6.4 %collective-permute-start.5 = (bf16[144,128]{1,0:T(8,128)(2,1)S(1)}, bf16[144,128]{1,0:T(8,128)(2,1)S(1)}, u32[]{:S(2)}, u32[]{:S(2)}) collective-permute-start(bf16[144,128]{1,0:T(8,128)(2,1)S(1)} %pack.1.p0), channel_id=1, source_target_pairs={{0,64},{16,80},{32,96},{48,112},{64,0},{80,16},{96,32},{112,48},{1... | collective-permute-start | bytes 110600 | tf_op jit(solution)/shard_map/ppermute | solution.py:366
  19.2 5.6 %collective-permute-start.4 = (bf16[144,128]{1,0:T(8,128)(2,1)S(1)}, bf16[144,128]{1,0:T(8,128)(2,1)S(1)}, u32[]{:S(2)}, u32[]{:S(2)}) collective-permute-start(bf16[144,128]{1,0:T(8,128)(2,1)S(1)} %pack.1.p0), channel_id=1, source_target_pairs={{0,1},{1,0},{2,3},{3,2},{4,5},{5,4},{6,7},{7,6},{8,9},{9,8},{10,11... | collective-permute-start | bytes 110600 | tf_op jit(solution)/shard_map/ppermute | solution.py:367
  23.4 1.4 %collective-permute-start.6 = (bf16[144,128]{1,0:T(8,128)(2,1)S(1)}, bf16[144,128]{1,0:T(8,128)(2,1)S(1)}, u32[]{:S(2)}, u32[]{:S(2)}) collective-permute-start(bf16[144,128]{1,0:T(8,128)(2,1)S(1)} %collective-permute-done.5.p2), channel_id=1, source_target_pairs={{0,1},{1,0},{2,3},{3,2},{4,5},{5,4},{6,7},{7,6},{8,9},{9,8},{10,11... | collective-permute-start | bytes 110600 | tf_op jit(solution)/shard_map/ppermute | solution.py:368

commit v9 on v8

--- a/solution.py
+++ b/solution.py
@@ -224,10 +224,10 @@
         here = across[m // 2 * KA : (m // 2 + 1) * KA, m % 2 * N : (m % 2 + 1) * N]
         s = (here + along) * root_ref[...]
         s_ref[pl.ds(pl.multiple_of((to + m) * KA, 8), KA), :] = s
-        square_ref[pl.ds(to + m, 1), :] = jnp.sum(s * s, axis=0, keepdims=True)
-
-
-def smooth_top_kernel(t_ref, r0, r1, rc, ro, root_ref, band_ref, s_ref, square_ref, side_ref, south_ref, sides):
+        square_ref[pl.ds(pl.multiple_of(8 * (to + m), 8), 8), :] = jnp.sum((s * s).reshape(KA // 8, 8, N), axis=0)
+
+
+def smooth_top_kernel(t_ref, r0, r1, rc, ro, root_ref, band_ref, s_ref, square_ref, side_ref, south_ref, sides, parts):
     north, south, west, east = halos(r0, r1, rc, ro)
     low = iota((KA, N), 1) < 64
     side_ref[...] = jnp.where(low, pltpu.roll(west, 64, 1), east).astype(BF16)
@@ -240,22 +240,24 @@
 
     def rows(i, _):
         beyond = jnp.where(i == 0, north, 0.0)
-        smooth_rows(t_ref, sides, root_ref, band_ref, s_ref, square_ref, count * i, count, count * i, (0, beyond))
+        smooth_rows(t_ref, sides, root_ref, band_ref, s_ref, parts, count * i, count, count * i, (0, beyond))
         return 0
 
     lax.fori_loop(0, 2, rows, 0)
-
-
-def smooth_bottom_kernel(t_ref, side_ref, south_ref, root_ref, band_ref, s_ref, square_ref):
+    square_ref[...] = sum(parts[pl.ds(m, TOP, stride=8), :] for m in range(8))
+
+
+def smooth_bottom_kernel(t_ref, side_ref, south_ref, root_ref, band_ref, s_ref, square_ref, parts):
     count = (N - TOP) // 2
 
     def rows(i, _):
         beyond = jnp.where(i == 1, south_ref[...], 0.0)
         row = TOP + count * i
-        smooth_rows(t_ref, side_ref[...], root_ref, band_ref, s_ref, square_ref, row, count, count * i, (count - 1, beyond))
+        smooth_rows(t_ref, side_ref[...], root_ref, band_ref, s_ref, parts, row, count, count * i, (count - 1, beyond))
         return 0
 
     lax.fori_loop(0, 2, rows, 0)
+    square_ref[...] = sum(parts[pl.ds(m, N - TOP, stride=8), :] for m in range(8))
 
 
 def final_kernel(p0, p1, p2, p3, s0_ref, s1_ref, square0, square1, lab_ref, own_ref, root_ref, out_ref, e_ref, cross_ref):
@@ -371,7 +373,7 @@
         out_shape=(pltpu.VMEM((TOP * KA, N), F32), pltpu.VMEM((TOP, N), F32), edge, wide),
         in_specs=[vmem] * 7,
         out_specs=[vmem] * 4,
-        scratch_shapes=[pltpu.VMEM((2 * KA, N), BF16)],
+        scratch_shapes=[pltpu.VMEM((2 * KA, N), BF16), pltpu.VMEM((8 * TOP, N), F32)],
         compiler_params=params(12),
         cost_estimate=cost(600_000_000, 9_500_000),
         name="smooth_top",
@@ -381,6 +383,7 @@
         out_shape=(pltpu.VMEM(((N - TOP) * KA, N), F32), pltpu.VMEM((N - TOP, N), F32)),
         in_specs=[vmem] * 5,
         out_specs=[vmem] * 2,
+        scratch_shapes=[pltpu.VMEM((8 * (N - TOP), N), F32)],
         compiler_params=params(12),
         cost_estimate=cost(600_000_000, 9_500_000),
         name="smooth_bottom",

time: 27.1 us -> 27.1 us (level)
  no operation moved by 1% of the time
where the time goes in v9:
time: 27.1 us; the launch traced here: 27 us
  Pallas kernels  13.7 us (51%)
  starting transfers between devices  13.2 us (49%)
    pallas_call x1, Pallas kernels, shards(): pl.pallas_call(transport_kernel, out_shape=(pltpu.VMEM(((N + 2) * KP, N),...  6.27 us
    ppermute x1, starting transfers between devices, shards(): r1 = lax.ppermute(s1, ('lat', 'lon'), vertical(1))  3.4 us
    ppermute x1, starting transfers between devices, shards(): rc = lax.ppermute(c0, 'lon', [(j, j ^ 1) for j in range(16)])  2.7 us
    pallas_call x1, Pallas kernels, shards(): pl.pallas_call(smooth_top_kernel, out_shape=(pltpu.VMEM((TOP * KA, N), F3...  2.29 us
    ppermute x1, starting transfers between devices, shards(): p2 = lax.ppermute(pay, 'lat', [(i, (i + 4) % 8) for i in range(8)])  2.2 us
    pallas_call x1, Pallas kernels, shards(): pl.pallas_call(final_kernel, out_shape=jax.ShapeDtypeStruct((N, N), F32),...  2.14 us
    ppermute x1, starting transfers between devices, shards(): p1 = lax.ppermute(pay, 'lon', [(j, j ^ 1) for j in range(16)])  1.94 us
    pallas_call x1, Pallas kernels, shards(): pl.pallas_call(sums_kernel, out_shape=(wide, wide, pltpu.VMEM((N, N), F32...  1.62 us
  transfers between devices with their start and end apart: 7, of which 0 were waited for; matrix products, arithmetic and copies ran while one was open for 0% of the time, Pallas kernels for 19%

profile of v9, /device:TPU:1, one launch (start us, length us, event | category | flops | bytes accessed | tf_op | source)
XLA Modules:
  0.0 27.0 jit_solution(13571078584334729641)
XLA Ops:
  0.0 0.0 copy-start
  0.0 0.0 copy-start.2
  0.0 0.0 copy-start.1
  0.0 6.3 %transport.1 = (f32[19760,128]{1,0:T(8,128)S(1)}, bf16[144,128]{1,0:T(8,128)(2,1)S(1)}, bf16[144,128]{1,0:T(8,128)(2,1)S(1)}, bf16[144,128]{1,0:T(8,128)(2,1)S(1...) custom-call(bf16[137,128,128]{2,1,0:T(8,128)(2,1)} %h_hbm.1, bf16[137,128,128]{2,1,0:T(8,128)(2,1)} %u_hbm.1, ...), custom_call_target="tpu_custom_call" | custom-call | flops 30000000 | bytes 23000000 | tf_op jit(solution)/shard_map/transport/pallas_call | solution.py:333
  6.3 1.5 %collective-permute-start = (bf16[144,128]{1,0:T(8,128)(2,1)S(1)}, bf16[144,128]{1,0:T(8,128)(2,1)S(1)}, u32[]{:S(2)}, u32[]{:S(2)}) collective-permute-start(bf16[144,128]{1,0:T(8,128)(2,1)S(1)} %get-tuple-element.23), channel_id=1, source_target_pairs={{0,1},{1,0},{2,18},{3,19},{4,5},{5,4},{6,22},{7,23},{8,9},{9,8},{1... | collective-permute-start | bytes 110600 | tf_op jit(solution)/shard_map/ppermute | solution.py:345
  7.8 3.4 %collective-permute-start.1 = (bf16[144,128]{1,0:T(8,128)(2,1)S(1)}, bf16[144,128]{1,0:T(8,128)(2,1)S(1)}, u32[]{:S(2)}, u32[]{:S(2)}) collective-permute-start(bf16[144,128]{1,0:T(8,128)(2,1)S(1)} %get-tuple-element.24), channel_id=1, source_target_pairs={{0,16},{1,17},{2,3},{3,2},{4,20},{5,21},{6,7},{7,6},{8,24},{9,25},... | collective-permute-start | bytes 110600 | tf_op jit(solution)/shard_map/ppermute | solution.py:346
  11.2 1.2 %collective-permute-start.2 = (bf16[144,128]{1,0:T(8,128)(2,1)S(1)}, bf16[144,128]{1,0:T(8,128)(2,1)S(1)}, u32[]{:S(2)}, u32[]{:S(2)}) collective-permute-start(bf16[144,128]{1,0:T(8,128)(2,1)S(1)} %get-tuple-element.25), channel_id=1, source_target_pairs={{0,15},{1,2},{2,1},{3,4},{4,3},{5,6},{6,5},{7,8},{8,7},{9,10},{10,... | collective-permute-start | bytes 110600 | tf_op jit(solution)/shard_map/ppermute | solution.py:347
  12.4 2.7 %collective-permute-start.3 = (bf16[144,128]{1,0:T(8,128)(2,1)S(1)}, bf16[144,128]{1,0:T(8,128)(2,1)S(1)}, u32[]{:S(2)}, u32[]{:S(2)}) collective-permute-start(bf16[144,128]{1,0:T(8,128)(2,1)S(1)} %get-tuple-element.26), channel_id=1, source_target_pairs={{0,1},{1,0},{2,3},{3,2},{4,5},{5,4},{6,7},{7,6},{8,9},{9,8},{10,11... | collective-permute-start | bytes 110600 | tf_op jit(solution)/shard_map/ppermute | solution.py:348
  15.1 0.0 copy-done
  15.1 0.0 copy-done.2
  15.1 0.0 copy-done.1
  15.1 1.6 %sums.1 = (f32[144,128]{1,0:T(8,128)S(1)}, f32[144,128]{1,0:T(8,128)S(1)}, f32[128,128]{1,0:T(8,128)S(1)}, bf16[128,512]{1,0:T(8,128)(2,1)S(1)}) custom-call(f32[19760,128]{1,0:T(8,128)S(1)} %get-tuple-element.21.t_ref, s32[128,128]{1,0:T(8,128)S(1)} %copy-done, s32[1,128]{1,0:T(1,128)S(1)} %bitcast.3, f32[1,137]{1,0:T(1,128)S(1)} %bitcast.2), custom_call_target="tpu_custom_call" | custom-call | flops 600000000 | bytes 9500000 | tf_op jit(solution)/shard_map/sums/pallas_call | solution.py:349
  16.7 0.0 collective-permute-done.r0
  16.7 0.0 collective-permute-done.1.r1
  16.7 0.0 collective-permute-done.2.ro
  16.7 0.0 collective-permute-done.3.rc
  16.8 0.2 pack.1.p0
  17.0 2.2 %collective-permute-start.5 = (bf16[144,128]{1,0:T(8,128)(2,1)S(1)}, bf16[144,128]{1,0:T(8,128)(2,1)S(1)}, u32[]{:S(2)}, u32[]{:S(2)}) collective-permute-start(bf16[144,128]{1,0:T(8,128)(2,1)S(1)} %pack.1.p0), channel_id=1, source_target_pairs={{0,64},{16,80},{32,96},{48,112},{64,0},{80,16},{96,32},{112,48},{1... | collective-permute-start | bytes 110600 | tf_op jit(solution)/shard_map/ppermute | solution.py:368
  19.2 1.9 %collective-permute-start.4 = (bf16[144,128]{1,0:T(8,128)(2,1)S(1)}, bf16[144,128]{1,0:T(8,128)(2,1)S(1)}, u32[]{:S(2)}, u32[]{:S(2)}) collective-permute-start(bf16[144,128]{1,0:T(8,128)(2,1)S(1)} %pack.1.p0), channel_id=1, source_target_pairs={{0,1},{1,0},{2,3},{3,2},{4,5},{5,4},{6,7},{7,6},{8,9},{9,8},{10,11... | collective-permute-start | bytes 110600 | tf_op jit(solution)/shard_map/ppermute | solution.py:369
  21.1 2.3 %smooth_top.1 = (f32[12672,128]{1,0:T(8,128)S(1)}, f32[88,128]{1,0:T(8,128)S(1)}, bf16[144,128]{1,0:T(8,128)(2,1)S(1)}, f32[144,128]{1,0:T(8,128)S(1)}) custom-call(f32[19760,128]{1,0:T(8,128)S(1)} %get-tuple-element.21.t_ref, bf16[144,128]{1,0:T(8,128)(2,1)S(1)} %collective-permute-done.r0, bf16[144,128]{1,0:T(8,128)(2,1)S(1)} %collective-permute-done.1.r1, ...), custom_call_target="tpu_custom_call" | custom-call | flops 600000000 | bytes 9500000 | tf_op jit(solution)/shard_map/smooth_top/pallas_call | solution.py:371
  23.4 0.0 collective-permute-done.5.p2
  23.4 0.3 collective-permute-start.6
  23.7 1.1 %smooth_bottom.1 = (f32[5760,128]{1,0:T(8,128)S(1)}, f32[40,128]{1,0:T(8,128)S(1)}) custom-call(f32[19760,128]{1,0:T(8,128)S(1)} %get-tuple-element.21.t_ref, bf16[144,128]{1,0:T(8,128)(2,1)S(1)} %get-tuple-element.31.side_ref, f32[144,128]{1,0:T(8,128)S(1)} %get-tuple-element.32.south_ref, f32[144,128]{1,0:T(8,128)S(1)} %get-tuple-element.28.root_ref, ...), custom_call_target="tpu_custom_call" | custom-call | flops 600000000 | bytes 9500000 | tf_op jit(solution)/shard_map/smooth_bottom/pallas_call | solution.py:381
  24.8 0.0 collective-permute-done.4.p1
  24.8 0.0 collective-permute-done.6.p3
  24.8 2.1 %final.1 = f32[128,128]{1,0:T(8,128)} custom-call(bf16[144,128]{1,0:T(8,128)(2,1)S(1)} %pack.1.p0, bf16[144,128]{1,0:T(8,128)(2,1)S(1)} %collective-permute-done.4.p1, bf16[144,128]{1,0:T(8,128)(2,1)S(1)} %collective-permute-done.5.p2, bf16[144,128]{1,0:T(8,128)(2,1)S(1)} %collective-permute-done.6.p3, f32[12672,128]{1,0:T(8,128)S(1)} %get-tuple-element.30.s0_ref, ...), custom_call_target="tpu_custom_call" | custom-call | flops 300000000 | bytes 9500000 | tf_op jit(solution)/shard_map/final/pallas_call | solution.py:391
Async XLA Ops:
  0.0 15.1 %copy-start = (s32[128,128]{1,0:T(8,128)S(1)}, s32[128,128]{1,0:T(8,128)}, u32[]{:S(2)}) copy-start(s32[128,128]{1,0:T(8,128)} %lab_ref.3) | copy-start | bytes 196612
  0.0 15.1 %copy-start.2 = (s32[1,1,128]{2,1,0:T(1,128)S(1)}, s32[1,1,128]{2,1,0:T(1,128)}, u32[]{:S(2)}) copy-start(s32[1,1,128]{2,1,0:T(1,128)} %param.11) | copy-start | bytes 1540
  0.0 15.1 %copy-start.1 = (f32[137]{0:T(256)S(1)}, f32[137]{0:T(256)}, u32[]{:S(2)}) copy-start(f32[137]{0:T(256)} %param.9) | copy-start | bytes 1648
  6.3 10.4 %collective-permute-start = (bf16[144,128]{1,0:T(8,128)(2,1)S(1)}, bf16[144,128]{1,0:T(8,128)(2,1)S(1)}, u32[]{:S(2)}, u32[]{:S(2)}) collective-permute-start(bf16[144,128]{1,0:T(8,128)(2,1)S(1)} %get-tuple-element.23), channel_id=1, source_target_pairs={{0,1},{1,0},{2,18},{3,19},{4,5},{5,4},{6,22},{7,23},{8,9},{9,8},{1... | collective-permute-start | bytes 110600 | tf_op jit(solution)/shard_map/ppermute | solution.py:345
  7.8 8.9 %collective-permute-start.1 = (bf16[144,128]{1,0:T(8,128)(2,1)S(1)}, bf16[144,128]{1,0:T(8,128)(2,1)S(1)}, u32[]{:S(2)}, u32[]{:S(2)}) collective-permute-start(bf16[144,128]{1,0:T(8,128)(2,1)S(1)} %get-tuple-element.24), channel_id=1, source_target_pairs={{0,16},{1,17},{2,3},{3,2},{4,20},{5,21},{6,7},{7,6},{8,24},{9,25},... | collective-permute-start | bytes 110600 | tf_op jit(solution)/shard_map/ppermute | solution.py:346
  11.2 5.6 %collective-permute-start.2 = (bf16[144,128]{1,0:T(8,128)(2,1)S(1)}, bf16[144,128]{1,0:T(8,128)(2,1)S(1)}, u32[]{:S(2)}, u32[]{:S(2)}) collective-permute-start(bf16[144,128]{1,0:T(8,128)(2,1)S(1)} %get-tuple-element.25), channel_id=1, source_target_pairs={{0,15},{1,2},{2,1},{3,4},{4,3},{5,6},{6,5},{7,8},{8,7},{9,10},{10,... | collective-permute-start | bytes 110600 | tf_op jit(solution)/shard_map/ppermute | solution.py:347
  12.4 4.4 %collective-permute-start.3 = (bf16[144,128]{1,0:T(8,128)(2,1)S(1)}, bf16[144,128]{1,0:T(8,128)(2,1)S(1)}, u32[]{:S(2)}, u32[]{:S(2)}) collective-permute-start(bf16[144,128]{1,0:T(8,128)(2,1)S(1)} %get-tuple-element.26), channel_id=1, source_target_pairs={{0,1},{1,0},{2,3},{3,2},{4,5},{5,4},{6,7},{7,6},{8,9},{9,8},{10,11... | collective-permute-start | bytes 110600 | tf_op jit(solution)/shard_map/ppermute | solution.py:348
  17.0 6.4 %collective-permute-start.5 = (bf16[144,128]{1,0:T(8,128)(2,1)S(1)}, bf16[144,128]{1,0:T(8,128)(2,1)S(1)}, u32[]{:S(2)}, u32[]{:S(2)}) collective-permute-start(bf16[144,128]{1,0:T(8,128)(2,1)S(1)} %pack.1.p0), channel_id=1, source_target_pairs={{0,64},{16,80},{32,96},{48,112},{64,0},{80,16},{96,32},{112,48},{1... | collective-permute-start | bytes 110600 | tf_op jit(solution)/shard_map/ppermute | solution.py:368
  19.2 5.7 %collective-permute-start.4 = (bf16[144,128]{1,0:T(8,128)(2,1)S(1)}, bf16[144,128]{1,0:T(8,128)(2,1)S(1)}, u32[]{:S(2)}, u32[]{:S(2)}) collective-permute-start(bf16[144,128]{1,0:T(8,128)(2,1)S(1)} %pack.1.p0), channel_id=1, source_target_pairs={{0,1},{1,0},{2,3},{3,2},{4,5},{5,4},{6,7},{7,6},{8,9},{9,8},{10,11... | collective-permute-start | bytes 110600 | tf_op jit(solution)/shard_map/ppermute | solution.py:369
  23.4 1.4 %collective-permute-start.6 = (bf16[144,128]{1,0:T(8,128)(2,1)S(1)}, bf16[144,128]{1,0:T(8,128)(2,1)S(1)}, u32[]{:S(2)}, u32[]{:S(2)}) collective-permute-start(bf16[144,128]{1,0:T(8,128)(2,1)S(1)} %collective-permute-done.5.p2), channel_id=1, source_target_pairs={{0,1},{1,0},{2,3},{3,2},{4,5},{5,4},{6,7},{7,6},{8,9},{9,8},{10,11... | collective-permute-start | bytes 110600 | tf_op jit(solution)/shard_map/ppermute | solution.py:370
